TPU v7x, 128 devices: a whole 4x4x4 slice. The times are simulated.
128 devices in a mesh: fold: 8 (over y, x_hi), col: 16 (over z, x_lo, core).
Axes of the slice: x: 4 (x_hi: 2, x_lo: 2; x = x_hi * 2 + x_lo), y: 4, z: 4, core: 2. Of those that a mesh axis runs over, the one named last changes fastest.
Arguments:
- bin_embed: bfloat16 [48, 2048], P(None, 'col'), may hold values from -6 to 6
- conv_weight: bfloat16 [9, 48, 48], replicated, may hold values from -0.3125 to 0.3125
- conv_bias: float32 [48], replicated, may hold values from -3 to 3
- dilation: int32 [2], replicated, may hold values from 1 to 16, as said below
- fold_map: int32 [128, 2], replicated, may hold values from 0 to 15, as said below
- cotangent: bfloat16 [8, 16, 48, 128, 128], P('fold', 'col'), may hold values from -6 to 6
Outputs:
- pair_out: bfloat16 [8, 16, 48, 128, 128], P('fold', 'col')
- grad_embed: float32 [48, 2048], P(None, 'col')
- grad_weight: float32 [9, 48, 48], replicated
- grad_bias: float32 [48], replicated
Inputs may be any that keep to these rules, and one draw needn't show every extreme that they name: `dilation`: one rate is exactly 16, the other is smaller; which one is drawn. `fold_map`: rows are tile pairs below 16. Every pair i < j appears once; every pair (i, j) with i > j and i + j = 15 appears once; nothing else. The order is random.
All inputs are finite; a program needn't handle non-finite values.
Results may differ from a plain program's by a relative error of at most 0.0047.
Values may be sent and summed in bfloat16 or wider, within the bound.
No kernel may reach another device: no remote copies, remote signals or barrier semaphores. Data moves between devices by JAX's collectives and lax.ppermute only.
A program may use at most 192 MiB of HBM per device.

v0:
```python
import jax
import jax.numpy as jnp
from jax import lax
from jax.sharding import PartitionSpec as P

DMAX = 16


tap_rows = (-1, -1, -1, 0, 0, 0, 1, 1, 1)
tap_cols = (-1, 0, 1, -1, 0, 1, -1, 0, 1)


def build_tile(padded_embed, padded_valid, row_index, col_index, tile_width):
    extent = tile_width + 2 * DMAX
    row_values = lax.dynamic_slice_in_dim(padded_embed, row_index * tile_width, extent, 1)
    col_values = lax.dynamic_slice_in_dim(padded_embed, col_index * tile_width, extent, 1)
    row_live = lax.dynamic_slice_in_dim(padded_valid, row_index * tile_width, extent, 0)
    col_live = lax.dynamic_slice_in_dim(padded_valid, col_index * tile_width, extent, 0)
    pre_act = row_values[:, :, None] + col_values[:, None, :]
    open_mask = (pre_act > 0).astype(jnp.float32) * (row_live[:, None] * col_live[None, :])[None]
    return ((pre_act * open_mask).astype(jnp.bfloat16), open_mask)


def conv_forward(activity, weight, dilation, tile_width):
    channels = activity.shape[0]
    summed = jnp.zeros((weight.shape[2], tile_width, tile_width), jnp.float32)
    for tap_index in range(9):
        start_row = DMAX + tap_rows[tap_index] * dilation[0]
        start_col = DMAX + tap_cols[tap_index] * dilation[1]
        window = lax.dynamic_slice(
            activity, (jnp.int32(0), start_row, start_col), (channels, tile_width, tile_width)
        )
        summed = summed + jnp.einsum(
            "io,irs->ors", weight[tap_index], window, preferred_element_type=jnp.float32
        )
    return summed


def conv_backward(activity, open_mask, grad_tile, weight, dilation, tile_width):
    channels = activity.shape[0]
    extent = activity.shape[1]
    out_channels = grad_tile.shape[0]
    grad_padded = jnp.pad(grad_tile, ((0, 0), (2 * DMAX, 2 * DMAX), (2 * DMAX, 2 * DMAX)))
    grad_ext = jnp.zeros(activity.shape, jnp.float32)
    tap_grads = []
    for tap_index in range(9):
        start_row = DMAX + tap_rows[tap_index] * dilation[0]
        start_col = DMAX + tap_cols[tap_index] * dilation[1]
        window = lax.dynamic_slice(
            activity, (jnp.int32(0), start_row, start_col), (channels, tile_width, tile_width)
        )
        tap_grads.append(
            jnp.einsum("irs,ors->io", window, grad_tile, preferred_element_type=jnp.float32)
        )
        back_row = DMAX - tap_rows[tap_index] * dilation[0]
        back_col = DMAX - tap_cols[tap_index] * dilation[1]
        shifted = lax.dynamic_slice(
            grad_padded, (jnp.int32(0), back_row, back_col), (out_channels, extent, extent)
        )
        grad_ext = grad_ext + jnp.einsum(
            "io,ors->irs", weight[tap_index], shifted, preferred_element_type=jnp.float32
        )
    grad_pre = grad_ext * open_mask
    bias_grad = jnp.sum(grad_tile.astype(jnp.float32), axis=(1, 2))
    return (jnp.sum(grad_pre, axis=2), jnp.sum(grad_pre, axis=1), jnp.stack(tap_grads), bias_grad)


def add_block(partial_value, piece, offset):
    region = lax.dynamic_slice_in_dim(partial_value, offset, piece.shape[1], 1)
    return lax.dynamic_update_slice_in_dim(partial_value, region + piece, offset, 1)


def tile_step(padded_embed, padded_valid, weight, bias, dilation, tile_pair, cot_tile, tile_width):
    row_index = tile_pair[0]
    col_index = tile_pair[1]
    channels = weight.shape[1]
    span = padded_embed.shape[1]

    def one_tile():
        activity, open_mask = build_tile(
            padded_embed, padded_valid, row_index, col_index, tile_width
        )
        summed = conv_forward(activity, weight, dilation, tile_width) + bias[:, None, None]
        row_part, col_part, weight_grad, bias_grad = conv_backward(
            activity, open_mask, cot_tile, weight, dilation, tile_width
        )
        partial_value = jnp.zeros((channels, span), jnp.float32)
        partial_value = add_block(partial_value, row_part, row_index * tile_width)
        partial_value = add_block(partial_value, col_part, col_index * tile_width)
        return (summed.astype(jnp.bfloat16), partial_value, weight_grad, bias_grad)

    def two_tiles():
        act_high, mask_high = build_tile(
            padded_embed, padded_valid, row_index, row_index, tile_width
        )
        act_low, mask_low = build_tile(padded_embed, padded_valid, col_index, col_index, tile_width)
        out_high = conv_forward(act_high, weight, dilation, tile_width) + bias[:, None, None]
        out_low = conv_forward(act_low, weight, dilation, tile_width) + bias[:, None, None]
        line = lax.broadcasted_iota(jnp.int32, (tile_width, tile_width), 0)
        column = lax.broadcasted_iota(jnp.int32, (tile_width, tile_width), 1)
        upper_mask = (column >= line)[None]
        merged = jnp.where(upper_mask, out_high, jnp.swapaxes(out_low, 1, 2))
        zero_tile = jnp.zeros_like(cot_tile)
        grad_high = jnp.where(upper_mask, cot_tile, zero_tile)
        grad_low = jnp.swapaxes(jnp.where(upper_mask, zero_tile, cot_tile), 1, 2)
        rows_high, cols_high, wgrad_high, bgrad_high = conv_backward(
            act_high, mask_high, grad_high, weight, dilation, tile_width
        )
        rows_low, cols_low, wgrad_low, bgrad_low = conv_backward(
            act_low, mask_low, grad_low, weight, dilation, tile_width
        )
        partial_value = jnp.zeros((channels, span), jnp.float32)
        partial_value = add_block(partial_value, rows_high, row_index * tile_width)
        partial_value = add_block(partial_value, cols_high, row_index * tile_width)
        partial_value = add_block(partial_value, rows_low, col_index * tile_width)
        partial_value = add_block(partial_value, cols_low, col_index * tile_width)
        return (
            merged.astype(jnp.bfloat16),
            partial_value,
            wgrad_high + wgrad_low,
            bgrad_high + bgrad_low,
        )

    return lax.cond(row_index > col_index, two_tiles, one_tile)


def body(bin_embed, conv_weight, conv_bias, dilation, fold_map, cotangent):
    gathered = lax.all_gather(bin_embed, "col", axis=1, tiled=True)
    channels, bin_count = gathered.shape
    tile_width = cotangent.shape[-1]
    padded_embed = jnp.pad(gathered.astype(jnp.float32), ((0, 0), (DMAX, DMAX)))
    padded_valid = jnp.pad(jnp.ones((bin_count,), jnp.float32), (DMAX, DMAX))
    device_slot = lax.axis_index("fold") * lax.axis_size("col") + lax.axis_index("col")
    tile_pair = lax.dynamic_slice_in_dim(fold_map, device_slot, 1, 0)[0]
    tile_out, partial_value, weight_grad, bias_grad = tile_step(
        padded_embed,
        padded_valid,
        conv_weight,
        conv_bias,
        dilation,
        tile_pair,
        cotangent[0, 0],
        tile_width,
    )
    inner = partial_value[:, DMAX : DMAX + bin_count]
    embed_sum, weight_sum, bias_sum = lax.psum((inner, weight_grad, bias_grad), ("fold", "col"))
    own_block = lax.dynamic_slice_in_dim(
        embed_sum, lax.axis_index("col") * tile_width, tile_width, 1
    )
    grad_embed = own_block * bin_count ** (-0.5)
    return (tile_out[None, None], grad_embed, weight_sum / bin_count, bias_sum / bin_count)


def solution(mesh):
    placed = (P(None, "col"), P(), P(), P(), P(), P("fold", "col", None, None, None))
    return jax.shard_map(
        body,
        mesh=mesh,
        in_specs=placed,
        out_specs=(P("fold", "col", None, None, None), P(None, "col"), P(), P()),
        check_vma=False,
    )
```

profile of v0, /device:TPU:0, one launch (start us, length us, event | category | flops | bytes accessed | tf_op | source)
XLA Modules:
  0.0 647.1 jit_solution(977645371694716866)
XLA Ops:
  7.3 0.6 copy-done
  7.9 0.5 fusion.340
  8.5 2.4 copy.314
  10.9 21.8 %all_gather.3 = bf16[48,2048]{1,0:T(8,128)(2,1)S(1)} all-gather(bf16[48,128]{1,0:T(8,128)(2,1)S(1)} %copy-done.34), channel_id=1, replica_groups=mesh['fold'=8,'col'=16] {'col'}, dimensions={1}, use_global_device_ids=true | all-gather | bytes 208896 | tf_op jit(solution)/shard_map/all_gather | solution.py:128
  32.7 0.1 pad_convert_fusion
  34.2 131.8 %conditional.1 = (f32[48,2080]{1,0:T(8,128)}, f32[9,48,48]{2,1,0:T(8,128)}, f32[48]{0:T(128)}, bf16[1,1,48,128,128]{4,3,2,1,0:T(8,128)(2,1)}) conditional(s32[]{:T(128)} %convert_element_type.39, (bf16[48,128,128]{2,0,1:T(8,128)(2,1)S(1)}, s32[2]{0:T(128)S(1)}, bf16[9,48,48]{2,1,0:T(8,128)(2,1)S(1)}, s32[]{:T(128)}, f32[48,2080]{1,0:T(8,128)S(1)}, ...), branch_computations={%region_0.4_spmd, %region_4.11_spmd} | conditional | flops 4908497920 | bytes 713957632 | solution.py:124
  35.9 2.9 fusion
  38.8 0.6 fusion.335
  40.7 4.2 fusion.42
  46.2 4.3 fusion.34
  51.8 2.7 fusion.38
  54.6 0.3 copy-done.2
  54.9 0.7 fusion.23
  55.6 2.4 fusion.27
  57.9 2.4 fusion.15
  60.3 2.4 fusion.19
  62.7 2.3 fusion.11
  65.1 6.3 fusion.10
  71.4 1.6 copy.311
  72.9 4.6 fusion.1
  78.8 4.7 fusion.3
  84.8 5.3 fusion.7
  90.1 4.3 fusion.2
  94.4 4.6 fusion.4
  98.9 4.5 fusion.6
  103.5 4.4 fusion.8
  107.8 4.3 fusion.5
  112.1 21.2 %fusion.331 = (f32[48,160]{1,0:T(8,128)S(1)}, f32[48,160]{0,1:T(8,128)S(1)}) fusion(f32[160,160]{1,0:T(8,128)S(1)} %broadcast_multiply_fusion, f32[48,160]{1,0:T(8,128)S(1)} %get-tuple-element.87, f32[48,160]{0,1:T(8,128)S(1)} %copy.149, s32[]{:T(128)S(6)} %select_n.21, s32[]{:T(128)S(6)} %select_n.10, bf16[48,128,128]{2,0,1:T(8,128)(2,1)S(1)} %get-tuple-element.33, ...), kind=kOutput, calls=%fused_computation.391 | convolution fusion | flops 135152640 | bytes 41263112 | tf_op jit(solution)/shard_map/cond/branch_0_fun/io,ors->irs/dot_general | solution.py:60
  133.5 0.8 broadcast.81
  134.3 1.5 dynamic_update_slice.12
  135.7 1.0 dynamic-slice_add_fusion
  136.7 1.5 dynamic_update_slice.13
  138.2 3.4 fusion.49
  141.6 3.3 fusion.73
  144.9 1.4 fusion.55
  146.3 1.4 fusion.79
  147.7 1.4 fusion.97
  149.1 1.4 fusion.85
  150.5 1.4 fusion.61
  152.0 1.4 fusion.91
  153.3 1.4 fusion.67
  154.8 0.9 convert_reduce_fusion
  166.0 1.9 slice.54
  168.0 388.6 %psum.23 = f32[48]{0:T(128)S(1)} all-reduce(f32[48]{0:T(128)} %get-tuple-element.60), channel_id=1, replica_groups=mesh['fold'=8,'col'=16] {'fold','col'}, use_global_device_ids=true, to_apply=%region_13.14 | all-reduce | flops 48 | bytes 384 | tf_op jit(solution)/shard_map/psum | solution.py:146
  556.5 0.5 broadcast_multiply_fusion.4
  557.1 80.0 %all-reduce.8.cloned.1.call-done = (f32[48,2048]{1,0:T(8,128)}, f32[9,48,48]{2,1,0:T(8,128)}) async-done(((f32[48,2048]{1,0:T(8,128)}, f32[9,48,48]{2,1,0:T(8,128)}), (f32[48,2048]{1,0:T(8,128)}, f32[9,48,48]{2,1,0:T(8,128)})) %all-reduce.8.cloned.1.call-update) | async-done | bytes 476176 | tf_op jit(solution)/shard_map/psum | solution.py:146
  637.0 1.6 broadcast_multiply_fusion.3
  638.7 1.3 dynamic-slice_multiply_fusion
  (28 shorter events, 0.7 us)
Async XLA Ops:
  7.2 0.7 copy-start
  7.2 3.7 copy-start.34
  7.2 27.0 %copy-start.36 = (f32[48]{0:T(128)S(1)}, f32[48]{0:T(128)}, u32[]{:S(2)}) copy-start(f32[48]{0:T(128)} %param.10) | copy-start | bytes 580
  7.2 27.0 %copy-start.35 = (s32[2]{0:T(128)S(1)}, s32[2]{0:T(128)}, u32[]{:S(2)}) copy-start(s32[2]{0:T(128)} %param.11) | copy-start | bytes 28
  7.2 27.0 %copy-start.25 = (bf16[9,48,48]{2,1,0:T(8,128)(2,1)S(1)}, bf16[9,48,48]{2,1,0:T(8,128)(2,1)}, u32[]{:S(2)}) copy-start(bf16[9,48,48]{2,1,0:T(8,128)(2,1)} %param.9) | copy-start | bytes 124420
  7.2 629.8 %all-reduce.8.cloned.1.call-start = ((), (), s32[]{:S(2)}) async-start(), calls=%async_computation | async-start | bytes 1228800 | tf_op jit(solution)/shard_map/psum | solution.py:146
  51.8 3.1 copy-start.2
  60.3 4.7 copy-start.24
  62.7 2.4 copy-start.23
  138.2 6.7 %copy-start.3 = (bf16[48,160,160]{2,0,1:T(8,128)(2,1)S(1)}, bf16[48,160,160]{2,0,1:T(8,128)(2,1)}, u32[]{:S(2)}) copy-start(bf16[48,160,160]{2,0,1:T(8,128)(2,1)} %fusion) | copy-start | bytes 7372804 | tf_op jit(solution)/shard_map/cond
  166.0 474.1 %copy-start.1 = (s32[128,2]{0,1:T(2,128)S(1)}, s32[128,2]{0,1:T(2,128)}, u32[]{:S(2)}) copy-start(s32[128,2]{0,1:T(2,128)} %param.12) | copy-start | bytes 3076
Sparse Core Ops, SparseCore 0:
  168.1 468.9 all-reduce.7
where the time goes:
time: 654 us; the launch traced here: 647 us
  blocking collectives  410 us (63%)
  matrix products  102 us (16%)
  waiting for transfers between devices  80 us (12%)
  loops' own time  18.2 us (3%)
  between operations  15.6 us (2%)
  local copies, waits for them, and re-layouts  12.2 us (2%)
  other arithmetic  8.46 us (1%)
    psum x1, blocking collectives, body(): lax.psum((inner, weight_grad, bias_grad), ('fold', 'col'))  389 us
    psum x1, waiting for transfers between devices, body(): lax.psum((inner, weight_grad, bias_grad), ('fold', 'col'))  80 us
    dot_general x9, matrix products, conv_backward(): jnp.einsum('io,ors->irs', weight[tap_index], shifted, preferred_element_t...  57.9 us
    dot_general x9, matrix products, conv_forward(): jnp.einsum('io,irs->ors', weight[tap_index], window, preferred_element_ty...  27.7 us
    all_gather x1, blocking collectives, body(): gathered = lax.all_gather(bin_embed, 'col', axis=1, tiled=True)  21.8 us
    another operation x1, loops' own time, tile_step(): return lax.cond(row_index > col_index, two_tiles, one_tile)  18.2 us
    dot_general x9, matrix products, conv_backward(): jnp.einsum('irs,ors->io', window, grad_tile, preferred_element_type=jnp.f...  16.6 us
  transfers between devices with their start and end apart: 1, of which 1 were waited for; matrix products, arithmetic and copies ran while one was open for 0% of the time, Pallas kernels for 0%

commit v1 on v0

v1 whole, which is shorter than its diff:
```python
import functools

import jax
import jax.numpy as jnp
import numpy as np
from jax import lax
from jax.experimental import pallas as pl
from jax.experimental.pallas import tpu as pltpu
from jax.sharding import PartitionSpec as P

C = 48
B = 128
DMAX = 16
NK = 448
OUTSIDE = -16384.0
F32 = jnp.float32
BF16 = jnp.bfloat16
UNROLL = 8
ROWS = 4
VMEM_BYTES = 48 * 1024 * 1024

NT = (((1,), (1,)), ((), ()))
TN = (((0,), (0,)), ((), ()))
NN = (((1,), (0,)), ((), ()))


def dot(a, b, dims):
    return lax.dot_general(a, b, dims, preferred_element_type=F32)


def repeat_table():
    table = np.zeros((2, 144, NK), np.float32)
    for u in range(3):
        for v in range(3):
            for i in range(C):
                column = (3 * u + v) * C + i
                table[0, u * C + i, column] = 1.0
                table[1, v * C + i, column] = 1.0
    return jnp.asarray(table, BF16)


def fill_blocks(meta, own, core, xlo, z1, z2, z3, blocks):
    z, x, c = meta[4], meta[5], meta[6]
    blocks[0] = jnp.full((C, B), OUTSIDE, F32)
    blocks[17] = jnp.full((C, B), OUTSIDE, F32)
    blocks[1 + z * 4 + x * 2 + c] = own[...].astype(F32)
    blocks[1 + z * 4 + x * 2 + (1 - c)] = core[...].astype(F32)
    blocks[1 + z * 4 + (1 - x) * 2 + c] = xlo[0].astype(F32)
    blocks[1 + z * 4 + (1 - x) * 2 + (1 - c)] = xlo[1].astype(F32)
    for step, got in ((1, z1), (2, z2), (3, z3)):
        zz = z ^ step
        blocks[1 + zz * 4 + x * 2 + c] = got[0].astype(F32)
        blocks[1 + zz * 4 + x * 2 + (1 - c)] = got[1].astype(F32)
        blocks[1 + zz * 4 + (1 - x) * 2 + c] = got[2].astype(F32)
        blocks[1 + zz * 4 + (1 - x) * 2 + (1 - c)] = got[3].astype(F32)


def spread_lanes(blocks, tile, table):
    before, here, after = blocks[tile], blocks[tile + 1], blocks[tile + 2]
    for q in range(-DMAX, B + DMAX):
        source, lane = (before, q + B) if q < 0 else ((here, q) if q < B else (after, q - B))
        table[DMAX + q] = jnp.broadcast_to(source[:, lane : lane + 1], (C, B)).astype(BF16)


def windows(blocks, tile, rate):
    lane = lax.broadcasted_iota(jnp.int32, (C, B), 1)
    before, here, after = blocks[tile], blocks[tile + 1], blocks[tile + 2]
    low = jnp.where(lane < rate, pltpu.roll(before, rate, 1), pltpu.roll(here, rate, 1))
    high = jnp.where(lane >= B - rate, pltpu.roll(after, B - rate, 1), pltpu.roll(here, B - rate, 1))
    return [low.astype(BF16), here.astype(BF16), high.astype(BF16)]


def scatter_back(grads, tile, rate, shifted):
    lane = lax.broadcasted_iota(jnp.int32, (C, B), 1)
    low, here, high = shifted
    low = pltpu.roll(low, B - rate, 1)
    high = pltpu.roll(high, rate, 1)
    zero = jnp.zeros((C, B), F32)
    grads[tile] += jnp.where(lane >= B - rate, low, zero)
    grads[tile + 2] += jnp.where(lane < rate, high, zero)
    grads[tile + 1] += (
        jnp.where(lane < B - rate, low, zero) + here + jnp.where(lane >= rate, high, zero)
    )


def backward_kernel(
    meta, own, core, xlo, z1, z2, z3, cot_rows, cot_cols, weight, repeat,
    send, keep,
    blocks, table_i, table_j, shift, sums, grads, wgrad,
):
    tile_i, tile_j, rate_r, rate_c, core_index = meta[0], meta[1], meta[2], meta[3], meta[6]
    fill_blocks(meta, own, core, xlo, z1, z2, z3, blocks)
    spread_lanes(blocks, tile_i, table_i)
    spread_lanes(blocks, tile_j, table_j)
    one, zero = jnp.ones((), BF16), jnp.zeros((), BF16)
    bias_rows = jnp.ones((NK - 432, B), BF16)
    column = lax.broadcasted_iota(jnp.int32, (B, NK), 1)
    bias_mark = jnp.where(column == 432, 1.0, 0.0)
    grads[...] = jnp.zeros_like(grads)

    def shifts_of(slot, window, which, mark):
        table = dot(jnp.concatenate(window, 0), repeat[which], TN)
        shift[slot] = table + bias_mark if mark else table

    def back_sums(slot, tile, rate, which):
        total = sums[slot]
        high = total.astype(BF16)
        low = (total - high.astype(F32)).astype(BF16)
        merged = dot(repeat[which], high, NT) + dot(repeat[which], low, NT)
        scatter_back(grads, tile, rate, [merged[k * C : (k + 1) * C] for k in range(3)])

    def each(step):
        def several(outer, carry):
            for inner in range(UNROLL):
                carry = step(outer * UNROLL + inner, carry)
            return carry
        return several

    weight_now = weight[...]

    def take(slot, q, products, total):
        sums[slot, pl.ds(q, 1), :] = jnp.sum(products * weight_now, axis=0, keepdims=True)
        return total + products * shift[slot, pl.ds(q, 1), :]

    empty = jnp.zeros((C, NK), F32)

    @pl.when(tile_i < tile_j)
    def one_tile():
        window_i, window_j = windows(blocks, tile_i, rate_r), windows(blocks, tile_j, rate_c)
        shifts_of(0, window_i, 0, True)
        shifts_of(1, window_j, 1, False)
        minus_i, minus_j = [-w for w in window_i], [-w for w in window_j]

        def row(q, total):
            at = [table_i[DMAX + q + k * rate_r] for k in (-1, 0, 1)]
            mask = [jnp.where(at[u] > minus_j[v], one, zero) for u in range(3) for v in range(3)]
            return take(0, q, dot(cot_rows[q], jnp.concatenate(mask + [bias_rows], 0), NT), total)

        def col(q, total):
            at = [table_j[DMAX + q + k * rate_c] for k in (-1, 0, 1)]
            mask = [jnp.where(at[v] > minus_i[u], one, zero) for u in range(3) for v in range(3)]
            return take(1, q, dot(cot_cols[q], jnp.concatenate(mask + [bias_rows], 0), NT), total)

        total = lax.fori_loop(0, B // UNROLL, each(row), empty)
        wgrad[...] = lax.fori_loop(0, B // UNROLL, each(col), total)
        back_sums(0, tile_i, rate_r, 0)
        back_sums(1, tile_j, rate_c, 1)

    @pl.when(tile_i > tile_j)
    def two_triangles():
        up_r, up_c = windows(blocks, tile_i, rate_r), windows(blocks, tile_i, rate_c)
        low_r, low_c = windows(blocks, tile_j, rate_r), windows(blocks, tile_j, rate_c)
        shifts_of(0, up_r, 0, True)
        shifts_of(1, up_c, 1, False)
        shifts_of(2, low_c, 1, True)
        shifts_of(3, low_r, 0, False)
        lane = lax.broadcasted_iota(jnp.int32, (C, B), 1)

        def both(q, total, cot, upper, up, up_window, low, low_window, slot):
            mask = []
            for u in range(3):
                for v in range(3):
                    at = jnp.where(upper, up(u, v), low(u, v))
                    other = jnp.where(upper, up_window(u, v), low_window(u, v))
                    mask.append(jnp.where(at > other, one, zero))
            mask = jnp.concatenate(mask + [bias_rows], 0)
            none = jnp.zeros_like(cot)
            parts = jnp.concatenate([jnp.where(upper, cot, none), jnp.where(upper, none, cot)], 0)
            products = dot(parts, mask, NT)
            total = take(slot, q, products[:C], total)
            return take(slot + 2, q, products[C:], total)

        m_up_r, m_up_c = [-w for w in up_r], [-w for w in up_c]
        m_low_r, m_low_c = [-w for w in low_r], [-w for w in low_c]

        def row(q, total):
            up = [table_i[DMAX + q + k * rate_r] for k in (-1, 0, 1)]
            low = [table_j[DMAX + q + k * rate_c] for k in (-1, 0, 1)]
            return both(
                q, total, cot_rows[q], lane >= q,
                lambda u, v: up[u], lambda u, v: m_up_c[v],
                lambda u, v: low[v], lambda u, v: m_low_r[u], 0,
            )

        def col(q, total):
            up = [table_i[DMAX + q + k * rate_c] for k in (-1, 0, 1)]
            low = [table_j[DMAX + q + k * rate_r] for k in (-1, 0, 1)]
            return both(
                q, total, cot_cols[q], lane <= q,
                lambda u, v: up[v], lambda u, v: m_up_r[u],
                lambda u, v: low[u], lambda u, v: m_low_c[v], 1,
            )

        total = lax.fori_loop(0, B // UNROLL, each(row), empty)
        wgrad[...] = lax.fori_loop(0, B // UNROLL, each(col), total)
        back_sums(0, tile_i, rate_r, 0)
        back_sums(1, tile_i, rate_c, 1)
        back_sums(2, tile_j, rate_c, 1)
        back_sums(3, tile_j, rate_r, 0)

    for pair in range(8):
        send[pair] = grads[1 + 2 * pair + (1 - core_index)].astype(BF16)
        keep[pair] = grads[1 + 2 * pair + core_index].astype(BF16)
    total = wgrad[...]
    for part in range(4):
        piece = total[:, part * B : min((part + 1) * B, NK)].astype(BF16)
        if piece.shape[1] < B:
            piece = jnp.concatenate([piece, jnp.zeros((C, B - piece.shape[1]), BF16)], 1)
        send[8 + part] = piece
        keep[8 + part] = piece


def forward_kernel(
    meta, own, core, xlo, z1, z2, z3, weight, bias, out, blocks, table_i, table_j
):
    tile_i, tile_j, rate_r, rate_c = meta[0], meta[1], meta[2], meta[3]
    fill_blocks(meta, own, core, xlo, z1, z2, z3, blocks)
    spread_lanes(blocks, tile_i, table_i)
    weight_now = weight[...]
    bias_now = bias[...]
    zero = jnp.zeros((), BF16)

    def finish(first, parts):
        full = dot(weight_now, jnp.concatenate(parts, 1), NN)
        for k in range(ROWS):
            out[first + k] = (full[:, k * B : (k + 1) * B] + bias_now).astype(BF16)

    @pl.when(tile_i < tile_j)
    def one_tile():
        window = windows(blocks, tile_j, rate_c)

        def some(step, carry):
            parts = []
            for k in range(ROWS):
                q = step * ROWS + k
                at = [table_i[DMAX + q + m * rate_r] for m in (-1, 0, 1)]
                parts.append(
                    jnp.concatenate(
                        [jnp.maximum(at[u] + window[v], zero) for u in range(3) for v in range(3)], 0
                    )
                )
            finish(step * ROWS, parts)
            return carry

        lax.fori_loop(0, B // ROWS, some, 0)

    @pl.when(tile_i > tile_j)
    def two_triangles():
        spread_lanes(blocks, tile_j, table_j)
        up_window, low_window = windows(blocks, tile_i, rate_c), windows(blocks, tile_j, rate_r)
        lane = lax.broadcasted_iota(jnp.int32, (C, B), 1)

        def some(step, carry):
            parts = []
            for k in range(ROWS):
                q = step * ROWS + k
                upper = lane >= q
                up = [table_i[DMAX + q + m * rate_r] for m in (-1, 0, 1)]
                low = [table_j[DMAX + q + m * rate_c] for m in (-1, 0, 1)]
                parts.append(
                    jnp.concatenate(
                        [
                            jnp.maximum(
                                jnp.where(upper, up[u] + up_window[v], low[v] + low_window[u]), zero
                            )
                            for u in range(3)
                            for v in range(3)
                        ],
                        0,
                    )
                )
            finish(step * ROWS, parts)
            return carry

        lax.fori_loop(0, B // ROWS, some, 0)


def shape(dims, kind):
    return jax.ShapeDtypeStruct(dims, kind)


def call(kernel, out_shape, n_in, scratch=(), **cost):
    specs = [pl.BlockSpec(memory_space=pltpu.SMEM)] + [pl.BlockSpec(memory_space=pltpu.VMEM)] * n_in
    return pl.pallas_call(
        kernel,
        out_shape=out_shape,
        in_specs=specs,
        scratch_shapes=list(scratch),
        compiler_params=pltpu.CompilerParams(vmem_limit_bytes=VMEM_BYTES),
        cost_estimate=pl.CostEstimate(**cost) if cost else None,
    )


def backward(meta, pieces, cot_rows, cot_cols, weight, repeat):
    return call(
        backward_kernel,
        (shape((12, C, B), BF16), shape((12, C, B), BF16)),
        len(pieces) + 4,
        [
            pltpu.VMEM((18, C, B), F32),
            pltpu.VMEM((B + 2 * DMAX, C, B), BF16),
            pltpu.VMEM((B + 2 * DMAX, C, B), BF16),
            pltpu.VMEM((4, B, NK), F32),
            pltpu.VMEM((4, B, NK), F32),
            pltpu.VMEM((18, C, B), F32),
            pltpu.VMEM((C, NK), F32),
        ],
        flops=2 * 2 * B * B * C * NK, bytes_accessed=4 * B * B * C, transcendentals=0,
    )(meta, *pieces, cot_rows, cot_cols, weight, repeat)


def forward(meta, pieces, weight, bias):
    return call(
        forward_kernel,
        shape((B, C, B), BF16),
        len(pieces) + 2,
        [
            pltpu.VMEM((18, C, B), F32),
            pltpu.VMEM((B + 2 * DMAX, C, B), BF16),
            pltpu.VMEM((B + 2 * DMAX, C, B), BF16),
        ],
        flops=2 * B * B * C * 432, bytes_accessed=2 * B * B * C, transcendentals=0,
    )(meta, *pieces, weight, bias)


def after_core_kernel(meta, keep, got, own, to1, to2, to3):
    z = meta[4]
    total = [keep[k].astype(F32) + got[k].astype(F32) for k in range(8, 12)]
    for step, out in ((0, own), (1, to1), (2, to2), (3, to3)):
        first = (z ^ step) * 2
        for k in range(2):
            out[k] = (keep[first + k].astype(F32) + got[first + k].astype(F32)).astype(BF16)
        for k in range(4):
            out[2 + k] = total[k].astype(BF16)


def sum4(own, a, b, c, k):
    return (own[k].astype(F32) + a[k].astype(F32)) + (b[k].astype(F32) + c[k].astype(F32))


def after_z_kernel(meta, keep, a, b, c, own, other):
    x = meta[5]
    own[0] = sum4(keep, a, b, c, x).astype(BF16)
    other[0] = sum4(keep, a, b, c, 1 - x).astype(BF16)
    for k in range(4):
        total = sum4(keep, a, b, c, 2 + k).astype(BF16)
        own[1 + k] = total
        other[1 + k] = total


def after_x_kernel(meta, keep, a, b, c, own):
    for k in range(5):
        own[k] = sum4(keep, a, b, c, k).astype(BF16)


def after_y_kernel(meta, keep, a, b, c, grad_embed, grad_weight, grad_bias):
    grad_embed[...] = sum4(keep, a, b, c, 0) * (2048.0**-0.5)
    total = jnp.concatenate([sum4(keep, a, b, c, 1 + k) for k in range(4)], 1) * (1.0 / 2048.0)
    turned = total.T
    grad_weight[...] = turned[:432].reshape(9, C, C)
    grad_bias[...] = turned[432:440]


def body(bin_embed, conv_weight, conv_bias, dilation, fold_map, cotangent):
    fold, col = lax.axis_index("fold"), lax.axis_index("col")
    pair = lax.dynamic_slice_in_dim(fold_map, fold * 16 + col, 1, 0)[0]
    meta = jnp.concatenate([pair, dilation, jnp.stack([col // 4, (col // 2) % 2, col % 2])])

    def swap(value, fold_bits, col_bits):
        route = [
            (f * 16 + c, (f ^ fold_bits) * 16 + (c ^ col_bits)) for f in range(8) for c in range(16)
        ]
        return lax.ppermute(value, ("fold", "col"), route)

    core = swap(bin_embed, 0, 1)
    pair_blocks = jnp.stack([bin_embed, core])
    xlo = swap(pair_blocks, 0, 2)
    quad = jnp.concatenate([pair_blocks, xlo], 0)
    z1, z2, z3 = (swap(quad, 0, 4 * step) for step in (1, 2, 3))
    pieces = (bin_embed, core, xlo, z1, z2, z3)

    cot = cotangent[0, 0]
    cot_rows = jnp.transpose(cot, (1, 0, 2))
    cot_cols = jnp.transpose(cot, (2, 0, 1))
    flat = jnp.transpose(conv_weight, (2, 0, 1)).reshape(C, 432)
    weight = jnp.pad(flat.astype(F32), ((0, 0), (0, NK - 432)))
    bias = jnp.broadcast_to(conv_bias[:, None], (C, B))

    send, keep = backward(meta, pieces, cot_rows, cot_cols, weight, repeat_table())
    got = swap(send, 0, 1)
    half = shape((6, C, B), BF16)
    keep, to1, to2, to3 = call(after_core_kernel, (half,) * 4, 2)(meta, keep, got)
    a, b, c = swap(to1, 0, 4), swap(to2, 0, 8), swap(to3, 0, 12)
    part = shape((5, C, B), BF16)
    keep, other = call(after_z_kernel, (part, part), 4)(meta, keep, a, b, c)
    a, b, c = swap(other, 0, 2), swap(keep, 1, 0), swap(other, 1, 2)
    keep = call(after_x_kernel, part, 4)(meta, keep, a, b, c)
    a, b, c = swap(keep, 2, 0), swap(keep, 4, 0), swap(keep, 6, 0)
    grad_embed, grad_weight, grad_bias = call(
        after_y_kernel, (shape((C, B), F32), shape((9, C, C), F32), shape((8, C), F32)), 4
    )(meta, keep, a, b, c)
    pair_out = jnp.transpose(forward(meta, pieces, flat, bias), (1, 0, 2))
    return pair_out[None, None], grad_embed, grad_weight, grad_bias[0]


def solution(mesh):
    placed = (P(None, "col"), P(), P(), P(), P(), P("fold", "col", None, None, None))
    return jax.shard_map(
        body,
        mesh=mesh,
        in_specs=placed,
        out_specs=(P("fold", "col", None, None, None), P(None, "col"), P(), P()),
        check_vma=False,
    )
```

time: 654 us -> 83.4 us (0.13)
  blocking collectives: 410 us -> 0 us
  matrix products: 102 us -> 0 us
  waiting for transfers between devices: 80 us -> 13.9 us
  Pallas kernels: 0 us -> 31.9 us
  starting transfers between devices: 0.04 us -> 25.2 us
  loops' own time: 18.2 us -> 0 us
  between operations: 15.6 us -> 0.83 us
  other arithmetic: 8.46 us -> 1.43 us
    psum x1 -> x0, blocking collectives: 389 us -> none  [body(): lax.psum((inner, weight_grad, bias_grad), ('fold', 'col'))]
    dot_general x27 -> x0, matrix products: 102 us -> none  [the longest x9 57.9 us: conv_backward(): jnp.einsum('io,ors->irs', weight[tap_index], shifted, preferred_element_t...]
    psum x1 -> x0, waiting for transfers between devices: 80 us -> none  [body(): lax.psum((inner, weight_grad, bias_grad), ('fold', 'col'))]
    pallas_call x0 -> x6, Pallas kernels: none -> 31.9 us  [the longest x1 20.1 us: backward(): call(backward_kernel, (shape((12, C, B), BF16), shape((12, C, B), BF16)),...]
    ppermute x0 -> x15, starting transfers between devices: none -> 25.2 us  [swap(): return lax.ppermute(value, ('fold', 'col'), route)]
    all_gather x1 -> x0, blocking collectives: 21.8 us -> none  [body(): gathered = lax.all_gather(bin_embed, 'col', axis=1, tiled=True)]
    another operation x1 -> x0, loops' own time: 18.2 us -> none  [tile_step(): return lax.cond(row_index > col_index, two_tiles, one_tile)]
    ppermute x0 -> x15, waiting for transfers between devices: none -> 13.9 us  [swap(): return lax.ppermute(value, ('fold', 'col'), route)]
  transfers between devices with their start and end apart: 1 -> 15, of which waited for: 1 -> 8; matrix products, arithmetic and copies ran while one was open for 0% -> 9% of each run, Pallas kernels for 0% -> 11%
where the time goes in v1:
time: 83.4 us; the launch traced here: 82 us
  Pallas kernels  31.9 us (38%)
  starting transfers between devices  25.2 us (30%)
  waiting for transfers between devices  13.9 us (17%)
  local copies, waits for them, and re-layouts  8.84 us (11%)
  other arithmetic  1.43 us (2%)
    ppermute x15, starting transfers between devices, swap(): return lax.ppermute(value, ('fold', 'col'), route)  25.2 us
    pallas_call x1, Pallas kernels, backward(): call(backward_kernel, (shape((12, C, B), BF16), shape((12, C, B), BF16)),...  20.1 us
    ppermute x15, waiting for transfers between devices, swap(): return lax.ppermute(value, ('fold', 'col'), route)  13.9 us
    pallas_call x1, Pallas kernels, forward(): call(forward_kernel, shape((B, C, B), BF16), len(pieces) + 2, [pltpu.VMEM...  8.72 us
    unnamed x12, local copies, waits for them, and re-layouts  4.57 us
    transpose x1, local copies, waits for them, and re-layouts, body(): cot_rows = jnp.transpose(cot, (1, 0, 2))  2.43 us
  transfers between devices with their start and end apart: 15, of which 8 were waited for; matrix products, arithmetic and copies ran while one was open for 9% of the time, Pallas kernels for 11%

profile of v1, /device:TPU:0, one launch (start us, length us, event | category | flops | bytes accessed | tf_op | source)
XLA Modules:
  0.0 82.0 jit_solution(16944765801383569203)
XLA Ops:
  0.6 0.0 copy-start
  0.6 0.1 collective-permute-start
  0.7 1.4 %collective-permute-done.core = bf16[48,128]{1,0:T(8,128)(2,1)S(1)} collective-permute-done((bf16[48,128]{1,0:T(8,128)(2,1)}, bf16[48,128]{1,0:T(8,128)(2,1)S(1)}, u32[]{:S(2)}, u32[]{:S(2)}) %collective-permute-start) | collective-permute-done | bytes 12320 | tf_op jit(solution)/shard_map/ppermute | solution.py:373
  2.1 0.7 pad_maximum_fusion.1
  2.8 1.6 %collective-permute-start.1 = (bf16[2,48,128]{2,1,0:T(8,128)(2,1)S(1)}, bf16[2,48,128]{2,1,0:T(8,128)(2,1)S(1)}, u32[]{:S(2)}, u32[]{:S(2)}) collective-permute-start(bf16[2,48,128]{2,1,0:T(8,128)(2,1)S(1)} %pad_maximum_fusion.1), channel_id=1, source_target_pairs={{0,2},{1,3},{2,0},{3,1},{4,6},{5,7},{6,4},{7,5},{8,10},{9,11},{10,... | collective-permute-start | bytes 73736 | tf_op jit(solution)/shard_map/ppermute | solution.py:373
  4.4 1.0 %copy.15.weight = bf16[48,432]{1,0:T(8,128)(2,1)S(1)} copy(bf16[48,432]{0,1:T(8,128)(2,1)} %bitcast.25) | data formatting | bytes 82944 | tf_op jit(solution)/shard_map/reshape | solution.py:385
  5.4 1.3 %collective-permute-done.1.xlo = bf16[2,48,128]{2,1,0:T(8,128)(2,1)S(1)} collective-permute-done((bf16[2,48,128]{2,1,0:T(8,128)(2,1)S(1)}, bf16[2,48,128]{2,1,0:T(8,128)(2,1)S(1)}, u32[]{:S(2)}, u32[]{:S(2)}) %collective-permute-start.1) | collective-permute-done | bytes 24608 | tf_op jit(solution)/shard_map/ppermute | solution.py:373
  6.7 0.7 pad_maximum_fusion
  7.4 2.0 %collective-permute-start.2 = (bf16[4,48,128]{2,1,0:T(8,128)(2,1)S(1)}, bf16[4,48,128]{2,1,0:T(8,128)(2,1)S(1)}, u32[]{:S(2)}, u32[]{:S(2)}) collective-permute-start(bf16[4,48,128]{2,1,0:T(8,128)(2,1)S(1)} %pad_maximum_fusion), channel_id=1, source_target_pairs={{0,4},{1,5},{2,6},{3,7},{4,0},{5,1},{6,2},{7,3},{8,12},{9,13},{10,... | collective-permute-start | bytes 147464 | tf_op jit(solution)/shard_map/ppermute | solution.py:373
  9.4 3.6 %collective-permute-start.3 = (bf16[4,48,128]{2,1,0:T(8,128)(2,1)S(1)}, bf16[4,48,128]{2,1,0:T(8,128)(2,1)S(1)}, u32[]{:S(2)}, u32[]{:S(2)}) collective-permute-start(bf16[4,48,128]{2,1,0:T(8,128)(2,1)S(1)} %pad_maximum_fusion), channel_id=1, source_target_pairs={{0,8},{1,9},{2,10},{3,11},{4,12},{5,13},{6,14},{7,15},{8,0},{9,1},... | collective-permute-start | bytes 147464 | tf_op jit(solution)/shard_map/ppermute | solution.py:373
  13.0 0.0 collective-permute-start.4
  13.0 2.0 %copy.16 = bf16[1,1,48,128,128]{3,2,4,1,0:T(8,128)(2,1)S(1)} copy(bf16[1,1,48,128,128]{4,3,2,1,0:T(8,128)(2,1)} %param.12) | data formatting | bytes 3145728 | tf_op args[5]
  15.0 0.0 copy-start.4
  15.1 0.0 copy-start.1
  15.1 2.4 %copy.18.cot_rows = bf16[128,48,128]{2,1,0:T(8,128)(2,1)S(1)} copy(bf16[128,48,128]{2,0,1:T(8,128)(2,1)} %bitcast.24) | data formatting | bytes 3145728 | tf_op jit(solution)/shard_map/transpose | solution.py:383
  17.5 0.2 dynamic-slice_reduce_fusion
  17.7 0.1 concatenate.7.meta
  17.8 0.0 collective-permute-done.2.z1
  17.8 0.0 collective-permute-done.3.z2
  17.8 0.4 collective-permute-done.4.z3
  18.3 1.0 %copy-done.2 = bf16[2,144,448]{2,1,0:T(8,128)(2,1)S(1)} copy-done((bf16[2,144,448]{2,1,0:T(8,128)(2,1)S(1)}, bf16[2,144,448]{2,1,0:T(8,128)(2,1)}, u32[]{:S(2)}) %copy-start.2) | copy-done | bytes 258072
  19.2 20.1 %shard_map.103 = (bf16[12,48,128]{2,1,0:T(8,128)(2,1)S(1)}, bf16[12,48,128]{2,1,0:T(8,128)(2,1)S(1)}) custom-call(s32[7]{0:T(128)S(1)} %concatenate.7.meta, bf16[48,128]{1,0:T(8,128)(2,1)S(1)} %copy-done.1, bf16[48,128]{1,0:T(8,128)(2,1)S(1)} %collective-permute-done.core, bf16[2,48,128]{2,1,0:T(8,128)(2,1)S(1)} %collective-permute-done.1.xlo, ...), custom_call_target="tpu_custom_call" | custom-call | flops 1409286144 | bytes 3145728 | tf_op jit(solution)/shard_map/pallas_call | solution.py:295
  39.3 0.1 collective-permute-start.5
  39.4 1.4 %collective-permute-done.5.got = bf16[12,48,128]{2,1,0:T(8,128)(2,1)S(1)} collective-permute-done((bf16[12,48,128]{2,1,0:T(8,128)(2,1)S(1)}, bf16[12,48,128]{2,1,0:T(8,128)(2,1)S(1)}, u32[]{:S(2)}, u32[]{:S(2)}) %collective-permute-start.5) | collective-permute-done | bytes 147488 | tf_op jit(solution)/shard_map/ppermute | solution.py:373
  40.8 0.6 shard_map.104
  41.3 0.1 collective-permute-start.6
  41.4 4.3 %collective-permute-start.7 = (bf16[6,48,128]{2,1,0:T(8,128)(2,1)S(1)}, bf16[6,48,128]{2,1,0:T(8,128)(2,1)S(1)}, u32[]{:S(2)}, u32[]{:S(2)}) collective-permute-start(bf16[6,48,128]{2,1,0:T(8,128)(2,1)S(1)} %get-tuple-element.19), channel_id=1, source_target_pairs={{0,8},{1,9},{2,10},{3,11},{4,12},{5,13},{6,14},{7,15},{8,0},{9,1},... | collective-permute-start | bytes 221192 | tf_op jit(solution)/shard_map/ppermute | solution.py:373
  45.7 0.4 collective-permute-start.8
  46.1 0.0 collective-permute-done.6.a
  46.1 3.5 %collective-permute-done.7.b = bf16[6,48,128]{2,1,0:T(8,128)(2,1)S(1)} collective-permute-done((bf16[6,48,128]{2,1,0:T(8,128)(2,1)S(1)}, bf16[6,48,128]{2,1,0:T(8,128)(2,1)S(1)}, u32[]{:S(2)}, u32[]{:S(2)}) %collective-permute-start.7) | collective-permute-done | bytes 73760 | tf_op jit(solution)/shard_map/ppermute | solution.py:373
  49.6 1.6 %collective-permute-done.8.c = bf16[6,48,128]{2,1,0:T(8,128)(2,1)S(1)} collective-permute-done((bf16[6,48,128]{2,1,0:T(8,128)(2,1)S(1)}, bf16[6,48,128]{2,1,0:T(8,128)(2,1)S(1)}, u32[]{:S(2)}, u32[]{:S(2)}) %collective-permute-start.8) | collective-permute-done | bytes 73760 | tf_op jit(solution)/shard_map/ppermute | solution.py:373
  51.3 0.6 shard_map.105
  51.9 3.1 %collective-permute-start.10 = (bf16[5,48,128]{2,1,0:T(8,128)(2,1)S(1)}, bf16[5,48,128]{2,1,0:T(8,128)(2,1)S(1)}, u32[]{:S(2)}, u32[]{:S(2)}) collective-permute-start(bf16[5,48,128]{2,1,0:T(8,128)(2,1)S(1)} %get-tuple-element.21.keep), channel_id=1, source_target_pairs={{0,16},{1,17},{2,18},{3,19},{4,20},{5,21},{6,22},{7,23},{8,24},{9,... | collective-permute-start | bytes 184328 | tf_op jit(solution)/shard_map/ppermute | solution.py:373
  55.0 1.1 %collective-permute-start.11 = (bf16[5,48,128]{2,1,0:T(8,128)(2,1)S(1)}, bf16[5,48,128]{2,1,0:T(8,128)(2,1)S(1)}, u32[]{:S(2)}, u32[]{:S(2)}) collective-permute-start(bf16[5,48,128]{2,1,0:T(8,128)(2,1)S(1)} %get-tuple-element.22), channel_id=1, source_target_pairs={{0,18},{1,19},{2,16},{3,17},{4,22},{5,23},{6,20},{7,21},{8,26},{9,... | collective-permute-start | bytes 184328 | tf_op jit(solution)/shard_map/ppermute | solution.py:373
  56.1 0.0 collective-permute-start.9
  56.1 1.6 %collective-permute-done.10.b = bf16[5,48,128]{2,1,0:T(8,128)(2,1)S(1)} collective-permute-done((bf16[5,48,128]{2,1,0:T(8,128)(2,1)S(1)}, bf16[5,48,128]{2,1,0:T(8,128)(2,1)S(1)}, u32[]{:S(2)}, u32[]{:S(2)}) %collective-permute-start.10) | collective-permute-done | bytes 61472 | tf_op jit(solution)/shard_map/ppermute | solution.py:373
  57.7 2.7 %collective-permute-done.11.c = bf16[5,48,128]{2,1,0:T(8,128)(2,1)S(1)} collective-permute-done((bf16[5,48,128]{2,1,0:T(8,128)(2,1)S(1)}, bf16[5,48,128]{2,1,0:T(8,128)(2,1)S(1)}, u32[]{:S(2)}, u32[]{:S(2)}) %collective-permute-start.11) | collective-permute-done | bytes 61472 | tf_op jit(solution)/shard_map/ppermute | solution.py:373
  60.4 0.6 shard_map.106.keep
  61.0 6.0 %collective-permute-start.12 = (bf16[5,48,128]{2,1,0:T(8,128)(2,1)S(1)}, bf16[5,48,128]{2,1,0:T(8,128)(2,1)S(1)}, u32[]{:S(2)}, u32[]{:S(2)}) collective-permute-start(bf16[5,48,128]{2,1,0:T(8,128)(2,1)S(1)} %shard_map.106.keep), channel_id=1, source_target_pairs={{0,32},{1,33},{2,34},{3,35},{4,36},{5,37},{6,38},{7,39},{8,40},{9,... | collective-permute-start | bytes 184328 | tf_op jit(solution)/shard_map/ppermute | solution.py:373
  67.0 0.7 collective-permute-start.13
  67.7 2.1 %collective-permute-start.14 = (bf16[5,48,128]{2,1,0:T(8,128)(2,1)S(1)}, bf16[5,48,128]{2,1,0:T(8,128)(2,1)S(1)}, u32[]{:S(2)}, u32[]{:S(2)}) collective-permute-start(bf16[5,48,128]{2,1,0:T(8,128)(2,1)S(1)} %shard_map.106.keep), channel_id=1, source_target_pairs={{0,96},{1,97},{2,98},{3,99},{4,100},{5,101},{6,102},{7,103},{8,104... | collective-permute-start | bytes 184328 | tf_op jit(solution)/shard_map/ppermute | solution.py:373
  69.8 0.1 broadcast_in_dim.4.bias
  69.9 8.7 %shard_map.102 = bf16[128,48,128]{2,1,0:T(8,128)(2,1)S(1)} custom-call(s32[7]{0:T(128)S(1)} %concatenate.7.meta, bf16[48,128]{1,0:T(8,128)(2,1)S(1)} %copy-done.1, bf16[48,128]{1,0:T(8,128)(2,1)S(1)} %collective-permute-done.core, bf16[2,48,128]{2,1,0:T(8,128)(2,1)S(1)} %collective-permute-done.1.xlo, bf16[4,48,128]{2,1,0:T(8,128)(2,1)S(1)} %collective-permute-done.2.z1, ...), custom_call_target="tpu_custom_call" | custom-call | flops 679477248 | bytes 1572864 | tf_op jit(solution)/shard_map/pallas_call | solution.py:313
  78.6 1.6 %copy.19 = bf16[1,1,48,128,128]{4,3,2,1,0:T(8,128)(2,1)} copy(bf16[1,1,48,128,128]{4,2,3,1,0:T(8,128)(2,1)S(1)} %bitcast.19) | data formatting | bytes 3145728
  80.1 0.0 collective-permute-done.12.a
  80.2 0.0 collective-permute-done.13.b
  80.2 1.4 %shard_map.107 = (f32[48,128]{1,0:T(8,128)}, f32[9,48,48]{2,1,0:T(8,128)}, f32[8,48]{1,0:T(8,128)S(1)}) custom-call(s32[7]{0:T(128)S(1)} %concatenate.7.meta, bf16[5,48,128]{2,1,0:T(8,128)(2,1)S(1)} %shard_map.106.keep, bf16[5,48,128]{2,1,0:T(8,128)(2,1)S(1)} %collective-permute-done.12.a, bf16[5,48,128]{2,1,0:T(8,128)(2,1)S(1)} %collective-permute-done.13.b, ...), custom_call_target="tpu_custom_call" | custom-call | tf_op jit(solution)/shard_map/pallas_call | solution.py:399
  81.5 0.5 slice_bitcast_fusion
  (9 shorter events, 0.0 us)
Async XLA Ops:
  0.6 16.9 %copy-start = (s32[128,2]{0,1:T(2,128)S(1)}, s32[128,2]{0,1:T(2,128)}, u32[]{:S(2)}) copy-start(s32[128,2]{0,1:T(2,128)} %param.11) | copy-start | bytes 3076
  0.6 1.5 %collective-permute-start = (bf16[48,128]{1,0:T(8,128)(2,1)}, bf16[48,128]{1,0:T(8,128)(2,1)S(1)}, u32[]{:S(2)}, u32[]{:S(2)}) collective-permute-start(bf16[48,128]{1,0:T(8,128)(2,1)} %own.3), channel_id=1, source_target_pairs={{0,1},{1,0},{2,3},{3,2},{4,5},{5,4},{6,7},{7,6},{8,9},{9,8},{10,11... | collective-permute-start | bytes 36872 | tf_op jit(solution)/shard_map/ppermute | solution.py:373
  2.8 3.8 %collective-permute-start.1 = (bf16[2,48,128]{2,1,0:T(8,128)(2,1)S(1)}, bf16[2,48,128]{2,1,0:T(8,128)(2,1)S(1)}, u32[]{:S(2)}, u32[]{:S(2)}) collective-permute-start(bf16[2,48,128]{2,1,0:T(8,128)(2,1)S(1)} %pad_maximum_fusion.1), channel_id=1, source_target_pairs={{0,2},{1,3},{2,0},{3,1},{4,6},{5,7},{6,4},{7,5},{8,10},{9,11},{10,... | collective-permute-start | bytes 73736 | tf_op jit(solution)/shard_map/ppermute | solution.py:373
  7.4 10.5 %collective-permute-start.2 = (bf16[4,48,128]{2,1,0:T(8,128)(2,1)S(1)}, bf16[4,48,128]{2,1,0:T(8,128)(2,1)S(1)}, u32[]{:S(2)}, u32[]{:S(2)}) collective-permute-start(bf16[4,48,128]{2,1,0:T(8,128)(2,1)S(1)} %pad_maximum_fusion), channel_id=1, source_target_pairs={{0,4},{1,5},{2,6},{3,7},{4,0},{5,1},{6,2},{7,3},{8,12},{9,13},{10,... | collective-permute-start | bytes 147464 | tf_op jit(solution)/shard_map/ppermute | solution.py:373
  9.4 8.5 %collective-permute-start.3 = (bf16[4,48,128]{2,1,0:T(8,128)(2,1)S(1)}, bf16[4,48,128]{2,1,0:T(8,128)(2,1)S(1)}, u32[]{:S(2)}, u32[]{:S(2)}) collective-permute-start(bf16[4,48,128]{2,1,0:T(8,128)(2,1)S(1)} %pad_maximum_fusion), channel_id=1, source_target_pairs={{0,8},{1,9},{2,10},{3,11},{4,12},{5,13},{6,14},{7,15},{8,0},{9,1},... | collective-permute-start | bytes 147464 | tf_op jit(solution)/shard_map/ppermute | solution.py:373
  13.0 5.3 %collective-permute-start.4 = (bf16[4,48,128]{2,1,0:T(8,128)(2,1)S(1)}, bf16[4,48,128]{2,1,0:T(8,128)(2,1)S(1)}, u32[]{:S(2)}, u32[]{:S(2)}) collective-permute-start(bf16[4,48,128]{2,1,0:T(8,128)(2,1)S(1)} %pad_maximum_fusion), channel_id=1, source_target_pairs={{0,12},{1,13},{2,14},{3,15},{4,8},{5,9},{6,10},{7,11},{8,4},{9,5},... | collective-permute-start | bytes 147464 | tf_op jit(solution)/shard_map/ppermute | solution.py:373
  15.0 2.7 %copy-start.4 = (s32[2]{0:T(128)S(1)}, s32[2]{0:T(128)}, u32[]{:S(2)}) copy-start(s32[2]{0:T(128)} %param.10) | copy-start | bytes 28
  15.1 3.2 %copy-start.1 = (bf16[48,128]{1,0:T(8,128)(2,1)S(1)}, bf16[48,128]{1,0:T(8,128)(2,1)}, u32[]{:S(2)}) copy-start(bf16[48,128]{1,0:T(8,128)(2,1)} %own.3) | copy-start | bytes 36868
  18.3 1.0 %copy-start.2 = (bf16[2,144,448]{2,1,0:T(8,128)(2,1)S(1)}, bf16[2,144,448]{2,1,0:T(8,128)(2,1)}, u32[]{:S(2)}) copy-start(bf16[2,144,448]{2,1,0:T(8,128)(2,1)} %constant.57.clone.repeat) | copy-start | bytes 774148
  19.2 50.6 %copy-start.3 = (f32[48]{0:T(128)S(1)}, f32[48]{0:T(128)}, u32[]{:S(2)}) copy-start(f32[48]{0:T(128)} %param.9) | copy-start | bytes 580
  39.3 1.5 %collective-permute-start.5 = (bf16[12,48,128]{2,1,0:T(8,128)(2,1)S(1)}, bf16[12,48,128]{2,1,0:T(8,128)(2,1)S(1)}, u32[]{:S(2)}, u32[]{:S(2)}) collective-permute-start(bf16[12,48,128]{2,1,0:T(8,128)(2,1)S(1)} %get-tuple-element.16), channel_id=1, source_target_pairs={{0,1},{1,0},{2,3},{3,2},{4,5},{5,4},{6,7},{7,6},{8,9},{9,8},{10,11... | collective-permute-start | bytes 442376 | tf_op jit(solution)/shard_map/ppermute | solution.py:373
  41.3 4.8 %collective-permute-start.6 = (bf16[6,48,128]{2,1,0:T(8,128)(2,1)S(1)}, bf16[6,48,128]{2,1,0:T(8,128)(2,1)S(1)}, u32[]{:S(2)}, u32[]{:S(2)}) collective-permute-start(bf16[6,48,128]{2,1,0:T(8,128)(2,1)S(1)} %get-tuple-element.18), channel_id=1, source_target_pairs={{0,4},{1,5},{2,6},{3,7},{4,0},{5,1},{6,2},{7,3},{8,12},{9,13},{10,... | collective-permute-start | bytes 221192 | tf_op jit(solution)/shard_map/ppermute | solution.py:373
  41.4 8.2 %collective-permute-start.7 = (bf16[6,48,128]{2,1,0:T(8,128)(2,1)S(1)}, bf16[6,48,128]{2,1,0:T(8,128)(2,1)S(1)}, u32[]{:S(2)}, u32[]{:S(2)}) collective-permute-start(bf16[6,48,128]{2,1,0:T(8,128)(2,1)S(1)} %get-tuple-element.19), channel_id=1, source_target_pairs={{0,8},{1,9},{2,10},{3,11},{4,12},{5,13},{6,14},{7,15},{8,0},{9,1},... | collective-permute-start | bytes 221192 | tf_op jit(solution)/shard_map/ppermute | solution.py:373
  45.7 5.6 %collective-permute-start.8 = (bf16[6,48,128]{2,1,0:T(8,128)(2,1)S(1)}, bf16[6,48,128]{2,1,0:T(8,128)(2,1)S(1)}, u32[]{:S(2)}, u32[]{:S(2)}) collective-permute-start(bf16[6,48,128]{2,1,0:T(8,128)(2,1)S(1)} %get-tuple-element.20), channel_id=1, source_target_pairs={{0,12},{1,13},{2,14},{3,15},{4,8},{5,9},{6,10},{7,11},{8,4},{9,5},... | collective-permute-start | bytes 221192 | tf_op jit(solution)/shard_map/ppermute | solution.py:373
  51.9 5.8 %collective-permute-start.10 = (bf16[5,48,128]{2,1,0:T(8,128)(2,1)S(1)}, bf16[5,48,128]{2,1,0:T(8,128)(2,1)S(1)}, u32[]{:S(2)}, u32[]{:S(2)}) collective-permute-start(bf16[5,48,128]{2,1,0:T(8,128)(2,1)S(1)} %get-tuple-element.21.keep), channel_id=1, source_target_pairs={{0,16},{1,17},{2,18},{3,19},{4,20},{5,21},{6,22},{7,23},{8,24},{9,... | collective-permute-start | bytes 184328 | tf_op jit(solution)/shard_map/ppermute | solution.py:373
  55.0 5.4 %collective-permute-start.11 = (bf16[5,48,128]{2,1,0:T(8,128)(2,1)S(1)}, bf16[5,48,128]{2,1,0:T(8,128)(2,1)S(1)}, u32[]{:S(2)}, u32[]{:S(2)}) collective-permute-start(bf16[5,48,128]{2,1,0:T(8,128)(2,1)S(1)} %get-tuple-element.22), channel_id=1, source_target_pairs={{0,18},{1,19},{2,16},{3,17},{4,22},{5,23},{6,20},{7,21},{8,26},{9,... | collective-permute-start | bytes 184328 | tf_op jit(solution)/shard_map/ppermute | solution.py:373
  56.1 4.3 %collective-permute-start.9 = (bf16[5,48,128]{2,1,0:T(8,128)(2,1)S(1)}, bf16[5,48,128]{2,1,0:T(8,128)(2,1)S(1)}, u32[]{:S(2)}, u32[]{:S(2)}) collective-permute-start(bf16[5,48,128]{2,1,0:T(8,128)(2,1)S(1)} %get-tuple-element.22), channel_id=1, source_target_pairs={{0,2},{1,3},{2,0},{3,1},{4,6},{5,7},{6,4},{7,5},{8,10},{9,11},{10,... | collective-permute-start | bytes 184328 | tf_op jit(solution)/shard_map/ppermute | solution.py:373
  61.0 19.2 %collective-permute-start.12 = (bf16[5,48,128]{2,1,0:T(8,128)(2,1)S(1)}, bf16[5,48,128]{2,1,0:T(8,128)(2,1)S(1)}, u32[]{:S(2)}, u32[]{:S(2)}) collective-permute-start(bf16[5,48,128]{2,1,0:T(8,128)(2,1)S(1)} %shard_map.106.keep), channel_id=1, source_target_pairs={{0,32},{1,33},{2,34},{3,35},{4,36},{5,37},{6,38},{7,39},{8,40},{9,... | collective-permute-start | bytes 184328 | tf_op jit(solution)/shard_map/ppermute | solution.py:373
  67.0 13.1 %collective-permute-start.13 = (bf16[5,48,128]{2,1,0:T(8,128)(2,1)S(1)}, bf16[5,48,128]{2,1,0:T(8,128)(2,1)S(1)}, u32[]{:S(2)}, u32[]{:S(2)}) collective-permute-start(bf16[5,48,128]{2,1,0:T(8,128)(2,1)S(1)} %shard_map.106.keep), channel_id=1, source_target_pairs={{0,64},{1,65},{2,66},{3,67},{4,68},{5,69},{6,70},{7,71},{8,72},{9,... | collective-permute-start | bytes 184328 | tf_op jit(solution)/shard_map/ppermute | solution.py:373
  67.7 12.4 %collective-permute-start.14 = (bf16[5,48,128]{2,1,0:T(8,128)(2,1)S(1)}, bf16[5,48,128]{2,1,0:T(8,128)(2,1)S(1)}, u32[]{:S(2)}, u32[]{:S(2)}) collective-permute-start(bf16[5,48,128]{2,1,0:T(8,128)(2,1)S(1)} %shard_map.106.keep), channel_id=1, source_target_pairs={{0,96},{1,97},{2,98},{3,99},{4,100},{5,101},{6,102},{7,103},{8,104... | collective-permute-start | bytes 184328 | tf_op jit(solution)/shard_map/ppermute | solution.py:373

commit v2 on v1

v2 whole, which is shorter than its diff:
```python
import functools

import jax
import jax.numpy as jnp
import numpy as np
from jax import lax
from jax.experimental import pallas as pl
from jax.experimental.pallas import tpu as pltpu
from jax.sharding import PartitionSpec as P

C = 48
B = 128
DMAX = 16
NK = 512
OUTSIDE = -16384.0
F32 = jnp.float32
BF16 = jnp.bfloat16
UNROLL = 16
PARTS = 4
ROWS = 32
PAD = 8
PIECES = ((0, 48), (48, 48), (96, 32))
VMEM_BYTES = 48 * 1024 * 1024

NT = (((1,), (1,)), ((), ()))
TN = (((0,), (0,)), ((), ()))
NN = (((1,), (0,)), ((), ()))


def dot(a, b, dims):
    return lax.dot_general(a, b, dims, preferred_element_type=F32)


def repeat_table():
    table = np.zeros((2, 144, NK), np.float32)
    for u in range(3):
        for v in range(3):
            for i in range(C):
                column = (3 * u + v) * C + i
                table[0, u * C + i, column] = 1.0
                table[1, v * C + i, column] = 1.0
    return jnp.asarray(table, BF16)


def fill_blocks(meta, own, core, xlo, both, z1, z2, z3, blocks):
    z, x, c = meta[4], meta[5], meta[6]
    blocks[0] = jnp.full((C, B), OUTSIDE, F32)
    blocks[17] = jnp.full((C, B), OUTSIDE, F32)
    here = 1 + z * 4
    blocks[here + x * 2 + c] = own[...].astype(F32)
    blocks[here + x * 2 + (1 - c)] = core[...].astype(F32)
    blocks[here + (1 - x) * 2 + c] = xlo[...].astype(F32)
    blocks[here + (1 - x) * 2 + (1 - c)] = both[...].astype(F32)
    for step, got in ((1, z1), (2, z2), (3, z3)):
        there = 1 + (z ^ step) * 4
        blocks[there + x * 2 + c] = got[0].astype(F32)
        blocks[there + x * 2 + (1 - c)] = got[1].astype(F32)
        blocks[there + (1 - x) * 2 + c] = got[2].astype(F32)
        blocks[there + (1 - x) * 2 + (1 - c)] = got[3].astype(F32)


def spread_lanes(blocks, tile, table, first, count):
    before, here, after = blocks[tile], blocks[tile + 1], blocks[tile + 2]
    for q in range(first - DMAX, first + count + DMAX):
        source, lane = (before, q + B) if q < 0 else ((here, q) if q < B else (after, q - B))
        table[q - first + DMAX] = jnp.broadcast_to(source[:, lane : lane + 1], (C, B)).astype(BF16)


def windows(blocks, tile, rate):
    lane = lax.broadcasted_iota(jnp.int32, (C, B), 1)
    before, here, after = blocks[tile], blocks[tile + 1], blocks[tile + 2]
    low = jnp.where(lane < rate, pltpu.roll(before, rate, 1), pltpu.roll(here, rate, 1))
    high = jnp.where(lane >= B - rate, pltpu.roll(after, B - rate, 1), pltpu.roll(here, B - rate, 1))
    return [low.astype(BF16), here.astype(BF16), high.astype(BF16)]


def scatter_back(grads, tile, rate, shifted):
    lane = lax.broadcasted_iota(jnp.int32, (C, B), 1)
    low, here, high = shifted
    low = pltpu.roll(low, B - rate, 1)
    high = pltpu.roll(high, rate, 1)
    zero = jnp.zeros((C, B), F32)
    grads[tile] += jnp.where(lane >= B - rate, low, zero)
    grads[tile + 2] += jnp.where(lane < rate, high, zero)
    grads[tile + 1] += (
        jnp.where(lane < B - rate, low, zero) + here + jnp.where(lane >= rate, high, zero)
    )


def bias_lanes(bias):
    return jnp.broadcast_to(bias[...], (B, C)).T


def store_rows(full, bias, first, stage32, count):
    for k in range(full.shape[1] // B):
        stage32[pl.ds(first + k, C, stride=count + PAD), :] = full[:, k * B : (k + 1) * B] + bias


def round_rows(stage32, stage, count):
    for c in range(C):
        stage[c] = stage32[c * (count + PAD) : c * (count + PAD) + count, :].astype(BF16)


def gradient_kernel(
    meta, own, core, xlo, both, z1, z2, z3, conv_weight, conv_bias, repeat, cot_hbm, cols_hbm,
    send, keep, around, pair_hbm,
    blocks, shift, minus, sums, grads, wgrad, table, cot, rows, cols, cot32, stage32, stage, sems,
):
    tile_i, tile_j, rate_r, rate_c, core_index = meta[0], meta[1], meta[2], meta[3], meta[6]
    load_cot = pltpu.make_async_copy(cot_hbm, cot, sems.at[0])
    load_cols = pltpu.make_async_copy(cols_hbm, cols, sems.at[1])
    load_cot.start()
    load_cols.start()
    fill_blocks(meta, own, core, xlo, both, z1, z2, z3, blocks)
    for k in range(3):
        around[k] = blocks[tile_i + k]
        around[3 + k] = blocks[tile_j + k]
    one, zero = jnp.ones((), BF16), jnp.zeros((), BF16)
    column = lax.broadcasted_iota(jnp.int32, (B, NK), 1)
    bias_mark = jnp.where(column == 432, 1.0, 0.0)
    grads[...] = jnp.zeros_like(grads)
    weight = conv_weight[...].astype(F32).T
    weight_wide = jnp.concatenate([weight, jnp.zeros((C, NK - 432), F32)], 1)
    empty = jnp.zeros((C, NK), F32)

    def tables(slot, tile, rate, which, mark):
        table = dot(jnp.concatenate(windows(blocks, tile, rate), 0), repeat[which], TN)
        minus[slot] = (-table).astype(BF16)
        shift[slot] = table + bias_mark if mark else table

    def back_sums(slot, tile, rate, which):
        tiles = []
        for at in range(NK // B):
            total = sums[slot, at, pl.ds(0, B, stride=8), :]
            for part in range(1, 8):
                total += sums[slot, at, pl.ds(part, B, stride=8), :]
            tiles.append(total)
        total = jnp.concatenate(tiles, 1)
        high = total.astype(BF16)
        low = (total - high.astype(F32)).astype(BF16)
        merged = dot(repeat[which], high, NT) + dot(repeat[which], low, NT)
        scatter_back(grads, tile, rate, [merged[k * C : (k + 1) * C] for k in range(3)])

    def loop(steps, start, first=0, last=B):
        def several(outer, carry):
            for inner in range(UNROLL):
                for step in steps:
                    carry = step(outer * UNROLL + inner, carry)
            return carry

        return lax.fori_loop(first // UNROLL, last // UNROLL, several, start)

    def take(slot, q, products, total):
        weighted = products * weight_wide
        partial = weighted[:8]
        for part in range(1, C // 8):
            partial += weighted[8 * part : 8 * part + 8]
        for at in range(NK // B):
            sums[slot, at, pl.ds(pl.multiple_of(q * 8, 8), 8), :] = partial[:, at * B : (at + 1) * B]
        return total + products * shift[slot, pl.ds(q, 1), :]

    def row_of(q):
        return rows[q]

    def col_of(q):
        return cols[q]

    def cotangent_here():
        load_cot.wait()
        for c in range(C):
            cot32[c * (B + PAD) : c * (B + PAD) + B, :] = cot[c].astype(F32)
        for q in range(B):
            rows[q] = cot32[pl.ds(q, C, stride=B + PAD), :].astype(BF16)
        load_cols.wait()

    @pl.when(tile_i < tile_j)
    def one_tile():
        spread_lanes(blocks, tile_i, table, 0, B)
        bias, short = bias_lanes(conv_bias), weight.astype(BF16)
        window = windows(blocks, tile_j, rate_c)

        def some(step, carry):
            parts = []
            for k in range(ROWS):
                at = [table[DMAX + step * ROWS + k + m * rate_r] for m in (-1, 0, 1)]
                taps = [jnp.maximum(at[u] + window[v], zero) for u in range(3) for v in range(3)]
                parts.append(jnp.concatenate(taps, 0))
            store_rows(dot(short, jnp.concatenate(parts, 1), NN), bias, step * ROWS, stage32, B)
            return carry

        lax.fori_loop(0, B // ROWS, some, 0)
        round_rows(stage32, stage, B)
        save_pair = pltpu.make_async_copy(stage, pair_hbm, sems.at[2])
        save_pair.start()

        tables(0, tile_i, rate_r, 0, True)
        tables(1, tile_j, rate_c, 1, False)
        cotangent_here()

        def half(slot, other, grad_of):
            def step(q, total):
                at = jnp.broadcast_to(shift[slot, pl.ds(q, 1), :], (16, NK)).astype(BF16)
                at = jnp.concatenate([at] * (B // 16), 0)
                mask = jnp.where(at > minus[other], one, zero)
                return take(slot, q, dot(grad_of(q), mask, NN), total)

            return step

        wgrad[...] = loop([half(0, 1, row_of), half(1, 0, col_of)], empty)
        back_sums(0, tile_i, rate_r, 0)
        back_sums(1, tile_j, rate_c, 1)
        save_pair.wait()

    @pl.when(tile_i > tile_j)
    def two_triangles():
        tables(0, tile_i, rate_r, 0, True)
        tables(1, tile_i, rate_c, 1, False)
        tables(2, tile_j, rate_c, 1, True)
        tables(3, tile_j, rate_r, 0, False)
        cotangent_here()
        lane = lax.broadcasted_iota(jnp.int32, (C, B), 1).astype(BF16)

        def half(slot, other, grad_of, side, live):
            def step(q, total):
                at = jnp.broadcast_to(shift[slot, pl.ds(q, 1), :], (16, NK)).astype(BF16)
                at = jnp.concatenate([at] * ((live.stop - live.start) // 16), 0)
                mask = jnp.where(at > minus[other, live, :], one, zero)
                pads = [jnp.zeros((n, NK), BF16) for n in (live.start, B - live.stop)]
                mask = jnp.concatenate([x for x in (pads[0], mask, pads[1]) if x.shape[0]], 0)
                place = jnp.full((C, B), q, F32).astype(BF16)
                grad = jnp.where(side(lane, place), grad_of(q), zero)
                return take(slot, q, dot(grad, mask, NN), total)

            return step

        total = empty
        for part in range(PARTS):
            lines = (part * B // PARTS, (part + 1) * B // PARTS)
            after, before = slice(lines[0], B), slice(0, lines[1])
            total = loop(
                [
                    half(0, 1, row_of, lambda s, r: s >= r, after),
                    half(1, 0, col_of, lambda r, s: r <= s, before),
                    half(2, 3, row_of, lambda s, r: s < r, before),
                    half(3, 2, col_of, lambda r, s: r > s, after),
                ],
                total,
                *lines,
            )
        wgrad[...] = total
        back_sums(0, tile_i, rate_r, 0)
        back_sums(1, tile_i, rate_c, 1)
        back_sums(2, tile_j, rate_c, 1)
        back_sums(3, tile_j, rate_r, 0)

    for pair in range(8):
        send[pair] = grads[1 + 2 * pair + (1 - core_index)]
        keep[pair] = grads[1 + 2 * pair + core_index]
    total = wgrad[...]
    for part in range(4):
        piece = total[:, part * B : (part + 1) * B]
        send[8 + part] = piece
        keep[8 + part] = piece


def fold_kernel(
    first, count, meta, around, conv_weight, conv_bias, pair_before, after, pair_hbm, token,
    table_i, table_j, stage32, stage, sem,
):
    tile_i, tile_j, rate_r, rate_c = meta[0], meta[1], meta[2], meta[3]
    token[...] = jnp.zeros_like(token)

    @pl.when(tile_i > tile_j)
    def two_triangles():
        spread_lanes(around, 0, table_i, first, count)
        spread_lanes(around, 3, table_j, first, count)
        up_window, low_window = windows(around, 0, rate_c), windows(around, 3, rate_r)
        lane = lax.broadcasted_iota(jnp.int32, (C, B), 1)
        bias, short = bias_lanes(conv_bias), conv_weight[...].astype(F32).T.astype(BF16)
        zero = jnp.zeros((), BF16)

        def some(step, carry):
            parts = []
            for k in range(16):
                q = step * 16 + k
                upper = lane >= first + q
                up = [table_i[DMAX + q + m * rate_r] for m in (-1, 0, 1)]
                low = [table_j[DMAX + q + m * rate_c] for m in (-1, 0, 1)]
                taps = [
                    jnp.where(upper, up[u] + up_window[v], low[v] + low_window[u])
                    for u in range(3)
                    for v in range(3)
                ]
                parts.append(jnp.concatenate([jnp.maximum(x, zero) for x in taps], 0))
            store_rows(dot(short, jnp.concatenate(parts, 1), NN), bias, step * 16, stage32, count)
            return carry

        lax.fori_loop(0, count // 16, some, 0)
        round_rows(stage32, stage, count)
        save = pltpu.make_async_copy(stage, pair_hbm.at[:, pl.ds(first, count), :], sem)
        save.start()
        save.wait()


def shape(dims, kind):
    return jax.ShapeDtypeStruct(dims, kind)


SMEM = pl.BlockSpec(memory_space=pltpu.SMEM)
VMEM = pl.BlockSpec(memory_space=pltpu.VMEM)
ANY = pl.BlockSpec(memory_space=pl.ANY)


def call(kernel, in_specs, out_shape, out_specs, scratch=(), aliases={}):
    return pl.pallas_call(
        kernel,
        out_shape=out_shape,
        in_specs=in_specs,
        out_specs=out_specs,
        scratch_shapes=list(scratch),
        input_output_aliases=aliases,
        compiler_params=pltpu.CompilerParams(vmem_limit_bytes=VMEM_BYTES),
    )


def gradients(meta, pieces, conv_weight, conv_bias, cot, cot_cols):
    return call(
        gradient_kernel,
        [SMEM] + [VMEM] * (len(pieces) + 3) + [ANY, ANY],
        (shape((12, C, B), F32), shape((12, C, B), F32), shape((6, C, B), F32), shape((C, B, B), BF16)),
        (VMEM, VMEM, VMEM, ANY),
        [
            pltpu.VMEM((18, C, B), F32),
            pltpu.VMEM((4, B, NK), F32),
            pltpu.VMEM((4, B, NK), BF16),
            pltpu.VMEM((4, NK // B, 8 * B, B), F32),
            pltpu.VMEM((18, C, B), F32),
            pltpu.VMEM((C, NK), F32),
            pltpu.VMEM((B + 2 * DMAX, C, B), BF16),
            pltpu.VMEM((C, B, B), BF16),
            pltpu.VMEM((B, C, B), BF16),
            pltpu.VMEM((B, C, B), BF16),
            pltpu.VMEM((C * (B + PAD), B), F32),
            pltpu.VMEM((C * (B + PAD), B), F32),
            pltpu.VMEM((C, B, B), BF16),
            pltpu.SemaphoreType.DMA((3,)),
        ],
    )(meta, *pieces, conv_weight, conv_bias, repeat_table(), cot, cot_cols)


def fold(which, meta, around, conv_weight, conv_bias, pair, after):
    first, count = PIECES[which]
    return call(
        functools.partial(fold_kernel, first, count),
        [SMEM, VMEM, VMEM, VMEM, ANY, ANY],
        (shape((C, B, B), BF16), shape((8, B), F32)),
        (ANY, VMEM),
        [
            pltpu.VMEM((count + 2 * DMAX, C, B), BF16),
            pltpu.VMEM((count + 2 * DMAX, C, B), BF16),
            pltpu.VMEM((C * (count + PAD), B), F32),
            pltpu.VMEM((C, count, B), BF16),
            pltpu.SemaphoreType.DMA,
        ],
        {4: 0},
    )(meta, around, conv_weight, conv_bias, pair, after)


def after_core_kernel(meta, keep, got, own, to1, to2, to3):
    z = meta[4]
    total = [(keep[k] + got[k]).astype(BF16) for k in range(8, 12)]
    for step, out in ((0, own), (1, to1), (2, to2), (3, to3)):
        first = (z ^ step) * 2
        for k in range(2):
            out[k] = (keep[first + k] + got[first + k]).astype(BF16)
        for k in range(4):
            out[2 + k] = total[k]


def sum4(own, a, b, c, k):
    return (own[k].astype(F32) + a[k].astype(F32)) + (b[k].astype(F32) + c[k].astype(F32))


def after_z_kernel(meta, keep, a, b, c, token, own, other):
    x = meta[5]
    own[0] = sum4(keep, a, b, c, x).astype(BF16)
    other[0] = sum4(keep, a, b, c, 1 - x).astype(BF16)
    for k in range(4):
        total = sum4(keep, a, b, c, 2 + k).astype(BF16)
        own[1 + k] = total
        other[1 + k] = total


def after_x_kernel(meta, keep, a, b, c, token, own):
    for k in range(5):
        own[k] = sum4(keep, a, b, c, k).astype(BF16)


def after_y_kernel(meta, keep, a, b, c, grad_embed, grad_weight, grad_bias):
    grad_embed[...] = sum4(keep, a, b, c, 0) * (2048.0**-0.5)
    total = jnp.concatenate([sum4(keep, a, b, c, 1 + k) for k in range(4)], 1) * (1.0 / 2048.0)
    turned = total.T
    grad_weight[...] = turned[:432].reshape(9, C, C)
    grad_bias[...] = turned[432:433]


def body(bin_embed, conv_weight, conv_bias, dilation, fold_map, cotangent):
    fold_at, col = lax.axis_index("fold"), lax.axis_index("col")
    pair = lax.dynamic_slice_in_dim(fold_map, fold_at * 16 + col, 1, 0)[0]
    meta = jnp.concatenate([pair, dilation, jnp.stack([col // 4, (col // 2) % 2, col % 2])])

    def swap(value, fold_bits, col_bits):
        route = [
            (f * 16 + c, (f ^ fold_bits) * 16 + (c ^ col_bits)) for f in range(8) for c in range(16)
        ]
        return lax.ppermute(value, ("fold", "col"), route)

    core, xlo, both = swap(bin_embed, 0, 1), swap(bin_embed, 0, 2), swap(bin_embed, 0, 3)
    quad = jnp.stack([bin_embed, core, xlo, both])
    z1, z2, z3 = (swap(quad, 0, 4 * step) for step in (1, 2, 3))
    pieces = (bin_embed, core, xlo, both, z1, z2, z3)

    cot = cotangent[0, 0]
    cot_cols = jnp.transpose(cot, (2, 0, 1))
    weight, bias = conv_weight.reshape(9 * C, C), conv_bias.reshape(1, C)
    send, keep, around, pair_out = gradients(meta, pieces, weight, bias, cot, cot_cols)

    def next_rows(which, pair_out, after):
        return fold(which, meta, around, weight, bias, pair_out, after)

    got = swap(send, 0, 1)
    half, part = shape((6, C, B), BF16), shape((5, C, B), BF16)
    keep, to1, to2, to3 = call(
        after_core_kernel, [SMEM, VMEM, VMEM], (half,) * 4, (VMEM,) * 4
    )(meta, keep, got)
    pair_out, token = next_rows(0, pair_out, keep)
    a, b, c = swap(to1, 0, 4), swap(to2, 0, 8), swap(to3, 0, 12)
    keep, other = call(
        after_z_kernel, [SMEM] + [VMEM] * 4 + [ANY], (part, part), (VMEM, VMEM)
    )(meta, keep, a, b, c, token)
    pair_out, token = next_rows(1, pair_out, keep)
    a, b, c = swap(other, 0, 2), swap(keep, 1, 0), swap(other, 1, 2)
    keep = call(after_x_kernel, [SMEM] + [VMEM] * 4 + [ANY], part, VMEM)(meta, keep, a, b, c, token)
    pair_out, token = next_rows(2, pair_out, keep)
    a, b, c = swap(keep, 2, 0), swap(keep, 4, 0), swap(keep, 6, 0)
    grad_embed, grad_weight, grad_bias = call(
        after_y_kernel,
        [SMEM] + [VMEM] * 4,
        (shape((C, B), F32), shape((9, C, C), F32), shape((1, C), F32)),
        (VMEM,) * 3,
    )(meta, keep, a, b, c)
    return pair_out[None, None], grad_embed, grad_weight, grad_bias.reshape(C)


def solution(mesh):
    placed = (P(None, "col"), P(), P(), P(), P(), P("fold", "col", None, None, None))
    return jax.shard_map(
        body,
        mesh=mesh,
        in_specs=placed,
        out_specs=(P("fold", "col", None, None, None), P(None, "col"), P(), P()),
        check_vma=False,
    )
```

time: 83.4 us -> 70.5 us (0.85)
  Pallas kernels: 31.9 us -> 22 us
  starting transfers between devices: 25.2 us -> 20.7 us
  waiting for transfers between devices: 13.9 us -> 16.1 us
    pallas_call x6 -> x8, Pallas kernels: 31.9 us -> 22 us  [the longest x1 16.4 us: gradients(): call(gradient_kernel, [SMEM] + [VMEM] * (len(pieces) + 3) + [ANY, ANY], (...]
    ppermute x15 -> x16, starting transfers between devices: 25.2 us -> 20.7 us  [swap(): return lax.ppermute(value, ('fold', 'col'), route)]
    transpose x1 -> x0, local copies, waits for them, and re-layouts: 2.43 us -> none  [body(): cot_rows = jnp.transpose(cot, (1, 0, 2))]
    unnamed x12 -> x29, local copies, waits for them, and re-layouts: 4.57 us -> 6.88 us
    ppermute x15 -> x16, waiting for transfers between devices: 13.9 us -> 16.1 us  [swap(): return lax.ppermute(value, ('fold', 'col'), route)]
    concatenate x1, local copies, waits for them, and re-layouts: 0.08 us -> 1.27 us  [body(): jnp.concatenate([pair, dilation, jnp.stack([col // 4, col // 2 % 2, col %...]
    reshape x1 -> x0, local copies, waits for them, and re-layouts: 0.98 us -> none  [body(): flat = jnp.transpose(conv_weight, (2, 0, 1)).reshape(C, 432)]
  transfers between devices with their start and end apart: 15 -> 16, of which waited for: 8 -> 11; matrix products, arithmetic and copies ran while one was open for 9% -> 6% of each run, Pallas kernels for 11% -> 4%
where the time goes in v2:
time: 70.5 us; the launch traced here: 69.7 us
  Pallas kernels  22 us (31%)
  starting transfers between devices  20.7 us (29%)
  waiting for transfers between devices  16.1 us (23%)
  local copies, waits for them, and re-layouts  8.85 us (13%)
  other arithmetic  1.34 us (2%)
  between operations  0.8 us (1%)
    ppermute x16, starting transfers between devices, swap(): return lax.ppermute(value, ('fold', 'col'), route)  20.7 us
    pallas_call x1, Pallas kernels, gradients(): call(gradient_kernel, [SMEM] + [VMEM] * (len(pieces) + 3) + [ANY, ANY], (...  16.4 us
    ppermute x16, waiting for transfers between devices, swap(): return lax.ppermute(value, ('fold', 'col'), route)  16.1 us
    unnamed x29, local copies, waits for them, and re-layouts  6.88 us
    pallas_call x3, Pallas kernels, fold(): call(functools.partial(fold_kernel, first, count), [SMEM, VMEM, VMEM, VME...  2.48 us
  transfers between devices with their start and end apart: 16, of which 11 were waited for; matrix products, arithmetic and copies ran while one was open for 6% of the time, Pallas kernels for 4%

profile of v2, /device:TPU:0, one launch (start us, length us, event | category | flops | bytes accessed | tf_op | source)
XLA Modules:
  0.0 69.7 jit_solution(14609599486858056946)
XLA Ops:
  0.6 0.0 copy-start
  0.6 1.1 %collective-permute-start.2 = (bf16[48,128]{1,0:T(8,128)(2,1)}, bf16[48,128]{1,0:T(8,128)(2,1)S(1)}, u32[]{:S(2)}, u32[]{:S(2)}) collective-permute-start(bf16[48,128]{1,0:T(8,128)(2,1)} %own.1), channel_id=1, source_target_pairs={{0,3},{1,2},{2,1},{3,0},{4,7},{5,6},{6,5},{7,4},{8,11},{9,10},{10,... | collective-permute-start | bytes 36872 | tf_op jit(solution)/shard_map/ppermute | solution.py:416
  1.7 0.7 collective-permute-start.1
  2.4 0.2 collective-permute-start
  2.6 1.5 %collective-permute-done.2.both = bf16[48,128]{1,0:T(8,128)(2,1)S(1)} collective-permute-done((bf16[48,128]{1,0:T(8,128)(2,1)}, bf16[48,128]{1,0:T(8,128)(2,1)S(1)}, u32[]{:S(2)}, u32[]{:S(2)}) %collective-permute-start.2) | collective-permute-done | bytes 12320 | tf_op jit(solution)/shard_map/ppermute | solution.py:416
  4.1 1.6 %collective-permute-done.1.xlo = bf16[48,128]{1,0:T(8,128)(2,1)S(1)} collective-permute-done((bf16[48,128]{1,0:T(8,128)(2,1)}, bf16[48,128]{1,0:T(8,128)(2,1)S(1)}, u32[]{:S(2)}, u32[]{:S(2)}) %collective-permute-start.1) | collective-permute-done | bytes 12320 | tf_op jit(solution)/shard_map/ppermute | solution.py:416
  5.7 1.3 %pad_maximum_fusion = bf16[4,48,128]{2,1,0:T(8,128)(2,1)} fusion(bf16[1,48,128]{2,1,0:T(8,128)(2,1)S(1)} %bitcast.22, bf16[1,48,128]{2,1,0:T(8,128)(2,1)S(1)} %bitcast.23, bf16[1,48,128]{2,1,0:T(8,128)(2,1)S(1)} %bitcast.24, bf16[1,48,128]{2,1,0:T(8,128)(2,1)} %bitcast.21), kind=kLoop, calls=%fused_computation | loop fusion | flops 73728 | bytes 98304 | tf_op jit(solution)/shard_map/stack | solution.py:419
  7.0 0.6 copy-done.5
  7.6 4.0 %collective-permute-start.5 = (bf16[4,48,128]{2,1,0:T(8,128)(2,1)}, bf16[4,48,128]{2,1,0:T(8,128)(2,1)}, u32[]{:S(2)}, u32[]{:S(2)}) collective-permute-start(bf16[4,48,128]{2,1,0:T(8,128)(2,1)} %pad_maximum_fusion), channel_id=1, source_target_pairs={{0,12},{1,13},{2,14},{3,15},{4,8},{5,9},{6,10},{7,11},{8,4},{9,5},... | collective-permute-start | bytes 147464 | tf_op jit(solution)/shard_map/ppermute | solution.py:416
  11.6 0.9 %collective-permute-start.3 = (bf16[4,48,128]{2,1,0:T(8,128)(2,1)}, bf16[4,48,128]{2,1,0:T(8,128)(2,1)}, u32[]{:S(2)}, u32[]{:S(2)}) collective-permute-start(bf16[4,48,128]{2,1,0:T(8,128)(2,1)} %pad_maximum_fusion), channel_id=1, source_target_pairs={{0,4},{1,5},{2,6},{3,7},{4,0},{5,1},{6,2},{7,3},{8,12},{9,13},{10,... | collective-permute-start | bytes 147464 | tf_op jit(solution)/shard_map/ppermute | solution.py:416
  12.5 2.2 %copy.14 = bf16[1,1,48,128,128]{3,2,4,1,0:T(8,128)(2,1)S(1)} copy(bf16[1,1,48,128,128]{4,3,2,1,0:T(8,128)(2,1)} %param.12) | data formatting | bytes 3145728 | tf_op args[5]
  14.7 0.7 %dynamic-slice_reduce_fusion = s32[2]{0:T(128)} fusion(s32[128,2]{0,1:T(2,128)S(1)} %copy-done, s32[]{:T(128)S(6)} %select_n.21), kind=kLoop, calls=%fused_computation.1 | loop fusion | bytes 20 | tf_op jit(solution)/shard_map/dynamic_slice | solution.py:409
  15.4 1.3 %concatenate.3.meta = s32[7]{0:T(128)} concatenate(s32[2]{0:T(128)} %dynamic-slice_reduce_fusion, s32[2]{0:T(128)} %param.10, s32[1]{0:T(128)} %bitcast, s32[1]{0:T(128)} %bitcast.1, s32[1]{0:T(128)} %bitcast.2), dimensions={0} | concatenate | bytes 56 | tf_op jit(solution)/shard_map/concatenate | solution.py:410
  16.7 0.9 %collective-permute-done.4.z2 = bf16[4,48,128]{2,1,0:T(8,128)(2,1)} collective-permute-done((bf16[4,48,128]{2,1,0:T(8,128)(2,1)}, bf16[4,48,128]{2,1,0:T(8,128)(2,1)}, u32[]{:S(2)}, u32[]{:S(2)}) %collective-permute-start.4) | collective-permute-done | bytes 49184 | tf_op jit(solution)/shard_map/ppermute | solution.py:416
  17.5 0.0 collective-permute-done.3.z1
  17.6 0.0 copy-start.4
  17.6 0.7 %copy-done.4 = bf16[48,128]{1,0:T(8,128)(2,1)S(1)} copy-done((bf16[48,128]{1,0:T(8,128)(2,1)S(1)}, bf16[48,128]{1,0:T(8,128)(2,1)}, u32[]{:S(2)}) %copy-start.4) | copy-done | bytes 12312
  18.3 0.7 %copy-done.6 = bf16[48,128]{1,0:T(8,128)(2,1)S(1)} copy-done((bf16[48,128]{1,0:T(8,128)(2,1)S(1)}, bf16[48,128]{1,0:T(8,128)(2,1)}, u32[]{:S(2)}) %copy-start.6) | copy-done | bytes 12312
  19.0 0.7 %copy-done.8 = bf16[48,128]{1,0:T(8,128)(2,1)S(1)} copy-done((bf16[48,128]{1,0:T(8,128)(2,1)S(1)}, bf16[48,128]{1,0:T(8,128)(2,1)}, u32[]{:S(2)}) %copy-start.8) | copy-done | bytes 12312
  19.7 0.7 %copy-done.10 = bf16[48,128]{1,0:T(8,128)(2,1)S(1)} copy-done((bf16[48,128]{1,0:T(8,128)(2,1)S(1)}, bf16[48,128]{1,0:T(8,128)(2,1)}, u32[]{:S(2)}) %copy-start.10) | copy-done | bytes 12312
  20.4 0.6 copy-done.11
  21.0 0.7 copy-done.12
  21.7 16.4 %shard_map.102 = (f32[12,48,128]{2,1,0:T(8,128)S(1)}, f32[12,48,128]{2,1,0:T(8,128)S(1)}, f32[6,48,128]{2,1,0:T(8,128)S(1)}, bf16[48,128,128]{2,1,0:T(8,128)(2,1)}) custom-call(s32[7]{0:T(128)S(1)} %copy-done.11, bf16[48,128]{1,0:T(8,128)(2,1)S(1)} %copy-done.4, bf16[48,128]{1,0:T(8,128)(2,1)S(1)} %copy-done.10, bf16[48,128]{1,0:T(8,128)(2,1)S(1)} %copy-done.8, ...), custom_call_target="tpu_custom_call" | custom-call | tf_op jit(solution)/shard_map/pallas_call | solution.py:327
  38.1 0.1 collective-permute-start.6
  38.2 1.6 %collective-permute-done.6.got = f32[12,48,128]{2,1,0:T(8,128)S(1)} collective-permute-done((f32[12,48,128]{2,1,0:T(8,128)S(1)}, f32[12,48,128]{2,1,0:T(8,128)S(1)}, u32[]{:S(2)}, u32[]{:S(2)}) %collective-permute-start.6) | collective-permute-done | bytes 294944 | tf_op jit(solution)/shard_map/ppermute | solution.py:416
  39.7 0.6 shard_map.103
  40.3 0.4 collective-permute-start.7
  40.7 3.5 %collective-permute-start.8 = (bf16[6,48,128]{2,1,0:T(8,128)(2,1)S(1)}, bf16[6,48,128]{2,1,0:T(8,128)(2,1)S(1)}, u32[]{:S(2)}, u32[]{:S(2)}) collective-permute-start(bf16[6,48,128]{2,1,0:T(8,128)(2,1)S(1)} %get-tuple-element.29), channel_id=1, source_target_pairs={{0,8},{1,9},{2,10},{3,11},{4,12},{5,13},{6,14},{7,15},{8,0},{9,1},... | collective-permute-start | bytes 221192 | tf_op jit(solution)/shard_map/ppermute | solution.py:416
  44.2 0.9 %collective-permute-start.9 = (bf16[6,48,128]{2,1,0:T(8,128)(2,1)S(1)}, bf16[6,48,128]{2,1,0:T(8,128)(2,1)S(1)}, u32[]{:S(2)}, u32[]{:S(2)}) collective-permute-start(bf16[6,48,128]{2,1,0:T(8,128)(2,1)S(1)} %get-tuple-element.30), channel_id=1, source_target_pairs={{0,12},{1,13},{2,14},{3,15},{4,8},{5,9},{6,10},{7,11},{8,4},{9,5},... | collective-permute-start | bytes 221192 | tf_op jit(solution)/shard_map/ppermute | solution.py:416
  45.1 0.6 shard_map.104
  45.7 2.5 %collective-permute-done.8.b = bf16[6,48,128]{2,1,0:T(8,128)(2,1)S(1)} collective-permute-done((bf16[6,48,128]{2,1,0:T(8,128)(2,1)S(1)}, bf16[6,48,128]{2,1,0:T(8,128)(2,1)S(1)}, u32[]{:S(2)}, u32[]{:S(2)}) %collective-permute-start.8) | collective-permute-done | bytes 73760 | tf_op jit(solution)/shard_map/ppermute | solution.py:416
  48.2 1.7 %collective-permute-done.9.c = bf16[6,48,128]{2,1,0:T(8,128)(2,1)S(1)} collective-permute-done((bf16[6,48,128]{2,1,0:T(8,128)(2,1)S(1)}, bf16[6,48,128]{2,1,0:T(8,128)(2,1)S(1)}, u32[]{:S(2)}, u32[]{:S(2)}) %collective-permute-start.9) | collective-permute-done | bytes 73760 | tf_op jit(solution)/shard_map/ppermute | solution.py:416
  49.8 0.6 shard_map.105
  50.4 2.2 %collective-permute-start.12 = (bf16[5,48,128]{2,1,0:T(8,128)(2,1)S(1)}, bf16[5,48,128]{2,1,0:T(8,128)(2,1)S(1)}, u32[]{:S(2)}, u32[]{:S(2)}) collective-permute-start(bf16[5,48,128]{2,1,0:T(8,128)(2,1)S(1)} %get-tuple-element.34), channel_id=1, source_target_pairs={{0,18},{1,19},{2,16},{3,17},{4,22},{5,23},{6,20},{7,21},{8,26},{9,... | collective-permute-start | bytes 184328 | tf_op jit(solution)/shard_map/ppermute | solution.py:416
  52.6 0.6 collective-permute-start.10
  53.2 2.0 %collective-permute-start.11 = (bf16[5,48,128]{2,1,0:T(8,128)(2,1)S(1)}, bf16[5,48,128]{2,1,0:T(8,128)(2,1)S(1)}, u32[]{:S(2)}, u32[]{:S(2)}) collective-permute-start(bf16[5,48,128]{2,1,0:T(8,128)(2,1)S(1)} %get-tuple-element.32.after.keep), channel_id=1, source_target_pairs={{0,16},{1,17},{2,18},{3,19},{4,20},{5,21},{6,22},{7,23},{8,24},{9,... | collective-permute-start | bytes 184328 | tf_op jit(solution)/shard_map/ppermute | solution.py:416
  55.2 0.8 %shard_map.106 = (bf16[48,128,128]{2,1,0:T(8,128)(2,1)}, f32[8,128]{1,0:T(8,128)S(1)}) custom-call(s32[7]{0:T(128)S(1)} %copy-done.11, f32[6,48,128]{2,1,0:T(8,128)S(1)} %get-tuple-element.22.around, bf16[432,48]{1,0:T(8,128)(2,1)S(1)} %bitcast.19, f32[1,48]{1,0:T(1,128)S(1)} %bitcast.27, ...), custom_call_target="tpu_custom_call", output_to_operand_aliasing={{0}: (4, {})} | custom-call | tf_op jit(solution)/shard_map/pallas_call | solution.py:353
  56.0 0.6 collective-permute-done.12.c
  56.6 0.2 collective-permute-done.10.a
  56.8 2.1 %collective-permute-done.11.b = bf16[5,48,128]{2,1,0:T(8,128)(2,1)S(1)} collective-permute-done((bf16[5,48,128]{2,1,0:T(8,128)(2,1)S(1)}, bf16[5,48,128]{2,1,0:T(8,128)(2,1)S(1)}, u32[]{:S(2)}, u32[]{:S(2)}) %collective-permute-start.11) | collective-permute-done | bytes 61472 | tf_op jit(solution)/shard_map/ppermute | solution.py:416
  58.9 0.6 shard_map.107.after.keep
  59.5 3.1 %collective-permute-start.15 = (bf16[5,48,128]{2,1,0:T(8,128)(2,1)S(1)}, bf16[5,48,128]{2,1,0:T(8,128)(2,1)S(1)}, u32[]{:S(2)}, u32[]{:S(2)}) collective-permute-start(bf16[5,48,128]{2,1,0:T(8,128)(2,1)S(1)} %shard_map.107.after.keep), channel_id=1, source_target_pairs={{0,96},{1,97},{2,98},{3,99},{4,100},{5,101},{6,102},{7,103},{8,104... | collective-permute-start | bytes 184328 | tf_op jit(solution)/shard_map/ppermute | solution.py:416
  62.6 0.6 collective-permute-start.14
  63.2 0.4 collective-permute-start.13
  63.7 1.1 %shard_map.108 = (bf16[48,128,128]{2,1,0:T(8,128)(2,1)}, f32[8,128]{1,0:T(8,128)}) custom-call(s32[7]{0:T(128)S(1)} %copy-done.11, f32[6,48,128]{2,1,0:T(8,128)S(1)} %get-tuple-element.22.around, bf16[432,48]{1,0:T(8,128)(2,1)S(1)} %bitcast.20, f32[1,48]{1,0:T(1,128)S(1)} %bitcast.28, ...), custom_call_target="tpu_custom_call", output_to_operand_aliasing={{0}: (4, {})} | custom-call | tf_op jit(solution)/shard_map/pallas_call | solution.py:353
  64.8 0.2 collective-permute-done.15.c
  65.0 3.3 %collective-permute-done.14.b = bf16[5,48,128]{2,1,0:T(8,128)(2,1)S(1)} collective-permute-done((bf16[5,48,128]{2,1,0:T(8,128)(2,1)S(1)}, bf16[5,48,128]{2,1,0:T(8,128)(2,1)S(1)}, u32[]{:S(2)}, u32[]{:S(2)}) %collective-permute-start.14) | collective-permute-done | bytes 61472 | tf_op jit(solution)/shard_map/ppermute | solution.py:416
  68.3 1.4 %shard_map.109 = (f32[48,128]{1,0:T(8,128)}, f32[9,48,48]{2,1,0:T(8,128)}, f32[1,48]{1,0:T(1,128)}) custom-call(s32[7]{0:T(128)S(1)} %copy-done.11, bf16[5,48,128]{2,1,0:T(8,128)(2,1)S(1)} %shard_map.107.after.keep, bf16[5,48,128]{2,1,0:T(8,128)(2,1)S(1)} %collective-permute-done.13.a, bf16[5,48,128]{2,1,0:T(8,128)(2,1)S(1)} %collective-permute-done.14.b, ...), custom_call_target="tpu_custom_call" | custom-call | tf_op jit(solution)/shard_map/pallas_call | solution.py:446
  (24 shorter events, 0.0 us)
Async XLA Ops:
  0.6 14.1 %copy-start = (s32[128,2]{0,1:T(2,128)S(1)}, s32[128,2]{0,1:T(2,128)}, u32[]{:S(2)}) copy-start(s32[128,2]{0,1:T(2,128)} %param.11) | copy-start | bytes 3076
  0.6 3.4 %collective-permute-start.2 = (bf16[48,128]{1,0:T(8,128)(2,1)}, bf16[48,128]{1,0:T(8,128)(2,1)S(1)}, u32[]{:S(2)}, u32[]{:S(2)}) collective-permute-start(bf16[48,128]{1,0:T(8,128)(2,1)} %own.1), channel_id=1, source_target_pairs={{0,3},{1,2},{2,1},{3,0},{4,7},{5,6},{6,5},{7,4},{8,11},{9,10},{10,... | collective-permute-start | bytes 36872 | tf_op jit(solution)/shard_map/ppermute | solution.py:416
  1.7 3.9 %collective-permute-start.1 = (bf16[48,128]{1,0:T(8,128)(2,1)}, bf16[48,128]{1,0:T(8,128)(2,1)S(1)}, u32[]{:S(2)}, u32[]{:S(2)}) collective-permute-start(bf16[48,128]{1,0:T(8,128)(2,1)} %own.1), channel_id=1, source_target_pairs={{0,2},{1,3},{2,0},{3,1},{4,6},{5,7},{6,4},{7,5},{8,10},{9,11},{10,... | collective-permute-start | bytes 36872 | tf_op jit(solution)/shard_map/ppermute | solution.py:416
  2.4 3.3 %collective-permute-start = (bf16[48,128]{1,0:T(8,128)(2,1)}, bf16[48,128]{1,0:T(8,128)(2,1)S(1)}, u32[]{:S(2)}, u32[]{:S(2)}) collective-permute-start(bf16[48,128]{1,0:T(8,128)(2,1)} %own.1), channel_id=1, source_target_pairs={{0,1},{1,0},{2,3},{3,2},{4,5},{5,4},{6,7},{7,6},{8,9},{9,8},{10,11... | collective-permute-start | bytes 36872 | tf_op jit(solution)/shard_map/ppermute | solution.py:416
  5.6 1.3 %copy-start.7 = (bf16[48,128]{1,0:T(8,128)(2,1)}, bf16[48,128]{1,0:T(8,128)(2,1)S(1)}, u32[]{:S(2)}) copy-start(bf16[48,128]{1,0:T(8,128)(2,1)S(1)} %collective-permute-done.1.xlo) | copy-start | bytes 36868
  5.7 6.0 %copy-start.9 = (bf16[48,128]{1,0:T(8,128)(2,1)}, bf16[48,128]{1,0:T(8,128)(2,1)S(1)}, u32[]{:S(2)}) copy-start(bf16[48,128]{1,0:T(8,128)(2,1)S(1)} %collective-permute-done.core) | copy-start | bytes 36868
  7.0 0.6 copy-start.5
  7.6 9.1 %collective-permute-start.5 = (bf16[4,48,128]{2,1,0:T(8,128)(2,1)}, bf16[4,48,128]{2,1,0:T(8,128)(2,1)}, u32[]{:S(2)}, u32[]{:S(2)}) collective-permute-start(bf16[4,48,128]{2,1,0:T(8,128)(2,1)} %pad_maximum_fusion), channel_id=1, source_target_pairs={{0,12},{1,13},{2,14},{3,15},{4,8},{5,9},{6,10},{7,11},{8,4},{9,5},... | collective-permute-start | bytes 147464 | tf_op jit(solution)/shard_map/ppermute | solution.py:416
  11.6 5.9 %collective-permute-start.4 = (bf16[4,48,128]{2,1,0:T(8,128)(2,1)}, bf16[4,48,128]{2,1,0:T(8,128)(2,1)}, u32[]{:S(2)}, u32[]{:S(2)}) collective-permute-start(bf16[4,48,128]{2,1,0:T(8,128)(2,1)} %pad_maximum_fusion), channel_id=1, source_target_pairs={{0,8},{1,9},{2,10},{3,11},{4,12},{5,13},{6,14},{7,15},{8,0},{9,1},... | collective-permute-start | bytes 147464 | tf_op jit(solution)/shard_map/ppermute | solution.py:416
  11.6 5.9 %collective-permute-start.3 = (bf16[4,48,128]{2,1,0:T(8,128)(2,1)}, bf16[4,48,128]{2,1,0:T(8,128)(2,1)}, u32[]{:S(2)}, u32[]{:S(2)}) collective-permute-start(bf16[4,48,128]{2,1,0:T(8,128)(2,1)} %pad_maximum_fusion), channel_id=1, source_target_pairs={{0,4},{1,5},{2,6},{3,7},{4,0},{5,1},{6,2},{7,3},{8,12},{9,13},{10,... | collective-permute-start | bytes 147464 | tf_op jit(solution)/shard_map/ppermute | solution.py:416
  12.5 5.1 %copy-start.1 = (bf16[1,1,48,128,128]{4,3,2,1,0:T(8,128)(2,1)S(1)}, bf16[1,1,48,128,128]{4,3,2,1,0:T(8,128)(2,1)}, u32[]{:S(2)}) copy-start(bf16[1,1,48,128,128]{4,3,2,1,0:T(8,128)(2,1)} %param.12) | copy-start | bytes 4718596
  12.5 5.1 %copy-start.2 = (bf16[9,48,48]{2,1,0:T(8,128)(2,1)S(1)}, bf16[9,48,48]{2,1,0:T(8,128)(2,1)}, u32[]{:S(2)}) copy-start(bf16[9,48,48]{2,1,0:T(8,128)(2,1)} %param.8) | copy-start | bytes 124420
  12.5 5.1 %copy-start.3 = (bf16[2,144,512]{2,1,0:T(8,128)(2,1)S(1)}, bf16[2,144,512]{2,1,0:T(8,128)(2,1)}, u32[]{:S(2)}) copy-start(bf16[2,144,512]{2,1,0:T(8,128)(2,1)} %constant.54.clone.repeat) | copy-start | bytes 884740
  17.6 0.7 %copy-start.4 = (bf16[48,128]{1,0:T(8,128)(2,1)S(1)}, bf16[48,128]{1,0:T(8,128)(2,1)}, u32[]{:S(2)}) copy-start(bf16[48,128]{1,0:T(8,128)(2,1)} %own.1) | copy-start | bytes 36868
  18.3 0.7 %copy-start.6 = (bf16[48,128]{1,0:T(8,128)(2,1)S(1)}, bf16[48,128]{1,0:T(8,128)(2,1)}, u32[]{:S(2)}) copy-start(bf16[48,128]{1,0:T(8,128)(2,1)} %copy-done.5) | copy-start | bytes 36868
  19.0 0.7 %copy-start.8 = (bf16[48,128]{1,0:T(8,128)(2,1)S(1)}, bf16[48,128]{1,0:T(8,128)(2,1)}, u32[]{:S(2)}) copy-start(bf16[48,128]{1,0:T(8,128)(2,1)} %copy-done.7) | copy-start | bytes 36868
  19.7 0.7 %copy-start.10 = (bf16[48,128]{1,0:T(8,128)(2,1)S(1)}, bf16[48,128]{1,0:T(8,128)(2,1)}, u32[]{:S(2)}) copy-start(bf16[48,128]{1,0:T(8,128)(2,1)} %copy-done.9) | copy-start | bytes 36868
  20.4 0.6 copy-start.11
  21.0 0.7 copy-start.12
  21.7 23.4 %copy-start.13 = (f32[48]{0:T(128)S(1)}, f32[48]{0:T(128)}, u32[]{:S(2)}) copy-start(f32[48]{0:T(128)} %param.9) | copy-start | bytes 580
  38.1 1.7 %collective-permute-start.6 = (f32[12,48,128]{2,1,0:T(8,128)S(1)}, f32[12,48,128]{2,1,0:T(8,128)S(1)}, u32[]{:S(2)}, u32[]{:S(2)}) collective-permute-start(f32[12,48,128]{2,1,0:T(8,128)S(1)} %get-tuple-element.25), channel_id=1, source_target_pairs={{0,1},{1,0},{2,3},{3,2},{4,5},{5,4},{6,7},{7,6},{8,9},{9,8},{10,11... | collective-permute-start | bytes 884744 | tf_op jit(solution)/shard_map/ppermute | solution.py:416
  40.3 5.3 %collective-permute-start.7 = (bf16[6,48,128]{2,1,0:T(8,128)(2,1)S(1)}, bf16[6,48,128]{2,1,0:T(8,128)(2,1)S(1)}, u32[]{:S(2)}, u32[]{:S(2)}) collective-permute-start(bf16[6,48,128]{2,1,0:T(8,128)(2,1)S(1)} %get-tuple-element.28), channel_id=1, source_target_pairs={{0,4},{1,5},{2,6},{3,7},{4,0},{5,1},{6,2},{7,3},{8,12},{9,13},{10,... | collective-permute-start | bytes 221192 | tf_op jit(solution)/shard_map/ppermute | solution.py:416
  40.7 7.4 %collective-permute-start.8 = (bf16[6,48,128]{2,1,0:T(8,128)(2,1)S(1)}, bf16[6,48,128]{2,1,0:T(8,128)(2,1)S(1)}, u32[]{:S(2)}, u32[]{:S(2)}) collective-permute-start(bf16[6,48,128]{2,1,0:T(8,128)(2,1)S(1)} %get-tuple-element.29), channel_id=1, source_target_pairs={{0,8},{1,9},{2,10},{3,11},{4,12},{5,13},{6,14},{7,15},{8,0},{9,1},... | collective-permute-start | bytes 221192 | tf_op jit(solution)/shard_map/ppermute | solution.py:416
  44.2 5.6 %collective-permute-start.9 = (bf16[6,48,128]{2,1,0:T(8,128)(2,1)S(1)}, bf16[6,48,128]{2,1,0:T(8,128)(2,1)S(1)}, u32[]{:S(2)}, u32[]{:S(2)}) collective-permute-start(bf16[6,48,128]{2,1,0:T(8,128)(2,1)S(1)} %get-tuple-element.30), channel_id=1, source_target_pairs={{0,12},{1,13},{2,14},{3,15},{4,8},{5,9},{6,10},{7,11},{8,4},{9,5},... | collective-permute-start | bytes 221192 | tf_op jit(solution)/shard_map/ppermute | solution.py:416
  50.4 6.2 %collective-permute-start.12 = (bf16[5,48,128]{2,1,0:T(8,128)(2,1)S(1)}, bf16[5,48,128]{2,1,0:T(8,128)(2,1)S(1)}, u32[]{:S(2)}, u32[]{:S(2)}) collective-permute-start(bf16[5,48,128]{2,1,0:T(8,128)(2,1)S(1)} %get-tuple-element.34), channel_id=1, source_target_pairs={{0,18},{1,19},{2,16},{3,17},{4,22},{5,23},{6,20},{7,21},{8,26},{9,... | collective-permute-start | bytes 184328 | tf_op jit(solution)/shard_map/ppermute | solution.py:416
  52.6 4.2 %collective-permute-start.10 = (bf16[5,48,128]{2,1,0:T(8,128)(2,1)S(1)}, bf16[5,48,128]{2,1,0:T(8,128)(2,1)S(1)}, u32[]{:S(2)}, u32[]{:S(2)}) collective-permute-start(bf16[5,48,128]{2,1,0:T(8,128)(2,1)S(1)} %get-tuple-element.34), channel_id=1, source_target_pairs={{0,2},{1,3},{2,0},{3,1},{4,6},{5,7},{6,4},{7,5},{8,10},{9,11},{10,... | collective-permute-start | bytes 184328 | tf_op jit(solution)/shard_map/ppermute | solution.py:416
  53.2 5.7 %collective-permute-start.11 = (bf16[5,48,128]{2,1,0:T(8,128)(2,1)S(1)}, bf16[5,48,128]{2,1,0:T(8,128)(2,1)S(1)}, u32[]{:S(2)}, u32[]{:S(2)}) collective-permute-start(bf16[5,48,128]{2,1,0:T(8,128)(2,1)S(1)} %get-tuple-element.32.after.keep), channel_id=1, source_target_pairs={{0,16},{1,17},{2,18},{3,19},{4,20},{5,21},{6,22},{7,23},{8,24},{9,... | collective-permute-start | bytes 184328 | tf_op jit(solution)/shard_map/ppermute | solution.py:416
  59.5 5.5 %collective-permute-start.15 = (bf16[5,48,128]{2,1,0:T(8,128)(2,1)S(1)}, bf16[5,48,128]{2,1,0:T(8,128)(2,1)S(1)}, u32[]{:S(2)}, u32[]{:S(2)}) collective-permute-start(bf16[5,48,128]{2,1,0:T(8,128)(2,1)S(1)} %shard_map.107.after.keep), channel_id=1, source_target_pairs={{0,96},{1,97},{2,98},{3,99},{4,100},{5,101},{6,102},{7,103},{8,104... | collective-permute-start | bytes 184328 | tf_op jit(solution)/shard_map/ppermute | solution.py:416
  62.6 5.7 %collective-permute-start.14 = (bf16[5,48,128]{2,1,0:T(8,128)(2,1)S(1)}, bf16[5,48,128]{2,1,0:T(8,128)(2,1)S(1)}, u32[]{:S(2)}, u32[]{:S(2)}) collective-permute-start(bf16[5,48,128]{2,1,0:T(8,128)(2,1)S(1)} %shard_map.107.after.keep), channel_id=1, source_target_pairs={{0,64},{1,65},{2,66},{3,67},{4,68},{5,69},{6,70},{7,71},{8,72},{9,... | collective-permute-start | bytes 184328 | tf_op jit(solution)/shard_map/ppermute | solution.py:416
  63.2 5.1 %collective-permute-start.13 = (bf16[5,48,128]{2,1,0:T(8,128)(2,1)S(1)}, bf16[5,48,128]{2,1,0:T(8,128)(2,1)S(1)}, u32[]{:S(2)}, u32[]{:S(2)}) collective-permute-start(bf16[5,48,128]{2,1,0:T(8,128)(2,1)S(1)} %shard_map.107.after.keep), channel_id=1, source_target_pairs={{0,32},{1,33},{2,34},{3,35},{4,36},{5,37},{6,38},{7,39},{8,40},{9,... | collective-permute-start | bytes 184328 | tf_op jit(solution)/shard_map/ppermute | solution.py:416

commit v3 on v2

--- a/solution.py
+++ b/solution.py
@@ -42,21 +42,34 @@
     return jnp.asarray(table, BF16)
 
 
-def fill_blocks(meta, own, core, xlo, both, z1, z2, z3, blocks):
-    z, x, c = meta[4], meta[5], meta[6]
+def position():
+    return lax.axis_index("fold"), lax.axis_index("col")
+
+
+def tile_of(fold_map, dilation):
+    fold, col = position()
+    slot = fold * 16 + col
+    return fold_map[0, slot], fold_map[1, slot], dilation[0], dilation[1]
+
+
+def place_of():
+    col = position()[1]
+    return col // 4, (col // 2) % 2, col % 2
+
+
+def quad_kernel(own, core, xlo, both, out):
+    for k, block in enumerate((own, core, xlo, both)):
+        out[k] = block[...]
+
+
+def fill_blocks(quad, z1, z2, z3, blocks):
+    z, x, c = place_of()
     blocks[0] = jnp.full((C, B), OUTSIDE, F32)
     blocks[17] = jnp.full((C, B), OUTSIDE, F32)
-    here = 1 + z * 4
-    blocks[here + x * 2 + c] = own[...].astype(F32)
-    blocks[here + x * 2 + (1 - c)] = core[...].astype(F32)
-    blocks[here + (1 - x) * 2 + c] = xlo[...].astype(F32)
-    blocks[here + (1 - x) * 2 + (1 - c)] = both[...].astype(F32)
-    for step, got in ((1, z1), (2, z2), (3, z3)):
+    for step, got in ((0, quad), (1, z1), (2, z2), (3, z3)):
         there = 1 + (z ^ step) * 4
-        blocks[there + x * 2 + c] = got[0].astype(F32)
-        blocks[there + x * 2 + (1 - c)] = got[1].astype(F32)
-        blocks[there + (1 - x) * 2 + c] = got[2].astype(F32)
-        blocks[there + (1 - x) * 2 + (1 - c)] = got[3].astype(F32)
+        for k in range(4):
+            blocks[there + (x ^ (k // 2)) * 2 + (c ^ (k % 2))] = got[k].astype(F32)
 
 
 def spread_lanes(blocks, tile, table, first, count):
@@ -102,16 +115,20 @@
 
 
 def gradient_kernel(
-    meta, own, core, xlo, both, z1, z2, z3, conv_weight, conv_bias, repeat, cot_hbm, cols_hbm,
+    fold_map, dilation, quad, z1, z2, z3, conv_weight, repeat, bias_hbm, cot_hbm, cols_hbm,
     send, keep, around, pair_hbm,
-    blocks, shift, minus, sums, grads, wgrad, table, cot, rows, cols, cot32, stage32, stage, sems,
+    blocks, shift, minus, sums, grads, wgrad, table, cot, rows, cols, cot32, stage32, stage, bias_row, sems,
 ):
-    tile_i, tile_j, rate_r, rate_c, core_index = meta[0], meta[1], meta[2], meta[3], meta[6]
+    tile_i, tile_j, rate_r, rate_c = tile_of(fold_map, dilation)
+    core_index = place_of()[2]
+    load_bias = pltpu.make_async_copy(bias_hbm, bias_row, sems.at[3])
+    load_bias.start()
     load_cot = pltpu.make_async_copy(cot_hbm, cot, sems.at[0])
     load_cols = pltpu.make_async_copy(cols_hbm, cols, sems.at[1])
     load_cot.start()
     load_cols.start()
-    fill_blocks(meta, own, core, xlo, both, z1, z2, z3, blocks)
+    fill_blocks(quad, z1, z2, z3, blocks)
+    load_bias.wait()
     for k in range(3):
         around[k] = blocks[tile_i + k]
         around[3 + k] = blocks[tile_j + k]
@@ -176,7 +193,7 @@
     @pl.when(tile_i < tile_j)
     def one_tile():
         spread_lanes(blocks, tile_i, table, 0, B)
-        bias, short = bias_lanes(conv_bias), weight.astype(BF16)
+        bias, short = bias_lanes(bias_row), weight.astype(BF16)
         window = windows(blocks, tile_j, rate_c)
 
         def some(step, carry):
@@ -264,26 +281,30 @@
 
 
 def fold_kernel(
-    first, count, meta, around, conv_weight, conv_bias, pair_before, after, pair_hbm, token,
-    table_i, table_j, stage32, stage, sem,
+    first, count, fold_map, dilation, around, conv_weight, bias_hbm, pair_before, after,
+    pair_hbm, token,
+    table_i, table_j, stage32, stage, bias_row, sems,
 ):
-    tile_i, tile_j, rate_r, rate_c = meta[0], meta[1], meta[2], meta[3]
+    tile_i, tile_j, rate_r, rate_c = tile_of(fold_map, dilation)
     token[...] = jnp.zeros_like(token)
 
     @pl.when(tile_i > tile_j)
     def two_triangles():
+        load_bias = pltpu.make_async_copy(bias_hbm, bias_row, sems.at[0])
+        load_bias.start()
         spread_lanes(around, 0, table_i, first, count)
         spread_lanes(around, 3, table_j, first, count)
         up_window, low_window = windows(around, 0, rate_c), windows(around, 3, rate_r)
-        lane = lax.broadcasted_iota(jnp.int32, (C, B), 1)
-        bias, short = bias_lanes(conv_bias), conv_weight[...].astype(F32).T.astype(BF16)
-        zero = jnp.zeros((), BF16)
-
-        def some(step, carry):
+        lane = lax.broadcasted_iota(jnp.int32, (C, B), 1).astype(BF16)
+        short = conv_weight[...].astype(F32).T.astype(BF16)
+        load_bias.wait()
+        bias, zero = bias_lanes(bias_row), jnp.zeros((), BF16)
+        saves = []
+        for chunk in range(count // 16):
             parts = []
             for k in range(16):
-                q = step * 16 + k
-                upper = lane >= first + q
+                q = chunk * 16 + k
+                upper = lane >= jnp.full((C, B), first + q, BF16)
                 up = [table_i[DMAX + q + m * rate_r] for m in (-1, 0, 1)]
                 low = [table_j[DMAX + q + m * rate_c] for m in (-1, 0, 1)]
                 taps = [
@@ -292,14 +313,14 @@
                     for v in range(3)
                 ]
                 parts.append(jnp.concatenate([jnp.maximum(x, zero) for x in taps], 0))
-            store_rows(dot(short, jnp.concatenate(parts, 1), NN), bias, step * 16, stage32, count)
-            return carry
-
-        lax.fori_loop(0, count // 16, some, 0)
-        round_rows(stage32, stage, count)
-        save = pltpu.make_async_copy(stage, pair_hbm.at[:, pl.ds(first, count), :], sem)
-        save.start()
-        save.wait()
+            full = dot(short, jnp.concatenate(parts, 1), NN)
+            store_rows(full, bias, 0, stage32.at[chunk], 16)
+            round_rows(stage32.at[chunk], stage.at[chunk], 16)
+            here = pair_hbm.at[:, pl.ds(first + chunk * 16, 16), :]
+            saves.append(pltpu.make_async_copy(stage.at[chunk], here, sems.at[1 + chunk]))
+            saves[-1].start()
+        for save in saves:
+            save.wait()
 
 
 def shape(dims, kind):
@@ -309,6 +330,7 @@
 SMEM = pl.BlockSpec(memory_space=pltpu.SMEM)
 VMEM = pl.BlockSpec(memory_space=pltpu.VMEM)
 ANY = pl.BlockSpec(memory_space=pl.ANY)
+HBM = pl.BlockSpec(memory_space=pltpu.HBM)
 
 
 def call(kernel, in_specs, out_shape, out_specs, scratch=(), aliases={}):
@@ -323,12 +345,12 @@
     )
 
 
-def gradients(meta, pieces, conv_weight, conv_bias, cot, cot_cols):
+def gradients(fold_map, dilation, pieces, conv_weight, conv_bias, cot, cot_cols):
     return call(
         gradient_kernel,
-        [SMEM] + [VMEM] * (len(pieces) + 3) + [ANY, ANY],
+        [SMEM, SMEM] + [VMEM] * 6 + [HBM] * 3,
         (shape((12, C, B), F32), shape((12, C, B), F32), shape((6, C, B), F32), shape((C, B, B), BF16)),
-        (VMEM, VMEM, VMEM, ANY),
+        (VMEM, VMEM, VMEM, HBM),
         [
             pltpu.VMEM((18, C, B), F32),
             pltpu.VMEM((4, B, NK), F32),
@@ -343,31 +365,33 @@
             pltpu.VMEM((C * (B + PAD), B), F32),
             pltpu.VMEM((C * (B + PAD), B), F32),
             pltpu.VMEM((C, B, B), BF16),
-            pltpu.SemaphoreType.DMA((3,)),
+            pltpu.VMEM((1, C), F32),
+            pltpu.SemaphoreType.DMA((4,)),
         ],
-    )(meta, *pieces, conv_weight, conv_bias, repeat_table(), cot, cot_cols)
-
-
-def fold(which, meta, around, conv_weight, conv_bias, pair, after):
+    )(fold_map, dilation, *pieces, conv_weight, repeat_table(), conv_bias, cot, cot_cols)
+
+
+def fold(which, fold_map, dilation, around, conv_weight, conv_bias, pair, after):
     first, count = PIECES[which]
     return call(
         functools.partial(fold_kernel, first, count),
-        [SMEM, VMEM, VMEM, VMEM, ANY, ANY],
+        [SMEM, SMEM, VMEM, VMEM, HBM, HBM, ANY],
         (shape((C, B, B), BF16), shape((8, B), F32)),
-        (ANY, VMEM),
+        (HBM, VMEM),
         [
             pltpu.VMEM((count + 2 * DMAX, C, B), BF16),
             pltpu.VMEM((count + 2 * DMAX, C, B), BF16),
-            pltpu.VMEM((C * (count + PAD), B), F32),
-            pltpu.VMEM((C, count, B), BF16),
-            pltpu.SemaphoreType.DMA,
+            pltpu.VMEM((count // 16, C * (16 + PAD), B), F32),
+            pltpu.VMEM((count // 16, C, 16, B), BF16),
+            pltpu.VMEM((1, C), F32),
+            pltpu.SemaphoreType.DMA((1 + count // 16,)),
         ],
-        {4: 0},
-    )(meta, around, conv_weight, conv_bias, pair, after)
-
-
-def after_core_kernel(meta, keep, got, own, to1, to2, to3):
-    z = meta[4]
+        {5: 0},
+    )(fold_map, dilation, around, conv_weight, conv_bias, pair, after)
+
+
+def after_core_kernel(keep, got, own, to1, to2, to3):
+    z = place_of()[0]
     total = [(keep[k] + got[k]).astype(BF16) for k in range(8, 12)]
     for step, out in ((0, own), (1, to1), (2, to2), (3, to3)):
         first = (z ^ step) * 2
@@ -381,8 +405,8 @@
     return (own[k].astype(F32) + a[k].astype(F32)) + (b[k].astype(F32) + c[k].astype(F32))
 
 
-def after_z_kernel(meta, keep, a, b, c, token, own, other):
-    x = meta[5]
+def after_z_kernel(keep, a, b, c, token, own, other):
+    x = place_of()[1]
     own[0] = sum4(keep, a, b, c, x).astype(BF16)
     other[0] = sum4(keep, a, b, c, 1 - x).astype(BF16)
     for k in range(4):
@@ -391,12 +415,12 @@
         other[1 + k] = total
 
 
-def after_x_kernel(meta, keep, a, b, c, token, own):
+def after_x_kernel(keep, a, b, c, token, own):
     for k in range(5):
         own[k] = sum4(keep, a, b, c, k).astype(BF16)
 
 
-def after_y_kernel(meta, keep, a, b, c, grad_embed, grad_weight, grad_bias):
+def after_y_kernel(keep, a, b, c, grad_embed, grad_weight, grad_bias):
     grad_embed[...] = sum4(keep, a, b, c, 0) * (2048.0**-0.5)
     total = jnp.concatenate([sum4(keep, a, b, c, 1 + k) for k in range(4)], 1) * (1.0 / 2048.0)
     turned = total.T
@@ -405,9 +429,7 @@
 
 
 def body(bin_embed, conv_weight, conv_bias, dilation, fold_map, cotangent):
-    fold_at, col = lax.axis_index("fold"), lax.axis_index("col")
-    pair = lax.dynamic_slice_in_dim(fold_map, fold_at * 16 + col, 1, 0)[0]
-    meta = jnp.concatenate([pair, dilation, jnp.stack([col // 4, (col // 2) % 2, col % 2])])
+    fold_map = fold_map.T
 
     def swap(value, fold_bits, col_bits):
         route = [
@@ -416,39 +438,41 @@
         return lax.ppermute(value, ("fold", "col"), route)
 
     core, xlo, both = swap(bin_embed, 0, 1), swap(bin_embed, 0, 2), swap(bin_embed, 0, 3)
-    quad = jnp.stack([bin_embed, core, xlo, both])
+    quad = call(quad_kernel, [VMEM] * 4, shape((4, C, B), BF16), VMEM)(bin_embed, core, xlo, both)
     z1, z2, z3 = (swap(quad, 0, 4 * step) for step in (1, 2, 3))
-    pieces = (bin_embed, core, xlo, both, z1, z2, z3)
+    pieces = (quad, z1, z2, z3)
 
     cot = cotangent[0, 0]
     cot_cols = jnp.transpose(cot, (2, 0, 1))
     weight, bias = conv_weight.reshape(9 * C, C), conv_bias.reshape(1, C)
-    send, keep, around, pair_out = gradients(meta, pieces, weight, bias, cot, cot_cols)
+    send, keep, around, pair_out = gradients(
+        fold_map, dilation, pieces, weight, bias, cot, cot_cols
+    )
 
     def next_rows(which, pair_out, after):
-        return fold(which, meta, around, weight, bias, pair_out, after)
+        return fold(which, fold_map, dilation, around, weight, bias, pair_out, after)
 
     got = swap(send, 0, 1)
     half, part = shape((6, C, B), BF16), shape((5, C, B), BF16)
     keep, to1, to2, to3 = call(
-        after_core_kernel, [SMEM, VMEM, VMEM], (half,) * 4, (VMEM,) * 4
-    )(meta, keep, got)
+        after_core_kernel, [VMEM, VMEM], (half,) * 4, (VMEM,) * 4
+    )(keep, got)
     pair_out, token = next_rows(0, pair_out, keep)
     a, b, c = swap(to1, 0, 4), swap(to2, 0, 8), swap(to3, 0, 12)
     keep, other = call(
-        after_z_kernel, [SMEM] + [VMEM] * 4 + [ANY], (part, part), (VMEM, VMEM)
-    )(meta, keep, a, b, c, token)
+        after_z_kernel, [VMEM] * 4 + [ANY], (part, part), (VMEM, VMEM)
+    )(keep, a, b, c, token)
     pair_out, token = next_rows(1, pair_out, keep)
     a, b, c = swap(other, 0, 2), swap(keep, 1, 0), swap(other, 1, 2)
-    keep = call(after_x_kernel, [SMEM] + [VMEM] * 4 + [ANY], part, VMEM)(meta, keep, a, b, c, token)
+    keep = call(after_x_kernel, [VMEM] * 4 + [ANY], part, VMEM)(keep, a, b, c, token)
     pair_out, token = next_rows(2, pair_out, keep)
     a, b, c = swap(keep, 2, 0), swap(keep, 4, 0), swap(keep, 6, 0)
     grad_embed, grad_weight, grad_bias = call(
         after_y_kernel,
-        [SMEM] + [VMEM] * 4,
+        [VMEM] * 4,
         (shape((C, B), F32), shape((9, C, C), F32), shape((1, C), F32)),
         (VMEM,) * 3,
-    )(meta, keep, a, b, c)
+    )(keep, a, b, c)
     return pair_out[None, None], grad_embed, grad_weight, grad_bias.reshape(C)
 
 

time: 70.5 us -> 64.6 us (0.916)
  local copies, waits for them, and re-layouts: 8.85 us -> 4.06 us
  Pallas kernels: 22 us -> 20.4 us
  other arithmetic: 1.34 us -> 0 us
  starting transfers between devices: 20.7 us -> 21.6 us
  waiting for transfers between devices: 16.1 us -> 17 us
    unnamed x29 -> x19, local copies, waits for them, and re-layouts: 6.88 us -> 4.06 us
    pallas_call x8 -> x9, Pallas kernels: 22 us -> 20.4 us  [the longest x1 16.2 us: gradients(): call(gradient_kernel, [SMEM, SMEM] + [VMEM] * 6 + [HBM] * 3, (shape((12,...]
    another operation x1 -> x0, other arithmetic: 1.34 us -> none  [body(): quad = jnp.stack([bin_embed, core, xlo, both])]
    concatenate x1 -> x0, local copies, waits for them, and re-layouts: 1.27 us -> none  [body(): jnp.concatenate([pair, dilation, jnp.stack([col // 4, col // 2 % 2, col %...]
    ppermute x16, waiting for transfers between devices: 16.1 us -> 17 us  [swap(): return lax.ppermute(value, ('fold', 'col'), route)]
    ppermute x16, starting transfers between devices: 20.7 us -> 21.6 us  [swap(): return lax.ppermute(value, ('fold', 'col'), route)]
  transfers between devices with their start and end apart: 16 -> 16, of which waited for: 11 -> 12; matrix products, arithmetic and copies ran while one was open for 6% -> 3% of each run, Pallas kernels for 4% -> 4%
where the time goes in v3:
time: 64.6 us; the launch traced here: 63.8 us
  starting transfers between devices  21.6 us (33%)
  Pallas kernels  20.4 us (32%)
  waiting for transfers between devices  17 us (26%)
  local copies, waits for them, and re-layouts  4.06 us (6%)
  between operations  0.76 us (1%)
    ppermute x16, starting transfers between devices, swap(): return lax.ppermute(value, ('fold', 'col'), route)  21.6 us
    ppermute x16, waiting for transfers between devices, swap(): return lax.ppermute(value, ('fold', 'col'), route)  17 us
    pallas_call x1, Pallas kernels, gradients(): call(gradient_kernel, [SMEM, SMEM] + [VMEM] * 6 + [HBM] * 3, (shape((12,...  16.2 us
    unnamed x19, local copies, waits for them, and re-layouts  4.06 us
    pallas_call x3, Pallas kernels, fold(): call(functools.partial(fold_kernel, first, count), [SMEM, SMEM, VMEM, VME...  2.63 us
  transfers between devices with their start and end apart: 16, of which 12 were waited for; matrix products, arithmetic and copies ran while one was open for 3% of the time, Pallas kernels for 4%

profile of v3, /device:TPU:0, one launch (start us, length us, event | category | flops | bytes accessed | tf_op | source)
XLA Modules:
  0.0 63.8 jit_solution(15408779410235467475)
XLA Ops:
  0.6 1.7 %collective-permute-start.1 = (bf16[48,128]{1,0:T(8,128)(2,1)}, bf16[48,128]{1,0:T(8,128)(2,1)S(1)}, u32[]{:S(2)}, u32[]{:S(2)}) collective-permute-start(bf16[48,128]{1,0:T(8,128)(2,1)} %own.1), channel_id=1, source_target_pairs={{0,2},{1,3},{2,0},{3,1},{4,6},{5,7},{6,4},{7,5},{8,10},{9,11},{10,... | collective-permute-start | bytes 36872 | tf_op jit(solution)/shard_map/ppermute | solution.py:438
  2.3 0.0 collective-permute-start
  2.3 0.6 collective-permute-start.2
  2.9 1.8 %collective-permute-done.1.xlo = bf16[48,128]{1,0:T(8,128)(2,1)S(1)} collective-permute-done((bf16[48,128]{1,0:T(8,128)(2,1)}, bf16[48,128]{1,0:T(8,128)(2,1)S(1)}, u32[]{:S(2)}, u32[]{:S(2)}) %collective-permute-start.1) | collective-permute-done | bytes 12320 | tf_op jit(solution)/shard_map/ppermute | solution.py:438
  4.6 0.0 collective-permute-done.core
  4.6 1.0 %collective-permute-done.2.both = bf16[48,128]{1,0:T(8,128)(2,1)S(1)} collective-permute-done((bf16[48,128]{1,0:T(8,128)(2,1)}, bf16[48,128]{1,0:T(8,128)(2,1)S(1)}, u32[]{:S(2)}, u32[]{:S(2)}) %collective-permute-start.2) | collective-permute-done | bytes 12320 | tf_op jit(solution)/shard_map/ppermute | solution.py:438
  5.6 0.7 %copy-done.4 = bf16[48,128]{1,0:T(8,128)(2,1)S(1)} copy-done((bf16[48,128]{1,0:T(8,128)(2,1)S(1)}, bf16[48,128]{1,0:T(8,128)(2,1)}, u32[]{:S(2)}) %copy-start.4) | copy-done | bytes 12312
  6.3 0.6 shard_map.102.quad
  7.0 4.1 %collective-permute-start.5 = (bf16[4,48,128]{2,1,0:T(8,128)(2,1)}, bf16[4,48,128]{2,1,0:T(8,128)(2,1)}, u32[]{:S(2)}, u32[]{:S(2)}) collective-permute-start(bf16[4,48,128]{2,1,0:T(8,128)(2,1)} %shard_map.102.quad), channel_id=1, source_target_pairs={{0,12},{1,13},{2,14},{3,15},{4,8},{5,9},{6,10},{7,11},{8,4},{9,5},... | collective-permute-start | bytes 147464 | tf_op jit(solution)/shard_map/ppermute | solution.py:438
  11.1 0.0 collective-permute-start.4
  11.1 0.9 %collective-permute-start.3 = (bf16[4,48,128]{2,1,0:T(8,128)(2,1)}, bf16[4,48,128]{2,1,0:T(8,128)(2,1)}, u32[]{:S(2)}, u32[]{:S(2)}) collective-permute-start(bf16[4,48,128]{2,1,0:T(8,128)(2,1)} %shard_map.102.quad), channel_id=1, source_target_pairs={{0,4},{1,5},{2,6},{3,7},{4,0},{5,1},{6,2},{7,3},{8,12},{9,13},{10,... | collective-permute-start | bytes 147464 | tf_op jit(solution)/shard_map/ppermute | solution.py:438
  12.0 2.0 %copy.14 = bf16[1,1,48,128,128]{3,2,4,1,0:T(8,128)(2,1)S(1)} copy(bf16[1,1,48,128,128]{4,3,2,1,0:T(8,128)(2,1)} %param.12) | data formatting | bytes 3145728 | tf_op args[5]
  14.1 0.1 collective-permute-done.5.z3
  14.2 3.1 %collective-permute-done.4.z2 = bf16[4,48,128]{2,1,0:T(8,128)(2,1)} collective-permute-done((bf16[4,48,128]{2,1,0:T(8,128)(2,1)}, bf16[4,48,128]{2,1,0:T(8,128)(2,1)}, u32[]{:S(2)}, u32[]{:S(2)}) %collective-permute-start.4) | collective-permute-done | bytes 49184 | tf_op jit(solution)/shard_map/ppermute | solution.py:438
  17.3 0.0 collective-permute-done.3.z1
  17.3 0.0 copy-done
  17.3 0.0 copy-done.1
  17.3 0.0 copy-done.2
  17.3 0.0 copy-done.3
  17.3 0.0 copy-start.5
  17.3 0.6 %copy-done.5 = s32[2]{0:T(128)S(1)} copy-done((s32[2]{0:T(128)S(1)}, s32[2]{0:T(128)}, u32[]{:S(2)}) %copy-start.5) | copy-done | bytes 32
  18.0 0.7 %copy-done.7 = f32[48]{0:T(128)S(1)} copy-done((f32[48]{0:T(128)S(1)}, f32[48]{0:T(128)}, u32[]{:S(2)}) %copy-start.7) | copy-done | bytes 216
  18.6 16.2 %shard_map.103 = (f32[12,48,128]{2,1,0:T(8,128)S(1)}, f32[12,48,128]{2,1,0:T(8,128)S(1)}, f32[6,48,128]{2,1,0:T(8,128)S(1)}, bf16[48,128,128]{2,1,0:T(8,128)(2,1)}) custom-call(s32[2,128]{1,0:T(2,128)S(1)} %bitcast.15, s32[2]{0:T(128)S(1)} %copy-done.5, bf16[4,48,128]{2,1,0:T(8,128)(2,1)} %shard_map.102.quad, bf16[4,48,128]{2,1,0:T(8,128)(2,1)} %collective-permute-done.3.z1, ...), custom_call_target="tpu_custom_call" | custom-call | tf_op jit(solution)/shard_map/pallas_call | solution.py:349
  34.9 0.1 collective-permute-start.6
  35.0 1.6 %collective-permute-done.6.got = f32[12,48,128]{2,1,0:T(8,128)S(1)} collective-permute-done((f32[12,48,128]{2,1,0:T(8,128)S(1)}, f32[12,48,128]{2,1,0:T(8,128)S(1)}, u32[]{:S(2)}, u32[]{:S(2)}) %collective-permute-start.6) | collective-permute-done | bytes 294944 | tf_op jit(solution)/shard_map/ppermute | solution.py:438
  36.6 0.1 collective-permute-start.7
  36.7 2.5 %collective-permute-start.8 = (bf16[6,48,128]{2,1,0:T(8,128)(2,1)S(1)}, bf16[6,48,128]{2,1,0:T(8,128)(2,1)S(1)}, u32[]{:S(2)}, u32[]{:S(2)}) collective-permute-start(bf16[6,48,128]{2,1,0:T(8,128)(2,1)S(1)} %get-tuple-element.29), channel_id=1, source_target_pairs={{0,8},{1,9},{2,10},{3,11},{4,12},{5,13},{6,14},{7,15},{8,0},{9,1},... | collective-permute-start | bytes 221192 | tf_op jit(solution)/shard_map/ppermute | solution.py:438
  39.2 2.1 %collective-permute-start.9 = (bf16[6,48,128]{2,1,0:T(8,128)(2,1)S(1)}, bf16[6,48,128]{2,1,0:T(8,128)(2,1)S(1)}, u32[]{:S(2)}, u32[]{:S(2)}) collective-permute-start(bf16[6,48,128]{2,1,0:T(8,128)(2,1)S(1)} %get-tuple-element.30), channel_id=1, source_target_pairs={{0,12},{1,13},{2,14},{3,15},{4,8},{5,9},{6,10},{7,11},{8,4},{9,5},... | collective-permute-start | bytes 221192 | tf_op jit(solution)/shard_map/ppermute | solution.py:438
  41.4 0.0 copy-done.8
  41.4 0.8 %shard_map.105 = (bf16[48,128,128]{2,1,0:T(8,128)(2,1)}, f32[8,128]{1,0:T(8,128)S(1)}) custom-call(s32[2,128]{1,0:T(2,128)S(1)} %bitcast.16, s32[2]{0:T(128)S(1)} %copy-done.6, f32[6,48,128]{2,1,0:T(8,128)S(1)} %get-tuple-element.22.around, bf16[432,48]{1,0:T(8,128)(2,1)S(1)} %bitcast.12, f32[1,48]{1,0:T(1,128)S(1)} %bitcast.20, ...), custom_call_target="tpu_custom_call", output_to_operand_aliasing={{0}: (5, {})} | custom-call | tf_op jit(solution)/shard_map/pallas_call | solution.py:376
  42.2 0.0 collective-permute-done.7.a
  42.2 1.0 %collective-permute-done.8.b = bf16[6,48,128]{2,1,0:T(8,128)(2,1)S(1)} collective-permute-done((bf16[6,48,128]{2,1,0:T(8,128)(2,1)S(1)}, bf16[6,48,128]{2,1,0:T(8,128)(2,1)S(1)}, u32[]{:S(2)}, u32[]{:S(2)}) %collective-permute-start.8) | collective-permute-done | bytes 73760 | tf_op jit(solution)/shard_map/ppermute | solution.py:438
  43.2 1.6 %collective-permute-done.9.c = bf16[6,48,128]{2,1,0:T(8,128)(2,1)S(1)} collective-permute-done((bf16[6,48,128]{2,1,0:T(8,128)(2,1)S(1)}, bf16[6,48,128]{2,1,0:T(8,128)(2,1)S(1)}, u32[]{:S(2)}, u32[]{:S(2)}) %collective-permute-start.9) | collective-permute-done | bytes 73760 | tf_op jit(solution)/shard_map/ppermute | solution.py:438
  44.8 2.2 %collective-permute-start.12 = (bf16[5,48,128]{2,1,0:T(8,128)(2,1)S(1)}, bf16[5,48,128]{2,1,0:T(8,128)(2,1)S(1)}, u32[]{:S(2)}, u32[]{:S(2)}) collective-permute-start(bf16[5,48,128]{2,1,0:T(8,128)(2,1)S(1)} %get-tuple-element.34), channel_id=1, source_target_pairs={{0,18},{1,19},{2,16},{3,17},{4,22},{5,23},{6,20},{7,21},{8,26},{9,... | collective-permute-start | bytes 184328 | tf_op jit(solution)/shard_map/ppermute | solution.py:438
  47.0 2.9 %collective-permute-start.10 = (bf16[5,48,128]{2,1,0:T(8,128)(2,1)S(1)}, bf16[5,48,128]{2,1,0:T(8,128)(2,1)S(1)}, u32[]{:S(2)}, u32[]{:S(2)}) collective-permute-start(bf16[5,48,128]{2,1,0:T(8,128)(2,1)S(1)} %get-tuple-element.34), channel_id=1, source_target_pairs={{0,2},{1,3},{2,0},{3,1},{4,6},{5,7},{6,4},{7,5},{8,10},{9,11},{10,... | collective-permute-start | bytes 184328 | tf_op jit(solution)/shard_map/ppermute | solution.py:438
  49.9 0.2 collective-permute-start.11
  50.1 0.6 shard_map.107
  50.7 0.0 collective-permute-done.12.c
  50.7 1.3 %collective-permute-done.10.a = bf16[5,48,128]{2,1,0:T(8,128)(2,1)S(1)} collective-permute-done((bf16[5,48,128]{2,1,0:T(8,128)(2,1)S(1)}, bf16[5,48,128]{2,1,0:T(8,128)(2,1)S(1)}, u32[]{:S(2)}, u32[]{:S(2)}) %collective-permute-start.10) | collective-permute-done | bytes 61472 | tf_op jit(solution)/shard_map/ppermute | solution.py:438
  52.1 3.5 %collective-permute-done.11.b = bf16[5,48,128]{2,1,0:T(8,128)(2,1)S(1)} collective-permute-done((bf16[5,48,128]{2,1,0:T(8,128)(2,1)S(1)}, bf16[5,48,128]{2,1,0:T(8,128)(2,1)S(1)}, u32[]{:S(2)}, u32[]{:S(2)}) %collective-permute-start.11) | collective-permute-done | bytes 61472 | tf_op jit(solution)/shard_map/ppermute | solution.py:438
  55.6 0.8 %collective-permute-start.15 = (bf16[5,48,128]{2,1,0:T(8,128)(2,1)S(1)}, bf16[5,48,128]{2,1,0:T(8,128)(2,1)S(1)}, u32[]{:S(2)}, u32[]{:S(2)}) collective-permute-start(bf16[5,48,128]{2,1,0:T(8,128)(2,1)S(1)} %shard_map.108.after.keep), channel_id=1, source_target_pairs={{0,96},{1,97},{2,98},{3,99},{4,100},{5,101},{6,102},{7,103},{8,104... | collective-permute-start | bytes 184328 | tf_op jit(solution)/shard_map/ppermute | solution.py:438
  56.5 2.3 %collective-permute-start.14 = (bf16[5,48,128]{2,1,0:T(8,128)(2,1)S(1)}, bf16[5,48,128]{2,1,0:T(8,128)(2,1)S(1)}, u32[]{:S(2)}, u32[]{:S(2)}) collective-permute-start(bf16[5,48,128]{2,1,0:T(8,128)(2,1)S(1)} %shard_map.108.after.keep), channel_id=1, source_target_pairs={{0,64},{1,65},{2,66},{3,67},{4,68},{5,69},{6,70},{7,71},{8,72},{9,... | collective-permute-start | bytes 184328 | tf_op jit(solution)/shard_map/ppermute | solution.py:438
  58.8 1.0 %collective-permute-start.13 = (bf16[5,48,128]{2,1,0:T(8,128)(2,1)S(1)}, bf16[5,48,128]{2,1,0:T(8,128)(2,1)S(1)}, u32[]{:S(2)}, u32[]{:S(2)}) collective-permute-start(bf16[5,48,128]{2,1,0:T(8,128)(2,1)S(1)} %shard_map.108.after.keep), channel_id=1, source_target_pairs={{0,32},{1,33},{2,34},{3,35},{4,36},{5,37},{6,38},{7,39},{8,40},{9,... | collective-permute-start | bytes 184328 | tf_op jit(solution)/shard_map/ppermute | solution.py:438
  59.8 1.2 %shard_map.109 = (bf16[48,128,128]{2,1,0:T(8,128)(2,1)}, f32[8,128]{1,0:T(8,128)}) custom-call(s32[2,128]{1,0:T(2,128)S(1)} %bitcast.18, s32[2]{0:T(128)S(1)} %copy-done.6, f32[6,48,128]{2,1,0:T(8,128)S(1)} %get-tuple-element.22.around, bf16[432,48]{1,0:T(8,128)(2,1)S(1)} %bitcast.14, f32[1,48]{1,0:T(1,128)S(1)} %bitcast.22, ...), custom_call_target="tpu_custom_call", output_to_operand_aliasing={{0}: (5, {})} | custom-call | tf_op jit(solution)/shard_map/pallas_call | solution.py:376
  61.0 0.1 collective-permute-done.15.c
  61.2 1.0 %collective-permute-done.14.b = bf16[5,48,128]{2,1,0:T(8,128)(2,1)S(1)} collective-permute-done((bf16[5,48,128]{2,1,0:T(8,128)(2,1)S(1)}, bf16[5,48,128]{2,1,0:T(8,128)(2,1)S(1)}, u32[]{:S(2)}, u32[]{:S(2)}) %collective-permute-start.14) | collective-permute-done | bytes 61472 | tf_op jit(solution)/shard_map/ppermute | solution.py:438
  62.2 0.8 %collective-permute-done.13.a = bf16[5,48,128]{2,1,0:T(8,128)(2,1)S(1)} collective-permute-done((bf16[5,48,128]{2,1,0:T(8,128)(2,1)S(1)}, bf16[5,48,128]{2,1,0:T(8,128)(2,1)S(1)}, u32[]{:S(2)}, u32[]{:S(2)}) %collective-permute-start.13) | collective-permute-done | bytes 61472 | tf_op jit(solution)/shard_map/ppermute | solution.py:438
  63.0 0.8 %shard_map.110 = (f32[48,128]{1,0:T(8,128)}, f32[9,48,48]{2,1,0:T(8,128)}, f32[1,48]{1,0:T(1,128)}) custom-call(bf16[5,48,128]{2,1,0:T(8,128)(2,1)S(1)} %shard_map.108.after.keep, bf16[5,48,128]{2,1,0:T(8,128)(2,1)S(1)} %collective-permute-done.13.a, bf16[5,48,128]{2,1,0:T(8,128)(2,1)S(1)} %collective-permute-done.14.b, ...), custom_call_target="tpu_custom_call" | custom-call | tf_op jit(solution)/shard_map/pallas_call | solution.py:470
  (12 shorter events, 0.1 us)
Async XLA Ops:
  0.6 4.0 %collective-permute-start.1 = (bf16[48,128]{1,0:T(8,128)(2,1)}, bf16[48,128]{1,0:T(8,128)(2,1)S(1)}, u32[]{:S(2)}, u32[]{:S(2)}) collective-permute-start(bf16[48,128]{1,0:T(8,128)(2,1)} %own.1), channel_id=1, source_target_pairs={{0,2},{1,3},{2,0},{3,1},{4,6},{5,7},{6,4},{7,5},{8,10},{9,11},{10,... | collective-permute-start | bytes 36872 | tf_op jit(solution)/shard_map/ppermute | solution.py:438
  2.3 2.3 %collective-permute-start = (bf16[48,128]{1,0:T(8,128)(2,1)}, bf16[48,128]{1,0:T(8,128)(2,1)S(1)}, u32[]{:S(2)}, u32[]{:S(2)}) collective-permute-start(bf16[48,128]{1,0:T(8,128)(2,1)} %own.1), channel_id=1, source_target_pairs={{0,1},{1,0},{2,3},{3,2},{4,5},{5,4},{6,7},{7,6},{8,9},{9,8},{10,11... | collective-permute-start | bytes 36872 | tf_op jit(solution)/shard_map/ppermute | solution.py:438
  2.3 3.3 %collective-permute-start.2 = (bf16[48,128]{1,0:T(8,128)(2,1)}, bf16[48,128]{1,0:T(8,128)(2,1)S(1)}, u32[]{:S(2)}, u32[]{:S(2)}) collective-permute-start(bf16[48,128]{1,0:T(8,128)(2,1)} %own.1), channel_id=1, source_target_pairs={{0,3},{1,2},{2,1},{3,0},{4,7},{5,6},{6,5},{7,4},{8,11},{9,10},{10,... | collective-permute-start | bytes 36872 | tf_op jit(solution)/shard_map/ppermute | solution.py:438
  5.6 0.7 %copy-start.4 = (bf16[48,128]{1,0:T(8,128)(2,1)S(1)}, bf16[48,128]{1,0:T(8,128)(2,1)}, u32[]{:S(2)}) copy-start(bf16[48,128]{1,0:T(8,128)(2,1)} %own.1) | copy-start | bytes 36868
  7.0 10.4 %copy-start = (bf16[1,1,48,128,128]{4,3,2,1,0:T(8,128)(2,1)S(1)}, bf16[1,1,48,128,128]{4,3,2,1,0:T(8,128)(2,1)}, u32[]{:S(2)}) copy-start(bf16[1,1,48,128,128]{4,3,2,1,0:T(8,128)(2,1)} %param.12) | copy-start | bytes 4718596
  7.0 10.4 %copy-start.1 = (bf16[9,48,48]{2,1,0:T(8,128)(2,1)S(1)}, bf16[9,48,48]{2,1,0:T(8,128)(2,1)}, u32[]{:S(2)}) copy-start(bf16[9,48,48]{2,1,0:T(8,128)(2,1)} %param.8) | copy-start | bytes 124420
  7.0 10.4 %copy-start.2 = (bf16[2,144,512]{2,1,0:T(8,128)(2,1)S(1)}, bf16[2,144,512]{2,1,0:T(8,128)(2,1)}, u32[]{:S(2)}) copy-start(bf16[2,144,512]{2,1,0:T(8,128)(2,1)} %constant.2.clone.repeat) | copy-start | bytes 884740
  7.0 10.4 %copy-start.3 = (s32[128,2]{0,1:T(2,128)S(1)}, s32[128,2]{0,1:T(2,128)}, u32[]{:S(2)}) copy-start(s32[128,2]{0,1:T(2,128)} %param.11) | copy-start | bytes 3076
  7.0 7.2 %collective-permute-start.5 = (bf16[4,48,128]{2,1,0:T(8,128)(2,1)}, bf16[4,48,128]{2,1,0:T(8,128)(2,1)}, u32[]{:S(2)}, u32[]{:S(2)}) collective-permute-start(bf16[4,48,128]{2,1,0:T(8,128)(2,1)} %shard_map.102.quad), channel_id=1, source_target_pairs={{0,12},{1,13},{2,14},{3,15},{4,8},{5,9},{6,10},{7,11},{8,4},{9,5},... | collective-permute-start | bytes 147464 | tf_op jit(solution)/shard_map/ppermute | solution.py:438
  11.1 6.2 %collective-permute-start.4 = (bf16[4,48,128]{2,1,0:T(8,128)(2,1)}, bf16[4,48,128]{2,1,0:T(8,128)(2,1)}, u32[]{:S(2)}, u32[]{:S(2)}) collective-permute-start(bf16[4,48,128]{2,1,0:T(8,128)(2,1)} %shard_map.102.quad), channel_id=1, source_target_pairs={{0,8},{1,9},{2,10},{3,11},{4,12},{5,13},{6,14},{7,15},{8,0},{9,1},... | collective-permute-start | bytes 147464 | tf_op jit(solution)/shard_map/ppermute | solution.py:438
  11.1 6.2 %collective-permute-start.3 = (bf16[4,48,128]{2,1,0:T(8,128)(2,1)}, bf16[4,48,128]{2,1,0:T(8,128)(2,1)}, u32[]{:S(2)}, u32[]{:S(2)}) collective-permute-start(bf16[4,48,128]{2,1,0:T(8,128)(2,1)} %shard_map.102.quad), channel_id=1, source_target_pairs={{0,4},{1,5},{2,6},{3,7},{4,0},{5,1},{6,2},{7,3},{8,12},{9,13},{10,... | collective-permute-start | bytes 147464 | tf_op jit(solution)/shard_map/ppermute | solution.py:438
  17.3 0.7 %copy-start.5 = (s32[2]{0:T(128)S(1)}, s32[2]{0:T(128)}, u32[]{:S(2)}) copy-start(s32[2]{0:T(128)} %dilation.7) | copy-start | bytes 28
  18.0 0.7 %copy-start.7 = (f32[48]{0:T(128)S(1)}, f32[48]{0:T(128)}, u32[]{:S(2)}) copy-start(f32[48]{0:T(128)} %param.9) | copy-start | bytes 580
  18.6 22.7 %copy-start.6 = (s32[2]{0:T(128)S(1)}, s32[2]{0:T(128)}, u32[]{:S(2)}) copy-start(s32[2]{0:T(128)} %dilation.7) | copy-start | bytes 28
  18.6 22.7 %copy-start.8 = (f32[48]{0:T(128)S(1)}, f32[48]{0:T(128)}, u32[]{:S(2)}) copy-start(f32[48]{0:T(128)} %param.9) | copy-start | bytes 580
  34.9 1.7 %collective-permute-start.6 = (f32[12,48,128]{2,1,0:T(8,128)S(1)}, f32[12,48,128]{2,1,0:T(8,128)S(1)}, u32[]{:S(2)}, u32[]{:S(2)}) collective-permute-start(f32[12,48,128]{2,1,0:T(8,128)S(1)} %get-tuple-element.25), channel_id=1, source_target_pairs={{0,1},{1,0},{2,3},{3,2},{4,5},{5,4},{6,7},{7,6},{8,9},{9,8},{10,11... | collective-permute-start | bytes 884744 | tf_op jit(solution)/shard_map/ppermute | solution.py:438
  36.6 5.6 %collective-permute-start.7 = (bf16[6,48,128]{2,1,0:T(8,128)(2,1)S(1)}, bf16[6,48,128]{2,1,0:T(8,128)(2,1)S(1)}, u32[]{:S(2)}, u32[]{:S(2)}) collective-permute-start(bf16[6,48,128]{2,1,0:T(8,128)(2,1)S(1)} %get-tuple-element.28), channel_id=1, source_target_pairs={{0,4},{1,5},{2,6},{3,7},{4,0},{5,1},{6,2},{7,3},{8,12},{9,13},{10,... | collective-permute-start | bytes 221192 | tf_op jit(solution)/shard_map/ppermute | solution.py:438
  36.7 6.5 %collective-permute-start.8 = (bf16[6,48,128]{2,1,0:T(8,128)(2,1)S(1)}, bf16[6,48,128]{2,1,0:T(8,128)(2,1)S(1)}, u32[]{:S(2)}, u32[]{:S(2)}) collective-permute-start(bf16[6,48,128]{2,1,0:T(8,128)(2,1)S(1)} %get-tuple-element.29), channel_id=1, source_target_pairs={{0,8},{1,9},{2,10},{3,11},{4,12},{5,13},{6,14},{7,15},{8,0},{9,1},... | collective-permute-start | bytes 221192 | tf_op jit(solution)/shard_map/ppermute | solution.py:438
  39.2 5.6 %collective-permute-start.9 = (bf16[6,48,128]{2,1,0:T(8,128)(2,1)S(1)}, bf16[6,48,128]{2,1,0:T(8,128)(2,1)S(1)}, u32[]{:S(2)}, u32[]{:S(2)}) collective-permute-start(bf16[6,48,128]{2,1,0:T(8,128)(2,1)S(1)} %get-tuple-element.30), channel_id=1, source_target_pairs={{0,12},{1,13},{2,14},{3,15},{4,8},{5,9},{6,10},{7,11},{8,4},{9,5},... | collective-permute-start | bytes 221192 | tf_op jit(solution)/shard_map/ppermute | solution.py:438
  44.8 5.9 %collective-permute-start.12 = (bf16[5,48,128]{2,1,0:T(8,128)(2,1)S(1)}, bf16[5,48,128]{2,1,0:T(8,128)(2,1)S(1)}, u32[]{:S(2)}, u32[]{:S(2)}) collective-permute-start(bf16[5,48,128]{2,1,0:T(8,128)(2,1)S(1)} %get-tuple-element.34), channel_id=1, source_target_pairs={{0,18},{1,19},{2,16},{3,17},{4,22},{5,23},{6,20},{7,21},{8,26},{9,... | collective-permute-start | bytes 184328 | tf_op jit(solution)/shard_map/ppermute | solution.py:438
  47.0 5.1 %collective-permute-start.10 = (bf16[5,48,128]{2,1,0:T(8,128)(2,1)S(1)}, bf16[5,48,128]{2,1,0:T(8,128)(2,1)S(1)}, u32[]{:S(2)}, u32[]{:S(2)}) collective-permute-start(bf16[5,48,128]{2,1,0:T(8,128)(2,1)S(1)} %get-tuple-element.34), channel_id=1, source_target_pairs={{0,2},{1,3},{2,0},{3,1},{4,6},{5,7},{6,4},{7,5},{8,10},{9,11},{10,... | collective-permute-start | bytes 184328 | tf_op jit(solution)/shard_map/ppermute | solution.py:438
  49.9 5.7 %collective-permute-start.11 = (bf16[5,48,128]{2,1,0:T(8,128)(2,1)S(1)}, bf16[5,48,128]{2,1,0:T(8,128)(2,1)S(1)}, u32[]{:S(2)}, u32[]{:S(2)}) collective-permute-start(bf16[5,48,128]{2,1,0:T(8,128)(2,1)S(1)} %get-tuple-element.32.after.keep), channel_id=1, source_target_pairs={{0,16},{1,17},{2,18},{3,19},{4,20},{5,21},{6,22},{7,23},{8,24},{9,... | collective-permute-start | bytes 184328 | tf_op jit(solution)/shard_map/ppermute | solution.py:438
  55.6 5.5 %collective-permute-start.15 = (bf16[5,48,128]{2,1,0:T(8,128)(2,1)S(1)}, bf16[5,48,128]{2,1,0:T(8,128)(2,1)S(1)}, u32[]{:S(2)}, u32[]{:S(2)}) collective-permute-start(bf16[5,48,128]{2,1,0:T(8,128)(2,1)S(1)} %shard_map.108.after.keep), channel_id=1, source_target_pairs={{0,96},{1,97},{2,98},{3,99},{4,100},{5,101},{6,102},{7,103},{8,104... | collective-permute-start | bytes 184328 | tf_op jit(solution)/shard_map/ppermute | solution.py:438
  56.5 5.7 %collective-permute-start.14 = (bf16[5,48,128]{2,1,0:T(8,128)(2,1)S(1)}, bf16[5,48,128]{2,1,0:T(8,128)(2,1)S(1)}, u32[]{:S(2)}, u32[]{:S(2)}) collective-permute-start(bf16[5,48,128]{2,1,0:T(8,128)(2,1)S(1)} %shard_map.108.after.keep), channel_id=1, source_target_pairs={{0,64},{1,65},{2,66},{3,67},{4,68},{5,69},{6,70},{7,71},{8,72},{9,... | collective-permute-start | bytes 184328 | tf_op jit(solution)/shard_map/ppermute | solution.py:438
  58.8 4.2 %collective-permute-start.13 = (bf16[5,48,128]{2,1,0:T(8,128)(2,1)S(1)}, bf16[5,48,128]{2,1,0:T(8,128)(2,1)S(1)}, u32[]{:S(2)}, u32[]{:S(2)}) collective-permute-start(bf16[5,48,128]{2,1,0:T(8,128)(2,1)S(1)} %shard_map.108.after.keep), channel_id=1, source_target_pairs={{0,32},{1,33},{2,34},{3,35},{4,36},{5,37},{6,38},{7,39},{8,40},{9,... | collective-permute-start | bytes 184328 | tf_op jit(solution)/shard_map/ppermute | solution.py:438

commit v4 on v3

--- a/solution.py
+++ b/solution.py
@@ -20,7 +20,7 @@
 ROWS = 32
 PAD = 8
 PIECES = ((0, 48), (48, 48), (96, 32))
-VMEM_BYTES = 48 * 1024 * 1024
+VMEM_BYTES = 40 * 1024 * 1024
 
 NT = (((1,), (1,)), ((), ()))
 TN = (((0,), (0,)), ((), ()))
@@ -49,7 +49,7 @@
 def tile_of(fold_map, dilation):
     fold, col = position()
     slot = fold * 16 + col
-    return fold_map[0, slot], fold_map[1, slot], dilation[0], dilation[1]
+    return fold_map[0, slot], fold_map[1, slot], dilation[0, 0], dilation[1, 0]
 
 
 def place_of():
@@ -100,10 +100,6 @@
     )
 
 
-def bias_lanes(bias):
-    return jnp.broadcast_to(bias[...], (B, C)).T
-
-
 def store_rows(full, bias, first, stage32, count):
     for k in range(full.shape[1] // B):
         stage32[pl.ds(first + k, C, stride=count + PAD), :] = full[:, k * B : (k + 1) * B] + bias
@@ -115,20 +111,13 @@
 
 
 def gradient_kernel(
-    fold_map, dilation, quad, z1, z2, z3, conv_weight, repeat, bias_hbm, cot_hbm, cols_hbm,
-    send, keep, around, pair_hbm,
-    blocks, shift, minus, sums, grads, wgrad, table, cot, rows, cols, cot32, stage32, stage, bias_row, sems,
+    fold_map, dilation, quad, z1, z2, z3, conv_weight, repeat, bias, cot, cols,
+    send, keep, around, short, pair_hbm,
+    blocks, shift, minus, sums, grads, wgrad, table, rows, cot32, stage32, stage, sem,
 ):
     tile_i, tile_j, rate_r, rate_c = tile_of(fold_map, dilation)
     core_index = place_of()[2]
-    load_bias = pltpu.make_async_copy(bias_hbm, bias_row, sems.at[3])
-    load_bias.start()
-    load_cot = pltpu.make_async_copy(cot_hbm, cot, sems.at[0])
-    load_cols = pltpu.make_async_copy(cols_hbm, cols, sems.at[1])
-    load_cot.start()
-    load_cols.start()
     fill_blocks(quad, z1, z2, z3, blocks)
-    load_bias.wait()
     for k in range(3):
         around[k] = blocks[tile_i + k]
         around[3 + k] = blocks[tile_j + k]
@@ -137,6 +126,7 @@
     bias_mark = jnp.where(column == 432, 1.0, 0.0)
     grads[...] = jnp.zeros_like(grads)
     weight = conv_weight[...].astype(F32).T
+    short[...] = weight.astype(BF16)
     weight_wide = jnp.concatenate([weight, jnp.zeros((C, NK - 432), F32)], 1)
     empty = jnp.zeros((C, NK), F32)
 
@@ -183,17 +173,15 @@
         return cols[q]
 
     def cotangent_here():
-        load_cot.wait()
         for c in range(C):
             cot32[c * (B + PAD) : c * (B + PAD) + B, :] = cot[c].astype(F32)
         for q in range(B):
             rows[q] = cot32[pl.ds(q, C, stride=B + PAD), :].astype(BF16)
-        load_cols.wait()
 
     @pl.when(tile_i < tile_j)
     def one_tile():
         spread_lanes(blocks, tile_i, table, 0, B)
-        bias, short = bias_lanes(bias_row), weight.astype(BF16)
+        bias_now, short_now = bias[...], weight.astype(BF16)
         window = windows(blocks, tile_j, rate_c)
 
         def some(step, carry):
@@ -202,12 +190,12 @@
                 at = [table[DMAX + step * ROWS + k + m * rate_r] for m in (-1, 0, 1)]
                 taps = [jnp.maximum(at[u] + window[v], zero) for u in range(3) for v in range(3)]
                 parts.append(jnp.concatenate(taps, 0))
-            store_rows(dot(short, jnp.concatenate(parts, 1), NN), bias, step * ROWS, stage32, B)
+            store_rows(dot(short_now, jnp.concatenate(parts, 1), NN), bias_now, step * ROWS, stage32, B)
             return carry
 
         lax.fori_loop(0, B // ROWS, some, 0)
         round_rows(stage32, stage, B)
-        save_pair = pltpu.make_async_copy(stage, pair_hbm, sems.at[2])
+        save_pair = pltpu.make_async_copy(stage, pair_hbm, sem)
         save_pair.start()
 
         tables(0, tile_i, rate_r, 0, True)
@@ -281,24 +269,20 @@
 
 
 def fold_kernel(
-    first, count, fold_map, dilation, around, conv_weight, bias_hbm, pair_before, after,
+    first, count, fold_map, dilation, around, short, bias, pair_before, after,
     pair_hbm, token,
-    table_i, table_j, stage32, stage, bias_row, sems,
+    table_i, table_j, stage32, stage, sems,
 ):
     tile_i, tile_j, rate_r, rate_c = tile_of(fold_map, dilation)
     token[...] = jnp.zeros_like(token)
 
     @pl.when(tile_i > tile_j)
     def two_triangles():
-        load_bias = pltpu.make_async_copy(bias_hbm, bias_row, sems.at[0])
-        load_bias.start()
         spread_lanes(around, 0, table_i, first, count)
         spread_lanes(around, 3, table_j, first, count)
         up_window, low_window = windows(around, 0, rate_c), windows(around, 3, rate_r)
         lane = lax.broadcasted_iota(jnp.int32, (C, B), 1).astype(BF16)
-        short = conv_weight[...].astype(F32).T.astype(BF16)
-        load_bias.wait()
-        bias, zero = bias_lanes(bias_row), jnp.zeros((), BF16)
+        short_now, bias_now, zero = short[...], bias[...], jnp.zeros((), BF16)
         saves = []
         for chunk in range(count // 16):
             parts = []
@@ -313,11 +297,11 @@
                     for v in range(3)
                 ]
                 parts.append(jnp.concatenate([jnp.maximum(x, zero) for x in taps], 0))
-            full = dot(short, jnp.concatenate(parts, 1), NN)
-            store_rows(full, bias, 0, stage32.at[chunk], 16)
+            full = dot(short_now, jnp.concatenate(parts, 1), NN)
+            store_rows(full, bias_now, 0, stage32.at[chunk], 16)
             round_rows(stage32.at[chunk], stage.at[chunk], 16)
             here = pair_hbm.at[:, pl.ds(first + chunk * 16, 16), :]
-            saves.append(pltpu.make_async_copy(stage.at[chunk], here, sems.at[1 + chunk]))
+            saves.append(pltpu.make_async_copy(stage.at[chunk], here, sems.at[chunk]))
             saves[-1].start()
         for save in saves:
             save.wait()
@@ -348,9 +332,15 @@
 def gradients(fold_map, dilation, pieces, conv_weight, conv_bias, cot, cot_cols):
     return call(
         gradient_kernel,
-        [SMEM, SMEM] + [VMEM] * 6 + [HBM] * 3,
-        (shape((12, C, B), F32), shape((12, C, B), F32), shape((6, C, B), F32), shape((C, B, B), BF16)),
-        (VMEM, VMEM, VMEM, HBM),
+        [SMEM, SMEM] + [VMEM] * 9,
+        (
+            shape((12, C, B), F32),
+            shape((12, C, B), F32),
+            shape((6, C, B), F32),
+            shape((C, 432), BF16),
+            shape((C, B, B), BF16),
+        ),
+        (VMEM, VMEM, VMEM, VMEM, HBM),
         [
             pltpu.VMEM((18, C, B), F32),
             pltpu.VMEM((4, B, NK), F32),
@@ -359,23 +349,20 @@
             pltpu.VMEM((18, C, B), F32),
             pltpu.VMEM((C, NK), F32),
             pltpu.VMEM((B + 2 * DMAX, C, B), BF16),
-            pltpu.VMEM((C, B, B), BF16),
-            pltpu.VMEM((B, C, B), BF16),
             pltpu.VMEM((B, C, B), BF16),
             pltpu.VMEM((C * (B + PAD), B), F32),
             pltpu.VMEM((C * (B + PAD), B), F32),
             pltpu.VMEM((C, B, B), BF16),
-            pltpu.VMEM((1, C), F32),
-            pltpu.SemaphoreType.DMA((4,)),
+            pltpu.SemaphoreType.DMA,
         ],
     )(fold_map, dilation, *pieces, conv_weight, repeat_table(), conv_bias, cot, cot_cols)
 
 
-def fold(which, fold_map, dilation, around, conv_weight, conv_bias, pair, after):
+def fold(which, fold_map, dilation, around, short, bias, pair, after):
     first, count = PIECES[which]
     return call(
         functools.partial(fold_kernel, first, count),
-        [SMEM, SMEM, VMEM, VMEM, HBM, HBM, ANY],
+        [SMEM, SMEM, VMEM, VMEM, VMEM, HBM, ANY],
         (shape((C, B, B), BF16), shape((8, B), F32)),
         (HBM, VMEM),
         [
@@ -383,11 +370,10 @@
             pltpu.VMEM((count + 2 * DMAX, C, B), BF16),
             pltpu.VMEM((count // 16, C * (16 + PAD), B), F32),
             pltpu.VMEM((count // 16, C, 16, B), BF16),
-            pltpu.VMEM((1, C), F32),
-            pltpu.SemaphoreType.DMA((1 + count // 16,)),
+            pltpu.SemaphoreType.DMA((count // 16,)),
         ],
         {5: 0},
-    )(fold_map, dilation, around, conv_weight, conv_bias, pair, after)
+    )(fold_map, dilation, around, short, bias, pair, after)
 
 
 def after_core_kernel(keep, got, own, to1, to2, to3):
@@ -429,7 +415,7 @@
 
 
 def body(bin_embed, conv_weight, conv_bias, dilation, fold_map, cotangent):
-    fold_map = fold_map.T
+    fold_map, dilation = fold_map.T, jnp.broadcast_to(dilation[:, None], (2, B))
 
     def swap(value, fold_bits, col_bits):
         route = [
@@ -444,13 +430,13 @@
 
     cot = cotangent[0, 0]
     cot_cols = jnp.transpose(cot, (2, 0, 1))
-    weight, bias = conv_weight.reshape(9 * C, C), conv_bias.reshape(1, C)
-    send, keep, around, pair_out = gradients(
+    weight, bias = conv_weight.reshape(9 * C, C), jnp.broadcast_to(conv_bias[:, None], (C, B))
+    send, keep, around, short, pair_out = gradients(
         fold_map, dilation, pieces, weight, bias, cot, cot_cols
     )
 
     def next_rows(which, pair_out, after):
-        return fold(which, fold_map, dilation, around, weight, bias, pair_out, after)
+        return fold(which, fold_map, dilation, around, short, bias, pair_out, after)
 
     got = swap(send, 0, 1)
     half, part = shape((6, C, B), BF16), shape((5, C, B), BF16)

time: 64.6 us -> 62.7 us (0.971); the launches traced: 63.8 us -> 62.9 us
  Pallas kernels: 20.4 us -> 19.2 us
  waiting for transfers between devices: 17 us -> 18.1 us
    ppermute x16, waiting for transfers between devices: 17 us -> 18.1 us  [swap(): return lax.ppermute(value, ('fold', 'col'), route)]
    pallas_call x1, Pallas kernels: 16.2 us -> 15.6 us  [gradients(): call(gradient_kernel, [SMEM, SMEM] + [VMEM] * 9, (shape((12, C, B), F32),...]
    unnamed x19 -> x15, local copies, waits for them, and re-layouts: 4.06 us -> 3.65 us
  transfers between devices with their start and end apart: 16 -> 16, of which waited for: 12 -> 11; matrix products, arithmetic and copies ran while one was open for 3% -> 3% of each run, Pallas kernels for 4% -> 4%
where the time goes in v4:
time: 62.7 us; the launch traced here: 62.9 us
  starting transfers between devices  21.1 us (34%)
  Pallas kernels  19.2 us (31%)
  waiting for transfers between devices  18.1 us (29%)
  local copies, waits for them, and re-layouts  3.79 us (6%)
  between operations  0.77 us (1%)
    ppermute x16, starting transfers between devices, swap(): return lax.ppermute(value, ('fold', 'col'), route)  21.1 us
    ppermute x16, waiting for transfers between devices, swap(): return lax.ppermute(value, ('fold', 'col'), route)  18.1 us
    pallas_call x1, Pallas kernels, gradients(): call(gradient_kernel, [SMEM, SMEM] + [VMEM] * 9, (shape((12, C, B), F32),...  15.6 us
    unnamed x15, local copies, waits for them, and re-layouts  3.65 us
    pallas_call x3, Pallas kernels, fold(): call(functools.partial(fold_kernel, first, count), [SMEM, SMEM, VMEM, VME...  2.62 us
  transfers between devices with their start and end apart: 16, of which 11 were waited for; matrix products, arithmetic and copies ran while one was open for 3% of the time, Pallas kernels for 4%

profile of v4, /device:TPU:0, one launch (start us, length us, event | category | flops | bytes accessed | tf_op | source)
XLA Modules:
  0.0 62.9 jit_solution(11964740261137766956)
XLA Ops:
  0.6 1.7 %collective-permute-start.1 = (bf16[48,128]{1,0:T(8,128)(2,1)}, bf16[48,128]{1,0:T(8,128)(2,1)S(1)}, u32[]{:S(2)}, u32[]{:S(2)}) collective-permute-start(bf16[48,128]{1,0:T(8,128)(2,1)} %own.1), channel_id=1, source_target_pairs={{0,2},{1,3},{2,0},{3,1},{4,6},{5,7},{6,4},{7,5},{8,10},{9,11},{10,... | collective-permute-start | bytes 36872 | tf_op jit(solution)/shard_map/ppermute | solution.py:424
  2.3 0.0 collective-permute-start
  2.3 0.6 collective-permute-start.2
  2.9 1.8 %collective-permute-done.1.xlo = bf16[48,128]{1,0:T(8,128)(2,1)S(1)} collective-permute-done((bf16[48,128]{1,0:T(8,128)(2,1)}, bf16[48,128]{1,0:T(8,128)(2,1)S(1)}, u32[]{:S(2)}, u32[]{:S(2)}) %collective-permute-start.1) | collective-permute-done | bytes 12320 | tf_op jit(solution)/shard_map/ppermute | solution.py:424
  4.6 0.0 collective-permute-done.core
  4.6 1.0 %collective-permute-done.2.both = bf16[48,128]{1,0:T(8,128)(2,1)S(1)} collective-permute-done((bf16[48,128]{1,0:T(8,128)(2,1)}, bf16[48,128]{1,0:T(8,128)(2,1)S(1)}, u32[]{:S(2)}, u32[]{:S(2)}) %collective-permute-start.2) | collective-permute-done | bytes 12320 | tf_op jit(solution)/shard_map/ppermute | solution.py:424
  5.6 0.7 %copy-done.4 = bf16[48,128]{1,0:T(8,128)(2,1)S(1)} copy-done((bf16[48,128]{1,0:T(8,128)(2,1)S(1)}, bf16[48,128]{1,0:T(8,128)(2,1)}, u32[]{:S(2)}) %copy-start.4) | copy-done | bytes 12312
  6.3 0.0 copy-start
  6.3 0.0 copy-start.1
  6.4 0.0 copy-start.3
  6.4 4.1 %collective-permute-start.5 = (bf16[4,48,128]{2,1,0:T(8,128)(2,1)S(1)}, bf16[4,48,128]{2,1,0:T(8,128)(2,1)S(1)}, u32[]{:S(2)}, u32[]{:S(2)}) collective-permute-start(bf16[4,48,128]{2,1,0:T(8,128)(2,1)S(1)} %shard_map.102.quad), channel_id=1, source_target_pairs={{0,12},{1,13},{2,14},{3,15},{4,8},{5,9},{6,10},{7,11},{8,4},{9,5},... | collective-permute-start | bytes 147464 | tf_op jit(solution)/shard_map/ppermute | solution.py:424
  10.5 0.0 collective-permute-start.4
  10.5 0.9 %collective-permute-start.3 = (bf16[4,48,128]{2,1,0:T(8,128)(2,1)S(1)}, bf16[4,48,128]{2,1,0:T(8,128)(2,1)}, u32[]{:S(2)}, u32[]{:S(2)}) collective-permute-start(bf16[4,48,128]{2,1,0:T(8,128)(2,1)S(1)} %shard_map.102.quad), channel_id=1, source_target_pairs={{0,4},{1,5},{2,6},{3,7},{4,0},{5,1},{6,2},{7,3},{8,12},{9,13},{10,... | collective-permute-start | bytes 147464 | tf_op jit(solution)/shard_map/ppermute | solution.py:424
  11.4 2.0 %copy.14 = bf16[1,1,48,128,128]{3,2,4,1,0:T(8,128)(2,1)S(1)} copy(bf16[1,1,48,128,128]{4,3,2,1,0:T(8,128)(2,1)} %param.12) | data formatting | bytes 3145728 | tf_op args[5]
  13.5 0.0 collective-permute-done.5.z3
  13.5 3.0 %collective-permute-done.4.z2 = bf16[4,48,128]{2,1,0:T(8,128)(2,1)} collective-permute-done((bf16[4,48,128]{2,1,0:T(8,128)(2,1)S(1)}, bf16[4,48,128]{2,1,0:T(8,128)(2,1)}, u32[]{:S(2)}, u32[]{:S(2)}) %collective-permute-start.4) | collective-permute-done | bytes 49184 | tf_op jit(solution)/shard_map/ppermute | solution.py:424
  16.5 0.0 collective-permute-done.3.z1
  16.5 0.1 broadcast_in_dim.6.dilation
  16.6 0.1 broadcast_in_dim.7.bias
  16.7 0.0 copy-done.1
  16.7 0.0 copy-start.2
  16.7 0.9 %copy-done.2 = bf16[9,48,48]{2,1,0:T(8,128)(2,1)S(1)} copy-done((bf16[9,48,48]{2,1,0:T(8,128)(2,1)S(1)}, bf16[9,48,48]{2,1,0:T(8,128)(2,1)}, u32[]{:S(2)}) %copy-start.2) | copy-done | bytes 41496
  17.6 15.6 %shard_map.103 = (f32[12,48,128]{2,1,0:T(8,128)S(1)}, f32[12,48,128]{2,1,0:T(8,128)S(1)}, f32[6,48,128]{2,1,0:T(8,128)S(1)}, bf16[48,432]{1,0:T(8,128)(2,1)S(1)}, bf16[48,128,128]{2,1,0:T(8,128)(2,1)}) custom-call(s32[2,128]{1,0:T(2,128)S(1)} %bitcast.11, s32[2,128]{1,0:T(2,128)S(1)} %broadcast_in_dim.6.dilation, bf16[4,48,128]{2,1,0:T(8,128)(2,1)S(1)} %shard_map.102.quad, ...), custom_call_target="tpu_custom_call" | custom-call | tf_op jit(solution)/shard_map/pallas_call | solution.py:333
  33.1 0.1 collective-permute-start.6
  33.2 1.6 %collective-permute-done.6.got = f32[12,48,128]{2,1,0:T(8,128)S(1)} collective-permute-done((f32[12,48,128]{2,1,0:T(8,128)S(1)}, f32[12,48,128]{2,1,0:T(8,128)S(1)}, u32[]{:S(2)}, u32[]{:S(2)}) %collective-permute-start.6) | collective-permute-done | bytes 294944 | tf_op jit(solution)/shard_map/ppermute | solution.py:424
  34.8 0.1 shard_map.104
  34.9 0.1 collective-permute-start.7
  34.9 2.5 %collective-permute-start.8 = (bf16[6,48,128]{2,1,0:T(8,128)(2,1)S(1)}, bf16[6,48,128]{2,1,0:T(8,128)(2,1)S(1)}, u32[]{:S(2)}, u32[]{:S(2)}) collective-permute-start(bf16[6,48,128]{2,1,0:T(8,128)(2,1)S(1)} %get-tuple-element.31), channel_id=1, source_target_pairs={{0,8},{1,9},{2,10},{3,11},{4,12},{5,13},{6,14},{7,15},{8,0},{9,1},... | collective-permute-start | bytes 221192 | tf_op jit(solution)/shard_map/ppermute | solution.py:424
  37.5 2.1 %collective-permute-start.9 = (bf16[6,48,128]{2,1,0:T(8,128)(2,1)S(1)}, bf16[6,48,128]{2,1,0:T(8,128)(2,1)S(1)}, u32[]{:S(2)}, u32[]{:S(2)}) collective-permute-start(bf16[6,48,128]{2,1,0:T(8,128)(2,1)S(1)} %get-tuple-element.32), channel_id=1, source_target_pairs={{0,12},{1,13},{2,14},{3,15},{4,8},{5,9},{6,10},{7,11},{8,4},{9,5},... | collective-permute-start | bytes 221192 | tf_op jit(solution)/shard_map/ppermute | solution.py:424
  39.6 0.8 %shard_map.105 = (bf16[48,128,128]{2,1,0:T(8,128)(2,1)}, f32[8,128]{1,0:T(8,128)S(1)}) custom-call(s32[2,128]{1,0:T(2,128)S(1)} %bitcast.12, s32[2,128]{1,0:T(2,128)S(1)} %broadcast_in_dim.6.dilation, f32[6,48,128]{2,1,0:T(8,128)S(1)} %get-tuple-element.23.around, bf16[48,432]{1,0:T(8,128)(2,1)S(1)} %get-tuple-element.24.short, ...), custom_call_target="tpu_custom_call", output_to_operand_aliasing={{0}: (5, {})} | custom-call | tf_op jit(solution)/shard_map/pallas_call | solution.py:363
  40.5 0.0 collective-permute-done.7.a
  40.5 1.0 %collective-permute-done.8.b = bf16[6,48,128]{2,1,0:T(8,128)(2,1)S(1)} collective-permute-done((bf16[6,48,128]{2,1,0:T(8,128)(2,1)S(1)}, bf16[6,48,128]{2,1,0:T(8,128)(2,1)S(1)}, u32[]{:S(2)}, u32[]{:S(2)}) %collective-permute-start.8) | collective-permute-done | bytes 73760 | tf_op jit(solution)/shard_map/ppermute | solution.py:424
  41.4 1.6 %collective-permute-done.9.c = bf16[6,48,128]{2,1,0:T(8,128)(2,1)S(1)} collective-permute-done((bf16[6,48,128]{2,1,0:T(8,128)(2,1)S(1)}, bf16[6,48,128]{2,1,0:T(8,128)(2,1)S(1)}, u32[]{:S(2)}, u32[]{:S(2)}) %collective-permute-start.9) | collective-permute-done | bytes 73760 | tf_op jit(solution)/shard_map/ppermute | solution.py:424
  43.1 2.2 %collective-permute-start.12 = (bf16[5,48,128]{2,1,0:T(8,128)(2,1)S(1)}, bf16[5,48,128]{2,1,0:T(8,128)(2,1)S(1)}, u32[]{:S(2)}, u32[]{:S(2)}) collective-permute-start(bf16[5,48,128]{2,1,0:T(8,128)(2,1)S(1)} %get-tuple-element.36), channel_id=1, source_target_pairs={{0,18},{1,19},{2,16},{3,17},{4,22},{5,23},{6,20},{7,21},{8,26},{9,... | collective-permute-start | bytes 184328 | tf_op jit(solution)/shard_map/ppermute | solution.py:424
  45.3 2.2 %collective-permute-start.10 = (bf16[5,48,128]{2,1,0:T(8,128)(2,1)S(1)}, bf16[5,48,128]{2,1,0:T(8,128)(2,1)S(1)}, u32[]{:S(2)}, u32[]{:S(2)}) collective-permute-start(bf16[5,48,128]{2,1,0:T(8,128)(2,1)S(1)} %get-tuple-element.36), channel_id=1, source_target_pairs={{0,2},{1,3},{2,0},{3,1},{4,6},{5,7},{6,4},{7,5},{8,10},{9,11},{10,... | collective-permute-start | bytes 184328 | tf_op jit(solution)/shard_map/ppermute | solution.py:424
  47.5 0.4 collective-permute-start.11
  47.9 0.6 shard_map.107
  48.5 0.1 collective-permute-done.12.c
  48.6 1.1 %collective-permute-done.10.a = bf16[5,48,128]{2,1,0:T(8,128)(2,1)S(1)} collective-permute-done((bf16[5,48,128]{2,1,0:T(8,128)(2,1)S(1)}, bf16[5,48,128]{2,1,0:T(8,128)(2,1)S(1)}, u32[]{:S(2)}, u32[]{:S(2)}) %collective-permute-start.10) | collective-permute-done | bytes 61472 | tf_op jit(solution)/shard_map/ppermute | solution.py:424
  49.7 3.5 %collective-permute-done.11.b = bf16[5,48,128]{2,1,0:T(8,128)(2,1)S(1)} collective-permute-done((bf16[5,48,128]{2,1,0:T(8,128)(2,1)S(1)}, bf16[5,48,128]{2,1,0:T(8,128)(2,1)S(1)}, u32[]{:S(2)}, u32[]{:S(2)}) %collective-permute-start.11) | collective-permute-done | bytes 61472 | tf_op jit(solution)/shard_map/ppermute | solution.py:424
  53.3 3.1 %collective-permute-start.15 = (bf16[5,48,128]{2,1,0:T(8,128)(2,1)S(1)}, bf16[5,48,128]{2,1,0:T(8,128)(2,1)S(1)}, u32[]{:S(2)}, u32[]{:S(2)}) collective-permute-start(bf16[5,48,128]{2,1,0:T(8,128)(2,1)S(1)} %shard_map.108.after.keep), channel_id=1, source_target_pairs={{0,96},{1,97},{2,98},{3,99},{4,100},{5,101},{6,102},{7,103},{8,104... | collective-permute-start | bytes 184328 | tf_op jit(solution)/shard_map/ppermute | solution.py:424
  56.4 0.0 collective-permute-start.14
  56.4 1.1 %collective-permute-start.13 = (bf16[5,48,128]{2,1,0:T(8,128)(2,1)S(1)}, bf16[5,48,128]{2,1,0:T(8,128)(2,1)S(1)}, u32[]{:S(2)}, u32[]{:S(2)}) collective-permute-start(bf16[5,48,128]{2,1,0:T(8,128)(2,1)S(1)} %shard_map.108.after.keep), channel_id=1, source_target_pairs={{0,32},{1,33},{2,34},{3,35},{4,36},{5,37},{6,38},{7,39},{8,40},{9,... | collective-permute-start | bytes 184328 | tf_op jit(solution)/shard_map/ppermute | solution.py:424
  57.5 1.2 %shard_map.109 = (bf16[48,128,128]{2,1,0:T(8,128)(2,1)}, f32[8,128]{1,0:T(8,128)}) custom-call(s32[2,128]{1,0:T(2,128)S(1)} %bitcast.14, s32[2,128]{1,0:T(2,128)S(1)} %broadcast_in_dim.6.dilation, f32[6,48,128]{2,1,0:T(8,128)S(1)} %get-tuple-element.23.around, bf16[48,432]{1,0:T(8,128)(2,1)S(1)} %get-tuple-element.24.short, ...), custom_call_target="tpu_custom_call", output_to_operand_aliasing={{0}: (5, {})} | custom-call | tf_op jit(solution)/shard_map/pallas_call | solution.py:363
  58.6 0.1 collective-permute-done.15.c
  58.8 3.3 %collective-permute-done.14.b = bf16[5,48,128]{2,1,0:T(8,128)(2,1)S(1)} collective-permute-done((bf16[5,48,128]{2,1,0:T(8,128)(2,1)S(1)}, bf16[5,48,128]{2,1,0:T(8,128)(2,1)S(1)}, u32[]{:S(2)}, u32[]{:S(2)}) %collective-permute-start.14) | collective-permute-done | bytes 61472 | tf_op jit(solution)/shard_map/ppermute | solution.py:424
  62.1 0.0 collective-permute-done.13.a
  62.1 0.8 %shard_map.110 = (f32[48,128]{1,0:T(8,128)}, f32[9,48,48]{2,1,0:T(8,128)}, f32[1,48]{1,0:T(1,128)}) custom-call(bf16[5,48,128]{2,1,0:T(8,128)(2,1)S(1)} %shard_map.108.after.keep, bf16[5,48,128]{2,1,0:T(8,128)(2,1)S(1)} %collective-permute-done.13.a, bf16[5,48,128]{2,1,0:T(8,128)(2,1)S(1)} %collective-permute-done.14.b, ...), custom_call_target="tpu_custom_call" | custom-call | tf_op jit(solution)/shard_map/pallas_call | solution.py:456
  (10 shorter events, 0.1 us)
Async XLA Ops:
  0.6 4.0 %collective-permute-start.1 = (bf16[48,128]{1,0:T(8,128)(2,1)}, bf16[48,128]{1,0:T(8,128)(2,1)S(1)}, u32[]{:S(2)}, u32[]{:S(2)}) collective-permute-start(bf16[48,128]{1,0:T(8,128)(2,1)} %own.1), channel_id=1, source_target_pairs={{0,2},{1,3},{2,0},{3,1},{4,6},{5,7},{6,4},{7,5},{8,10},{9,11},{10,... | collective-permute-start | bytes 36872 | tf_op jit(solution)/shard_map/ppermute | solution.py:424
  2.3 2.3 %collective-permute-start = (bf16[48,128]{1,0:T(8,128)(2,1)}, bf16[48,128]{1,0:T(8,128)(2,1)S(1)}, u32[]{:S(2)}, u32[]{:S(2)}) collective-permute-start(bf16[48,128]{1,0:T(8,128)(2,1)} %own.1), channel_id=1, source_target_pairs={{0,1},{1,0},{2,3},{3,2},{4,5},{5,4},{6,7},{7,6},{8,9},{9,8},{10,11... | collective-permute-start | bytes 36872 | tf_op jit(solution)/shard_map/ppermute | solution.py:424
  2.3 3.3 %collective-permute-start.2 = (bf16[48,128]{1,0:T(8,128)(2,1)}, bf16[48,128]{1,0:T(8,128)(2,1)S(1)}, u32[]{:S(2)}, u32[]{:S(2)}) collective-permute-start(bf16[48,128]{1,0:T(8,128)(2,1)} %own.1), channel_id=1, source_target_pairs={{0,3},{1,2},{2,1},{3,0},{4,7},{5,6},{6,5},{7,4},{8,11},{9,10},{10,... | collective-permute-start | bytes 36872 | tf_op jit(solution)/shard_map/ppermute | solution.py:424
  5.6 0.7 %copy-start.4 = (bf16[48,128]{1,0:T(8,128)(2,1)S(1)}, bf16[48,128]{1,0:T(8,128)(2,1)}, u32[]{:S(2)}) copy-start(bf16[48,128]{1,0:T(8,128)(2,1)} %own.1) | copy-start | bytes 36868
  6.3 10.2 %copy-start.6 = (s32[2]{0:T(128)S(1)}, s32[2]{0:T(128)}, u32[]{:S(2)}) copy-start(s32[2]{0:T(128)} %param.10) | copy-start | bytes 28
  6.3 10.2 %copy-start.5 = (f32[48]{0:T(128)S(1)}, f32[48]{0:T(128)}, u32[]{:S(2)}) copy-start(f32[48]{0:T(128)} %param.9) | copy-start | bytes 580
  6.3 10.3 %copy-start = (bf16[1,1,48,128,128]{4,3,2,1,0:T(8,128)(2,1)S(1)}, bf16[1,1,48,128,128]{4,3,2,1,0:T(8,128)(2,1)}, u32[]{:S(2)}) copy-start(bf16[1,1,48,128,128]{4,3,2,1,0:T(8,128)(2,1)} %param.12) | copy-start | bytes 4718596
  6.3 10.3 %copy-start.1 = (bf16[2,144,512]{2,1,0:T(8,128)(2,1)S(1)}, bf16[2,144,512]{2,1,0:T(8,128)(2,1)}, u32[]{:S(2)}) copy-start(bf16[2,144,512]{2,1,0:T(8,128)(2,1)} %constant.2.clone.repeat) | copy-start | bytes 884740
  6.4 10.3 %copy-start.3 = (s32[128,2]{0,1:T(2,128)S(1)}, s32[128,2]{0,1:T(2,128)}, u32[]{:S(2)}) copy-start(s32[128,2]{0,1:T(2,128)} %param.11) | copy-start | bytes 3076
  6.4 7.1 %collective-permute-start.5 = (bf16[4,48,128]{2,1,0:T(8,128)(2,1)S(1)}, bf16[4,48,128]{2,1,0:T(8,128)(2,1)S(1)}, u32[]{:S(2)}, u32[]{:S(2)}) collective-permute-start(bf16[4,48,128]{2,1,0:T(8,128)(2,1)S(1)} %shard_map.102.quad), channel_id=1, source_target_pairs={{0,12},{1,13},{2,14},{3,15},{4,8},{5,9},{6,10},{7,11},{8,4},{9,5},... | collective-permute-start | bytes 147464 | tf_op jit(solution)/shard_map/ppermute | solution.py:424
  10.5 6.0 %collective-permute-start.4 = (bf16[4,48,128]{2,1,0:T(8,128)(2,1)S(1)}, bf16[4,48,128]{2,1,0:T(8,128)(2,1)}, u32[]{:S(2)}, u32[]{:S(2)}) collective-permute-start(bf16[4,48,128]{2,1,0:T(8,128)(2,1)S(1)} %shard_map.102.quad), channel_id=1, source_target_pairs={{0,8},{1,9},{2,10},{3,11},{4,12},{5,13},{6,14},{7,15},{8,0},{9,1},... | collective-permute-start | bytes 147464 | tf_op jit(solution)/shard_map/ppermute | solution.py:424
  10.5 6.0 %collective-permute-start.3 = (bf16[4,48,128]{2,1,0:T(8,128)(2,1)S(1)}, bf16[4,48,128]{2,1,0:T(8,128)(2,1)}, u32[]{:S(2)}, u32[]{:S(2)}) collective-permute-start(bf16[4,48,128]{2,1,0:T(8,128)(2,1)S(1)} %shard_map.102.quad), channel_id=1, source_target_pairs={{0,4},{1,5},{2,6},{3,7},{4,0},{5,1},{6,2},{7,3},{8,12},{9,13},{10,... | collective-permute-start | bytes 147464 | tf_op jit(solution)/shard_map/ppermute | solution.py:424
  16.7 0.9 %copy-start.2 = (bf16[9,48,48]{2,1,0:T(8,128)(2,1)S(1)}, bf16[9,48,48]{2,1,0:T(8,128)(2,1)}, u32[]{:S(2)}) copy-start(bf16[9,48,48]{2,1,0:T(8,128)(2,1)} %param.8) | copy-start | bytes 124420
  33.1 1.7 %collective-permute-start.6 = (f32[12,48,128]{2,1,0:T(8,128)S(1)}, f32[12,48,128]{2,1,0:T(8,128)S(1)}, u32[]{:S(2)}, u32[]{:S(2)}) collective-permute-start(f32[12,48,128]{2,1,0:T(8,128)S(1)} %get-tuple-element.27), channel_id=1, source_target_pairs={{0,1},{1,0},{2,3},{3,2},{4,5},{5,4},{6,7},{7,6},{8,9},{9,8},{10,11... | collective-permute-start | bytes 884744 | tf_op jit(solution)/shard_map/ppermute | solution.py:424
  34.9 5.6 %collective-permute-start.7 = (bf16[6,48,128]{2,1,0:T(8,128)(2,1)S(1)}, bf16[6,48,128]{2,1,0:T(8,128)(2,1)S(1)}, u32[]{:S(2)}, u32[]{:S(2)}) collective-permute-start(bf16[6,48,128]{2,1,0:T(8,128)(2,1)S(1)} %get-tuple-element.30), channel_id=1, source_target_pairs={{0,4},{1,5},{2,6},{3,7},{4,0},{5,1},{6,2},{7,3},{8,12},{9,13},{10,... | collective-permute-start | bytes 221192 | tf_op jit(solution)/shard_map/ppermute | solution.py:424
  34.9 6.5 %collective-permute-start.8 = (bf16[6,48,128]{2,1,0:T(8,128)(2,1)S(1)}, bf16[6,48,128]{2,1,0:T(8,128)(2,1)S(1)}, u32[]{:S(2)}, u32[]{:S(2)}) collective-permute-start(bf16[6,48,128]{2,1,0:T(8,128)(2,1)S(1)} %get-tuple-element.31), channel_id=1, source_target_pairs={{0,8},{1,9},{2,10},{3,11},{4,12},{5,13},{6,14},{7,15},{8,0},{9,1},... | collective-permute-start | bytes 221192 | tf_op jit(solution)/shard_map/ppermute | solution.py:424
  37.5 5.6 %collective-permute-start.9 = (bf16[6,48,128]{2,1,0:T(8,128)(2,1)S(1)}, bf16[6,48,128]{2,1,0:T(8,128)(2,1)S(1)}, u32[]{:S(2)}, u32[]{:S(2)}) collective-permute-start(bf16[6,48,128]{2,1,0:T(8,128)(2,1)S(1)} %get-tuple-element.32), channel_id=1, source_target_pairs={{0,12},{1,13},{2,14},{3,15},{4,8},{5,9},{6,10},{7,11},{8,4},{9,5},... | collective-permute-start | bytes 221192 | tf_op jit(solution)/shard_map/ppermute | solution.py:424
  43.1 5.5 %collective-permute-start.12 = (bf16[5,48,128]{2,1,0:T(8,128)(2,1)S(1)}, bf16[5,48,128]{2,1,0:T(8,128)(2,1)S(1)}, u32[]{:S(2)}, u32[]{:S(2)}) collective-permute-start(bf16[5,48,128]{2,1,0:T(8,128)(2,1)S(1)} %get-tuple-element.36), channel_id=1, source_target_pairs={{0,18},{1,19},{2,16},{3,17},{4,22},{5,23},{6,20},{7,21},{8,26},{9,... | collective-permute-start | bytes 184328 | tf_op jit(solution)/shard_map/ppermute | solution.py:424
  45.3 4.4 %collective-permute-start.10 = (bf16[5,48,128]{2,1,0:T(8,128)(2,1)S(1)}, bf16[5,48,128]{2,1,0:T(8,128)(2,1)S(1)}, u32[]{:S(2)}, u32[]{:S(2)}) collective-permute-start(bf16[5,48,128]{2,1,0:T(8,128)(2,1)S(1)} %get-tuple-element.36), channel_id=1, source_target_pairs={{0,2},{1,3},{2,0},{3,1},{4,6},{5,7},{6,4},{7,5},{8,10},{9,11},{10,... | collective-permute-start | bytes 184328 | tf_op jit(solution)/shard_map/ppermute | solution.py:424
  47.5 5.7 %collective-permute-start.11 = (bf16[5,48,128]{2,1,0:T(8,128)(2,1)S(1)}, bf16[5,48,128]{2,1,0:T(8,128)(2,1)S(1)}, u32[]{:S(2)}, u32[]{:S(2)}) collective-permute-start(bf16[5,48,128]{2,1,0:T(8,128)(2,1)S(1)} %get-tuple-element.34.after.keep), channel_id=1, source_target_pairs={{0,16},{1,17},{2,18},{3,19},{4,20},{5,21},{6,22},{7,23},{8,24},{9,... | collective-permute-start | bytes 184328 | tf_op jit(solution)/shard_map/ppermute | solution.py:424
  53.3 5.5 %collective-permute-start.15 = (bf16[5,48,128]{2,1,0:T(8,128)(2,1)S(1)}, bf16[5,48,128]{2,1,0:T(8,128)(2,1)S(1)}, u32[]{:S(2)}, u32[]{:S(2)}) collective-permute-start(bf16[5,48,128]{2,1,0:T(8,128)(2,1)S(1)} %shard_map.108.after.keep), channel_id=1, source_target_pairs={{0,96},{1,97},{2,98},{3,99},{4,100},{5,101},{6,102},{7,103},{8,104... | collective-permute-start | bytes 184328 | tf_op jit(solution)/shard_map/ppermute | solution.py:424
  56.4 5.7 %collective-permute-start.14 = (bf16[5,48,128]{2,1,0:T(8,128)(2,1)S(1)}, bf16[5,48,128]{2,1,0:T(8,128)(2,1)S(1)}, u32[]{:S(2)}, u32[]{:S(2)}) collective-permute-start(bf16[5,48,128]{2,1,0:T(8,128)(2,1)S(1)} %shard_map.108.after.keep), channel_id=1, source_target_pairs={{0,64},{1,65},{2,66},{3,67},{4,68},{5,69},{6,70},{7,71},{8,72},{9,... | collective-permute-start | bytes 184328 | tf_op jit(solution)/shard_map/ppermute | solution.py:424
  56.4 5.7 %collective-permute-start.13 = (bf16[5,48,128]{2,1,0:T(8,128)(2,1)S(1)}, bf16[5,48,128]{2,1,0:T(8,128)(2,1)S(1)}, u32[]{:S(2)}, u32[]{:S(2)}) collective-permute-start(bf16[5,48,128]{2,1,0:T(8,128)(2,1)S(1)} %shard_map.108.after.keep), channel_id=1, source_target_pairs={{0,32},{1,33},{2,34},{3,35},{4,36},{5,37},{6,38},{7,39},{8,40},{9,... | collective-permute-start | bytes 184328 | tf_op jit(solution)/shard_map/ppermute | solution.py:424

commit v5 on v4

--- a/solution.py
+++ b/solution.py
@@ -58,8 +58,9 @@
 
 
 def quad_kernel(own, core, xlo, both, out):
-    for k, block in enumerate((own, core, xlo, both)):
-        out[k] = block[...]
+    out[0] = own[0]
+    for k, block in enumerate((core, xlo, both)):
+        out[1 + k] = block[...]
 
 
 def fill_blocks(quad, z1, z2, z3, blocks):
@@ -111,8 +112,8 @@
 
 
 def gradient_kernel(
-    fold_map, dilation, quad, z1, z2, z3, conv_weight, repeat, bias, cot, cols,
-    send, keep, around, short, pair_hbm,
+    fold_map, dilation, quad, z1, z2, z3, weight, repeat, bias, cot, cols,
+    send, keep, around, meta, pair_hbm,
     blocks, shift, minus, sums, grads, wgrad, table, rows, cot32, stage32, stage, sem,
 ):
     tile_i, tile_j, rate_r, rate_c = tile_of(fold_map, dilation)
@@ -125,9 +126,9 @@
     column = lax.broadcasted_iota(jnp.int32, (B, NK), 1)
     bias_mark = jnp.where(column == 432, 1.0, 0.0)
     grads[...] = jnp.zeros_like(grads)
-    weight = conv_weight[...].astype(F32).T
-    short[...] = weight.astype(BF16)
-    weight_wide = jnp.concatenate([weight, jnp.zeros((C, NK - 432), F32)], 1)
+    for k, value in enumerate((tile_i, tile_j, rate_r, rate_c)):
+        meta[k] = value
+    weight_wide = jnp.concatenate([weight[...].astype(F32), jnp.zeros((C, NK - 432), F32)], 1)
     empty = jnp.zeros((C, NK), F32)
 
     def tables(slot, tile, rate, which, mark):
@@ -181,7 +182,7 @@
     @pl.when(tile_i < tile_j)
     def one_tile():
         spread_lanes(blocks, tile_i, table, 0, B)
-        bias_now, short_now = bias[...], weight.astype(BF16)
+        bias_now, weight_now = bias[...], weight[...]
         window = windows(blocks, tile_j, rate_c)
 
         def some(step, carry):
@@ -190,7 +191,7 @@
                 at = [table[DMAX + step * ROWS + k + m * rate_r] for m in (-1, 0, 1)]
                 taps = [jnp.maximum(at[u] + window[v], zero) for u in range(3) for v in range(3)]
                 parts.append(jnp.concatenate(taps, 0))
-            store_rows(dot(short_now, jnp.concatenate(parts, 1), NN), bias_now, step * ROWS, stage32, B)
+            store_rows(dot(weight_now, jnp.concatenate(parts, 1), NN), bias_now, step * ROWS, stage32, B)
             return carry
 
         lax.fori_loop(0, B // ROWS, some, 0)
@@ -269,12 +270,10 @@
 
 
 def fold_kernel(
-    first, count, fold_map, dilation, around, short, bias, pair_before, after,
-    pair_hbm, token,
+    first, count, meta, around, weight, bias, pair_before, after, pair_hbm,
     table_i, table_j, stage32, stage, sems,
 ):
-    tile_i, tile_j, rate_r, rate_c = tile_of(fold_map, dilation)
-    token[...] = jnp.zeros_like(token)
+    tile_i, tile_j, rate_r, rate_c = meta[0], meta[1], meta[2], meta[3]
 
     @pl.when(tile_i > tile_j)
     def two_triangles():
@@ -282,7 +281,7 @@
         spread_lanes(around, 3, table_j, first, count)
         up_window, low_window = windows(around, 0, rate_c), windows(around, 3, rate_r)
         lane = lax.broadcasted_iota(jnp.int32, (C, B), 1).astype(BF16)
-        short_now, bias_now, zero = short[...], bias[...], jnp.zeros((), BF16)
+        weight_now, bias_now, zero = weight[...], bias[...], jnp.zeros((), BF16)
         saves = []
         for chunk in range(count // 16):
             parts = []
@@ -297,7 +296,7 @@
                     for v in range(3)
                 ]
                 parts.append(jnp.concatenate([jnp.maximum(x, zero) for x in taps], 0))
-            full = dot(short_now, jnp.concatenate(parts, 1), NN)
+            full = dot(weight_now, jnp.concatenate(parts, 1), NN)
             store_rows(full, bias_now, 0, stage32.at[chunk], 16)
             round_rows(stage32.at[chunk], stage.at[chunk], 16)
             here = pair_hbm.at[:, pl.ds(first + chunk * 16, 16), :]
@@ -329,7 +328,7 @@
     )
 
 
-def gradients(fold_map, dilation, pieces, conv_weight, conv_bias, cot, cot_cols):
+def gradients(fold_map, dilation, pieces, weight, bias, cot, cot_cols):
     return call(
         gradient_kernel,
         [SMEM, SMEM] + [VMEM] * 9,
@@ -337,10 +336,10 @@
             shape((12, C, B), F32),
             shape((12, C, B), F32),
             shape((6, C, B), F32),
-            shape((C, 432), BF16),
+            shape((4,), jnp.int32),
             shape((C, B, B), BF16),
         ),
-        (VMEM, VMEM, VMEM, VMEM, HBM),
+        (VMEM, VMEM, VMEM, SMEM, HBM),
         [
             pltpu.VMEM((18, C, B), F32),
             pltpu.VMEM((4, B, NK), F32),
@@ -355,16 +354,16 @@
             pltpu.VMEM((C, B, B), BF16),
             pltpu.SemaphoreType.DMA,
         ],
-    )(fold_map, dilation, *pieces, conv_weight, repeat_table(), conv_bias, cot, cot_cols)
-
-
-def fold(which, fold_map, dilation, around, short, bias, pair, after):
+    )(fold_map, dilation, *pieces, weight, repeat_table(), bias, cot, cot_cols)
+
+
+def fold(which, meta, around, weight, bias, pair, after):
     first, count = PIECES[which]
     return call(
         functools.partial(fold_kernel, first, count),
-        [SMEM, SMEM, VMEM, VMEM, VMEM, HBM, ANY],
-        (shape((C, B, B), BF16), shape((8, B), F32)),
-        (HBM, VMEM),
+        [SMEM, VMEM, VMEM, VMEM, HBM, ANY],
+        shape((C, B, B), BF16),
+        HBM,
         [
             pltpu.VMEM((count + 2 * DMAX, C, B), BF16),
             pltpu.VMEM((count + 2 * DMAX, C, B), BF16),
@@ -372,8 +371,8 @@
             pltpu.VMEM((count // 16, C, 16, B), BF16),
             pltpu.SemaphoreType.DMA((count // 16,)),
         ],
-        {5: 0},
-    )(fold_map, dilation, around, short, bias, pair, after)
+        {4: 0},
+    )(meta, around, weight, bias, pair, after)
 
 
 def after_core_kernel(keep, got, own, to1, to2, to3):
@@ -391,7 +390,7 @@
     return (own[k].astype(F32) + a[k].astype(F32)) + (b[k].astype(F32) + c[k].astype(F32))
 
 
-def after_z_kernel(keep, a, b, c, token, own, other):
+def after_z_kernel(keep, a, b, c, pair, own, other):
     x = place_of()[1]
     own[0] = sum4(keep, a, b, c, x).astype(BF16)
     other[0] = sum4(keep, a, b, c, 1 - x).astype(BF16)
@@ -401,7 +400,7 @@
         other[1 + k] = total
 
 
-def after_x_kernel(keep, a, b, c, token, own):
+def after_x_kernel(keep, a, b, c, pair, own):
     for k in range(5):
         own[k] = sum4(keep, a, b, c, k).astype(BF16)
 
@@ -424,34 +423,37 @@
         return lax.ppermute(value, ("fold", "col"), route)
 
     core, xlo, both = swap(bin_embed, 0, 1), swap(bin_embed, 0, 2), swap(bin_embed, 0, 3)
-    quad = call(quad_kernel, [VMEM] * 4, shape((4, C, B), BF16), VMEM)(bin_embed, core, xlo, both)
+    quad = call(quad_kernel, [VMEM] * 4, shape((4, C, B), BF16), VMEM)(
+        jnp.broadcast_to(bin_embed[None], (2, C, B)), core, xlo, both
+    )
     z1, z2, z3 = (swap(quad, 0, 4 * step) for step in (1, 2, 3))
     pieces = (quad, z1, z2, z3)
 
     cot = cotangent[0, 0]
     cot_cols = jnp.transpose(cot, (2, 0, 1))
-    weight, bias = conv_weight.reshape(9 * C, C), jnp.broadcast_to(conv_bias[:, None], (C, B))
-    send, keep, around, short, pair_out = gradients(
+    weight = jnp.transpose(conv_weight, (2, 0, 1)).reshape(C, 9 * C)
+    bias = jnp.broadcast_to(conv_bias[:, None], (C, B))
+    send, keep, around, meta, pair_out = gradients(
         fold_map, dilation, pieces, weight, bias, cot, cot_cols
     )
 
     def next_rows(which, pair_out, after):
-        return fold(which, fold_map, dilation, around, short, bias, pair_out, after)
+        return fold(which, meta, around, weight, bias, pair_out, after)
 
     got = swap(send, 0, 1)
     half, part = shape((6, C, B), BF16), shape((5, C, B), BF16)
     keep, to1, to2, to3 = call(
         after_core_kernel, [VMEM, VMEM], (half,) * 4, (VMEM,) * 4
     )(keep, got)
-    pair_out, token = next_rows(0, pair_out, keep)
+    pair_out = next_rows(0, pair_out, keep)
     a, b, c = swap(to1, 0, 4), swap(to2, 0, 8), swap(to3, 0, 12)
     keep, other = call(
-        after_z_kernel, [VMEM] * 4 + [ANY], (part, part), (VMEM, VMEM)
-    )(keep, a, b, c, token)
-    pair_out, token = next_rows(1, pair_out, keep)
+        after_z_kernel, [VMEM] * 4 + [HBM], (part, part), (VMEM, VMEM)
+    )(keep, a, b, c, pair_out)
+    pair_out = next_rows(1, pair_out, keep)
     a, b, c = swap(other, 0, 2), swap(keep, 1, 0), swap(other, 1, 2)
-    keep = call(after_x_kernel, [VMEM] * 4 + [ANY], part, VMEM)(keep, a, b, c, token)
-    pair_out, token = next_rows(2, pair_out, keep)
+    keep = call(after_x_kernel, [VMEM] * 4 + [HBM], part, VMEM)(keep, a, b, c, pair_out)
+    pair_out = next_rows(2, pair_out, keep)
     a, b, c = swap(keep, 2, 0), swap(keep, 4, 0), swap(keep, 6, 0)
     grad_embed, grad_weight, grad_bias = call(
         after_y_kernel,

time: 62.7 us -> 65.3 us (1.041)
  local copies, waits for them, and re-layouts: 3.79 us -> 6.84 us
  waiting for transfers between devices: 18.1 us -> 16.5 us
  starting transfers between devices: 21.1 us -> 22.2 us
    ppermute x16, waiting for transfers between devices: 18.1 us -> 16.5 us  [swap(): return lax.ppermute(value, ('fold', 'col'), route)]
    unnamed x15, local copies, waits for them, and re-layouts: 3.65 us -> 5.01 us
    ppermute x16, starting transfers between devices: 21.1 us -> 22.2 us  [swap(): return lax.ppermute(value, ('fold', 'col'), route)]
    reshape x0 -> x1, local copies, waits for them, and re-layouts: none -> 0.98 us  [body(): weight = jnp.transpose(conv_weight, (2, 0, 1)).reshape(C, 9 * C)]
    broadcast_in_dim x1 -> x2, local copies, waits for them, and re-layouts: 0.07 us -> 0.78 us  [the longest x1 0.71 us: body(): jnp.broadcast_to(bin_embed[None], (2, C, B))]
    pallas_call x5, Pallas kernels: 2.7 us -> 2.01 us  [the longest x3 1.93 us: fold(): call(functools.partial(fold_kernel, first, count), [SMEM, VMEM, VMEM, VME...]
  transfers between devices with their start and end apart: 16 -> 16, of which waited for: 11 -> 11; matrix products, arithmetic and copies ran while one was open for 3% -> 5% of each run, Pallas kernels for 4% -> 3%
where the time goes in v5:
time: 65.3 us; the launch traced here: 65.2 us
  starting transfers between devices  22.2 us (34%)
  Pallas kernels  18.9 us (29%)
  waiting for transfers between devices  16.5 us (25%)
  local copies, waits for them, and re-layouts  6.84 us (10%)
  between operations  0.8 us (1%)
    ppermute x16, starting transfers between devices, swap(): return lax.ppermute(value, ('fold', 'col'), route)  22.2 us
    ppermute x16, waiting for transfers between devices, swap(): return lax.ppermute(value, ('fold', 'col'), route)  16.5 us
    pallas_call x1, Pallas kernels, gradients(): call(gradient_kernel, [SMEM, SMEM] + [VMEM] * 9, (shape((12, C, B), F32),...  16 us
    unnamed x15, local copies, waits for them, and re-layouts  5.01 us
    pallas_call x3, Pallas kernels, fold(): call(functools.partial(fold_kernel, first, count), [SMEM, VMEM, VMEM, VME...  1.93 us
  transfers between devices with their start and end apart: 16, of which 11 were waited for; matrix products, arithmetic and copies ran while one was open for 5% of the time, Pallas kernels for 3%

profile of v5, /device:TPU:0, one launch (start us, length us, event | category | flops | bytes accessed | tf_op | source)
XLA Modules:
  0.0 65.2 jit_solution(9645837303084949691)
XLA Ops:
  0.6 0.1 collective-permute-start
  0.7 1.7 %collective-permute-start.2 = (bf16[48,128]{1,0:T(8,128)(2,1)}, bf16[48,128]{1,0:T(8,128)(2,1)S(1)}, u32[]{:S(2)}, u32[]{:S(2)}) collective-permute-start(bf16[48,128]{1,0:T(8,128)(2,1)} %param.7), channel_id=1, source_target_pairs={{0,3},{1,2},{2,1},{3,0},{4,7},{5,6},{6,5},{7,4},{8,11},{9,10},{10,... | collective-permute-start | bytes 36872 | tf_op jit(solution)/shard_map/ppermute | solution.py:423
  2.4 0.5 collective-permute-start.1
  2.9 0.0 collective-permute-done.core
  2.9 1.3 %collective-permute-done.2.both = bf16[48,128]{1,0:T(8,128)(2,1)S(1)} collective-permute-done((bf16[48,128]{1,0:T(8,128)(2,1)}, bf16[48,128]{1,0:T(8,128)(2,1)S(1)}, u32[]{:S(2)}, u32[]{:S(2)}) %collective-permute-start.2) | collective-permute-done | bytes 12320 | tf_op jit(solution)/shard_map/ppermute | solution.py:423
  4.1 2.2 %collective-permute-done.1.xlo = bf16[48,128]{1,0:T(8,128)(2,1)S(1)} collective-permute-done((bf16[48,128]{1,0:T(8,128)(2,1)}, bf16[48,128]{1,0:T(8,128)(2,1)S(1)}, u32[]{:S(2)}, u32[]{:S(2)}) %collective-permute-start.1) | collective-permute-done | bytes 12320 | tf_op jit(solution)/shard_map/ppermute | solution.py:423
  6.3 0.7 %broadcast_in_dim.9.own = bf16[2,48,128]{2,1,0:T(8,128)(2,1)S(1)} broadcast(bf16[48,128]{1,0:T(8,128)(2,1)} %param.7), dimensions={1,2} | broadcast | bytes 36864 | tf_op jit(solution)/shard_map/broadcast_in_dim | solution.py:427
  7.0 4.1 %collective-permute-start.5 = (bf16[4,48,128]{2,1,0:T(8,128)(2,1)S(1)}, bf16[4,48,128]{2,1,0:T(8,128)(2,1)}, u32[]{:S(2)}, u32[]{:S(2)}) collective-permute-start(bf16[4,48,128]{2,1,0:T(8,128)(2,1)S(1)} %shard_map.102.quad), channel_id=1, source_target_pairs={{0,12},{1,13},{2,14},{3,15},{4,8},{5,9},{6,10},{7,11},{8,4},{9,5},... | collective-permute-start | bytes 147464 | tf_op jit(solution)/shard_map/ppermute | solution.py:423
  11.1 0.0 collective-permute-start.4
  11.2 0.9 %collective-permute-start.3 = (bf16[4,48,128]{2,1,0:T(8,128)(2,1)S(1)}, bf16[4,48,128]{2,1,0:T(8,128)(2,1)}, u32[]{:S(2)}, u32[]{:S(2)}) collective-permute-start(bf16[4,48,128]{2,1,0:T(8,128)(2,1)S(1)} %shard_map.102.quad), channel_id=1, source_target_pairs={{0,4},{1,5},{2,6},{3,7},{4,0},{5,1},{6,2},{7,3},{8,12},{9,13},{10,... | collective-permute-start | bytes 147464 | tf_op jit(solution)/shard_map/ppermute | solution.py:423
  12.1 1.0 %copy.18.weight = bf16[48,432]{1,0:T(8,128)(2,1)S(1)} copy(bf16[48,432]{0,1:T(8,128)(2,1)} %bitcast.14) | data formatting | bytes 82944 | tf_op jit(solution)/shard_map/reshape | solution.py:434
  13.1 0.0 copy-start.6
  13.1 0.0 copy-start.5
  13.1 0.0 copy-start.2
  13.1 0.0 copy-start.3
  13.1 0.0 copy-start.4
  13.1 2.2 %copy.17 = bf16[1,1,48,128,128]{3,2,4,1,0:T(8,128)(2,1)S(1)} copy(bf16[1,1,48,128,128]{4,3,2,1,0:T(8,128)(2,1)} %param.12) | data formatting | bytes 3145728 | tf_op args[5]
  15.3 0.0 collective-permute-done.5.z3
  15.3 1.5 %collective-permute-done.4.z2 = bf16[4,48,128]{2,1,0:T(8,128)(2,1)} collective-permute-done((bf16[4,48,128]{2,1,0:T(8,128)(2,1)S(1)}, bf16[4,48,128]{2,1,0:T(8,128)(2,1)}, u32[]{:S(2)}, u32[]{:S(2)}) %collective-permute-start.4) | collective-permute-done | bytes 49184 | tf_op jit(solution)/shard_map/ppermute | solution.py:423
  16.8 0.0 collective-permute-done.3.z1
  16.9 0.1 broadcast_in_dim.8.dilation
  16.9 0.1 broadcast_in_dim.10.bias
  17.0 16.0 %shard_map.103 = (f32[12,48,128]{2,1,0:T(8,128)S(1)}, f32[12,48,128]{2,1,0:T(8,128)S(1)}, f32[6,48,128]{2,1,0:T(8,128)S(1)}, s32[4]{0:T(128)S(1)}, bf16[48,128,128]{2,1,0:T(8,128)(2,1)}) custom-call(s32[2,128]{1,0:T(2,128)S(1)} %bitcast.13, s32[2,128]{1,0:T(2,128)S(1)} %broadcast_in_dim.8.dilation, bf16[4,48,128]{2,1,0:T(8,128)(2,1)S(1)} %shard_map.102.quad, ...), custom_call_target="tpu_custom_call" | custom-call | tf_op jit(solution)/shard_map/pallas_call | solution.py:332
  33.1 0.1 collective-permute-start.6
  33.2 1.6 %collective-permute-done.6.got = f32[12,48,128]{2,1,0:T(8,128)S(1)} collective-permute-done((f32[12,48,128]{2,1,0:T(8,128)S(1)}, f32[12,48,128]{2,1,0:T(8,128)S(1)}, u32[]{:S(2)}, u32[]{:S(2)}) %collective-permute-start.6) | collective-permute-done | bytes 294944 | tf_op jit(solution)/shard_map/ppermute | solution.py:423
  34.8 0.1 collective-permute-start.7
  34.9 3.2 %collective-permute-start.8 = (bf16[6,48,128]{2,1,0:T(8,128)(2,1)S(1)}, bf16[6,48,128]{2,1,0:T(8,128)(2,1)S(1)}, u32[]{:S(2)}, u32[]{:S(2)}) collective-permute-start(bf16[6,48,128]{2,1,0:T(8,128)(2,1)S(1)} %get-tuple-element.25), channel_id=1, source_target_pairs={{0,8},{1,9},{2,10},{3,11},{4,12},{5,13},{6,14},{7,15},{8,0},{9,1},... | collective-permute-start | bytes 221192 | tf_op jit(solution)/shard_map/ppermute | solution.py:423
  38.0 1.5 %collective-permute-start.9 = (bf16[6,48,128]{2,1,0:T(8,128)(2,1)S(1)}, bf16[6,48,128]{2,1,0:T(8,128)(2,1)S(1)}, u32[]{:S(2)}, u32[]{:S(2)}) collective-permute-start(bf16[6,48,128]{2,1,0:T(8,128)(2,1)S(1)} %get-tuple-element.26), channel_id=1, source_target_pairs={{0,12},{1,13},{2,14},{3,15},{4,8},{5,9},{6,10},{7,11},{8,4},{9,5},... | collective-permute-start | bytes 221192 | tf_op jit(solution)/shard_map/ppermute | solution.py:423
  39.5 0.8 %shard_map.105.pair.pair_before = bf16[48,128,128]{2,1,0:T(8,128)(2,1)} custom-call(s32[4]{0:T(128)S(1)} %get-tuple-element.18.meta, f32[6,48,128]{2,1,0:T(8,128)S(1)} %get-tuple-element.19.around, bf16[48,432]{1,0:T(8,128)(2,1)S(1)} %copy.18.weight, f32[48,128]{1,0:T(8,128)S(1)} %broadcast_in_dim.10.bias, ...), custom_call_target="tpu_custom_call", output_to_operand_aliasing={{}: (4, {})} | custom-call | tf_op jit(solution)/shard_map/pallas_call | solution.py:362
  40.4 0.0 collective-permute-done.7.a
  40.4 1.8 %collective-permute-done.8.b = bf16[6,48,128]{2,1,0:T(8,128)(2,1)S(1)} collective-permute-done((bf16[6,48,128]{2,1,0:T(8,128)(2,1)S(1)}, bf16[6,48,128]{2,1,0:T(8,128)(2,1)S(1)}, u32[]{:S(2)}, u32[]{:S(2)}) %collective-permute-start.8) | collective-permute-done | bytes 73760 | tf_op jit(solution)/shard_map/ppermute | solution.py:423
  42.1 1.5 %collective-permute-done.9.c = bf16[6,48,128]{2,1,0:T(8,128)(2,1)S(1)} collective-permute-done((bf16[6,48,128]{2,1,0:T(8,128)(2,1)S(1)}, bf16[6,48,128]{2,1,0:T(8,128)(2,1)S(1)}, u32[]{:S(2)}, u32[]{:S(2)}) %collective-permute-start.9) | collective-permute-done | bytes 73760 | tf_op jit(solution)/shard_map/ppermute | solution.py:423
  43.7 1.4 %copy-done = bf16[48,128,128]{2,1,0:T(8,128)(2,1)S(1)} copy-done((bf16[48,128,128]{2,1,0:T(8,128)(2,1)S(1)}, bf16[48,128,128]{2,1,0:T(8,128)(2,1)}, u32[]{:S(2)}) %copy-start) | copy-done | bytes 1572888
  45.1 2.0 %collective-permute-start.12 = (bf16[5,48,128]{2,1,0:T(8,128)(2,1)S(1)}, bf16[5,48,128]{2,1,0:T(8,128)(2,1)S(1)}, u32[]{:S(2)}, u32[]{:S(2)}) collective-permute-start(bf16[5,48,128]{2,1,0:T(8,128)(2,1)S(1)} %get-tuple-element.28), channel_id=1, source_target_pairs={{0,18},{1,19},{2,16},{3,17},{4,22},{5,23},{6,20},{7,21},{8,26},{9,... | collective-permute-start | bytes 184328 | tf_op jit(solution)/shard_map/ppermute | solution.py:423
  47.1 0.6 collective-permute-start.10
  47.7 2.1 %collective-permute-start.11 = (bf16[5,48,128]{2,1,0:T(8,128)(2,1)S(1)}, bf16[5,48,128]{2,1,0:T(8,128)(2,1)S(1)}, u32[]{:S(2)}, u32[]{:S(2)}) collective-permute-start(bf16[5,48,128]{2,1,0:T(8,128)(2,1)S(1)} %get-tuple-element.27.after.keep), channel_id=1, source_target_pairs={{0,16},{1,17},{2,18},{3,19},{4,20},{5,21},{6,22},{7,23},{8,24},{9,... | collective-permute-start | bytes 184328 | tf_op jit(solution)/shard_map/ppermute | solution.py:423
  49.9 0.6 shard_map.107.pair.pair_before
  50.5 0.8 %collective-permute-done.12.c = bf16[5,48,128]{2,1,0:T(8,128)(2,1)S(1)} collective-permute-done((bf16[5,48,128]{2,1,0:T(8,128)(2,1)S(1)}, bf16[5,48,128]{2,1,0:T(8,128)(2,1)S(1)}, u32[]{:S(2)}, u32[]{:S(2)}) %collective-permute-start.12) | collective-permute-done | bytes 61472 | tf_op jit(solution)/shard_map/ppermute | solution.py:423
  51.3 0.1 collective-permute-done.10.a
  51.4 2.1 %collective-permute-done.11.b = bf16[5,48,128]{2,1,0:T(8,128)(2,1)S(1)} collective-permute-done((bf16[5,48,128]{2,1,0:T(8,128)(2,1)S(1)}, bf16[5,48,128]{2,1,0:T(8,128)(2,1)S(1)}, u32[]{:S(2)}, u32[]{:S(2)}) %collective-permute-start.11) | collective-permute-done | bytes 61472 | tf_op jit(solution)/shard_map/ppermute | solution.py:423
  53.5 1.4 %copy-done.1 = bf16[48,128,128]{2,1,0:T(8,128)(2,1)S(1)} copy-done((bf16[48,128,128]{2,1,0:T(8,128)(2,1)S(1)}, bf16[48,128,128]{2,1,0:T(8,128)(2,1)}, u32[]{:S(2)}) %copy-start.1) | copy-done | bytes 1572888
  54.9 3.1 %collective-permute-start.15 = (bf16[5,48,128]{2,1,0:T(8,128)(2,1)S(1)}, bf16[5,48,128]{2,1,0:T(8,128)(2,1)S(1)}, u32[]{:S(2)}, u32[]{:S(2)}) collective-permute-start(bf16[5,48,128]{2,1,0:T(8,128)(2,1)S(1)} %shard_map.108.after.keep), channel_id=1, source_target_pairs={{0,96},{1,97},{2,98},{3,99},{4,100},{5,101},{6,102},{7,103},{8,104... | collective-permute-start | bytes 184328 | tf_op jit(solution)/shard_map/ppermute | solution.py:423
  58.0 2.1 %collective-permute-start.14 = (bf16[5,48,128]{2,1,0:T(8,128)(2,1)S(1)}, bf16[5,48,128]{2,1,0:T(8,128)(2,1)S(1)}, u32[]{:S(2)}, u32[]{:S(2)}) collective-permute-start(bf16[5,48,128]{2,1,0:T(8,128)(2,1)S(1)} %shard_map.108.after.keep), channel_id=1, source_target_pairs={{0,64},{1,65},{2,66},{3,67},{4,68},{5,69},{6,70},{7,71},{8,72},{9,... | collective-permute-start | bytes 184328 | tf_op jit(solution)/shard_map/ppermute | solution.py:423
  60.1 0.0 collective-permute-start.13
  60.1 0.6 shard_map.109
  60.7 3.0 %collective-permute-done.14.b = bf16[5,48,128]{2,1,0:T(8,128)(2,1)S(1)} collective-permute-done((bf16[5,48,128]{2,1,0:T(8,128)(2,1)S(1)}, bf16[5,48,128]{2,1,0:T(8,128)(2,1)S(1)}, u32[]{:S(2)}, u32[]{:S(2)}) %collective-permute-start.14) | collective-permute-done | bytes 61472 | tf_op jit(solution)/shard_map/ppermute | solution.py:423
  63.7 0.6 collective-permute-done.13.a
  64.4 0.8 %shard_map.110 = (f32[48,128]{1,0:T(8,128)}, f32[9,48,48]{2,1,0:T(8,128)}, f32[1,48]{1,0:T(1,128)}) custom-call(bf16[5,48,128]{2,1,0:T(8,128)(2,1)S(1)} %shard_map.108.after.keep, bf16[5,48,128]{2,1,0:T(8,128)(2,1)S(1)} %collective-permute-done.13.a, bf16[5,48,128]{2,1,0:T(8,128)(2,1)S(1)} %collective-permute-done.14.b, ...), custom_call_target="tpu_custom_call" | custom-call | tf_op jit(solution)/shard_map/pallas_call | solution.py:458
  (12 shorter events, 0.1 us)
Async XLA Ops:
  0.6 2.2 %collective-permute-start = (bf16[48,128]{1,0:T(8,128)(2,1)}, bf16[48,128]{1,0:T(8,128)(2,1)S(1)}, u32[]{:S(2)}, u32[]{:S(2)}) collective-permute-start(bf16[48,128]{1,0:T(8,128)(2,1)} %param.7), channel_id=1, source_target_pairs={{0,1},{1,0},{2,3},{3,2},{4,5},{5,4},{6,7},{7,6},{8,9},{9,8},{10,11... | collective-permute-start | bytes 36872 | tf_op jit(solution)/shard_map/ppermute | solution.py:423
  0.7 3.4 %collective-permute-start.2 = (bf16[48,128]{1,0:T(8,128)(2,1)}, bf16[48,128]{1,0:T(8,128)(2,1)S(1)}, u32[]{:S(2)}, u32[]{:S(2)}) collective-permute-start(bf16[48,128]{1,0:T(8,128)(2,1)} %param.7), channel_id=1, source_target_pairs={{0,3},{1,2},{2,1},{3,0},{4,7},{5,6},{6,5},{7,4},{8,11},{9,10},{10,... | collective-permute-start | bytes 36872 | tf_op jit(solution)/shard_map/ppermute | solution.py:423
  2.4 3.9 %collective-permute-start.1 = (bf16[48,128]{1,0:T(8,128)(2,1)}, bf16[48,128]{1,0:T(8,128)(2,1)S(1)}, u32[]{:S(2)}, u32[]{:S(2)}) collective-permute-start(bf16[48,128]{1,0:T(8,128)(2,1)} %param.7), channel_id=1, source_target_pairs={{0,2},{1,3},{2,0},{3,1},{4,6},{5,7},{6,4},{7,5},{8,10},{9,11},{10,... | collective-permute-start | bytes 36872 | tf_op jit(solution)/shard_map/ppermute | solution.py:423
  7.0 8.3 %collective-permute-start.5 = (bf16[4,48,128]{2,1,0:T(8,128)(2,1)S(1)}, bf16[4,48,128]{2,1,0:T(8,128)(2,1)}, u32[]{:S(2)}, u32[]{:S(2)}) collective-permute-start(bf16[4,48,128]{2,1,0:T(8,128)(2,1)S(1)} %shard_map.102.quad), channel_id=1, source_target_pairs={{0,12},{1,13},{2,14},{3,15},{4,8},{5,9},{6,10},{7,11},{8,4},{9,5},... | collective-permute-start | bytes 147464 | tf_op jit(solution)/shard_map/ppermute | solution.py:423
  11.1 5.7 %collective-permute-start.4 = (bf16[4,48,128]{2,1,0:T(8,128)(2,1)S(1)}, bf16[4,48,128]{2,1,0:T(8,128)(2,1)}, u32[]{:S(2)}, u32[]{:S(2)}) collective-permute-start(bf16[4,48,128]{2,1,0:T(8,128)(2,1)S(1)} %shard_map.102.quad), channel_id=1, source_target_pairs={{0,8},{1,9},{2,10},{3,11},{4,12},{5,13},{6,14},{7,15},{8,0},{9,1},... | collective-permute-start | bytes 147464 | tf_op jit(solution)/shard_map/ppermute | solution.py:423
  11.2 5.7 %collective-permute-start.3 = (bf16[4,48,128]{2,1,0:T(8,128)(2,1)S(1)}, bf16[4,48,128]{2,1,0:T(8,128)(2,1)}, u32[]{:S(2)}, u32[]{:S(2)}) collective-permute-start(bf16[4,48,128]{2,1,0:T(8,128)(2,1)S(1)} %shard_map.102.quad), channel_id=1, source_target_pairs={{0,4},{1,5},{2,6},{3,7},{4,0},{5,1},{6,2},{7,3},{8,12},{9,13},{10,... | collective-permute-start | bytes 147464 | tf_op jit(solution)/shard_map/ppermute | solution.py:423
  13.1 3.8 %copy-start.6 = (s32[2]{0:T(128)S(1)}, s32[2]{0:T(128)}, u32[]{:S(2)}) copy-start(s32[2]{0:T(128)} %param.10) | copy-start | bytes 28
  13.1 3.8 %copy-start.5 = (f32[48]{0:T(128)S(1)}, f32[48]{0:T(128)}, u32[]{:S(2)}) copy-start(f32[48]{0:T(128)} %param.9) | copy-start | bytes 580
  13.1 3.9 %copy-start.2 = (bf16[1,1,48,128,128]{4,3,2,1,0:T(8,128)(2,1)S(1)}, bf16[1,1,48,128,128]{4,3,2,1,0:T(8,128)(2,1)}, u32[]{:S(2)}) copy-start(bf16[1,1,48,128,128]{4,3,2,1,0:T(8,128)(2,1)} %param.12) | copy-start | bytes 4718596
  13.1 3.9 %copy-start.3 = (bf16[2,144,512]{2,1,0:T(8,128)(2,1)S(1)}, bf16[2,144,512]{2,1,0:T(8,128)(2,1)}, u32[]{:S(2)}) copy-start(bf16[2,144,512]{2,1,0:T(8,128)(2,1)} %constant.2.clone.repeat) | copy-start | bytes 884740
  13.1 3.9 %copy-start.4 = (s32[128,2]{0,1:T(2,128)S(1)}, s32[128,2]{0,1:T(2,128)}, u32[]{:S(2)}) copy-start(s32[128,2]{0,1:T(2,128)} %param.11) | copy-start | bytes 3076
  33.1 1.7 %collective-permute-start.6 = (f32[12,48,128]{2,1,0:T(8,128)S(1)}, f32[12,48,128]{2,1,0:T(8,128)S(1)}, u32[]{:S(2)}, u32[]{:S(2)}) collective-permute-start(f32[12,48,128]{2,1,0:T(8,128)S(1)} %get-tuple-element.22), channel_id=1, source_target_pairs={{0,1},{1,0},{2,3},{3,2},{4,5},{5,4},{6,7},{7,6},{8,9},{9,8},{10,11... | collective-permute-start | bytes 884744 | tf_op jit(solution)/shard_map/ppermute | solution.py:423
  34.8 5.6 %collective-permute-start.7 = (bf16[6,48,128]{2,1,0:T(8,128)(2,1)S(1)}, bf16[6,48,128]{2,1,0:T(8,128)(2,1)S(1)}, u32[]{:S(2)}, u32[]{:S(2)}) collective-permute-start(bf16[6,48,128]{2,1,0:T(8,128)(2,1)S(1)} %get-tuple-element.24), channel_id=1, source_target_pairs={{0,4},{1,5},{2,6},{3,7},{4,0},{5,1},{6,2},{7,3},{8,12},{9,13},{10,... | collective-permute-start | bytes 221192 | tf_op jit(solution)/shard_map/ppermute | solution.py:423
  34.9 7.3 %collective-permute-start.8 = (bf16[6,48,128]{2,1,0:T(8,128)(2,1)S(1)}, bf16[6,48,128]{2,1,0:T(8,128)(2,1)S(1)}, u32[]{:S(2)}, u32[]{:S(2)}) collective-permute-start(bf16[6,48,128]{2,1,0:T(8,128)(2,1)S(1)} %get-tuple-element.25), channel_id=1, source_target_pairs={{0,8},{1,9},{2,10},{3,11},{4,12},{5,13},{6,14},{7,15},{8,0},{9,1},... | collective-permute-start | bytes 221192 | tf_op jit(solution)/shard_map/ppermute | solution.py:423
  38.0 5.6 %collective-permute-start.9 = (bf16[6,48,128]{2,1,0:T(8,128)(2,1)S(1)}, bf16[6,48,128]{2,1,0:T(8,128)(2,1)S(1)}, u32[]{:S(2)}, u32[]{:S(2)}) collective-permute-start(bf16[6,48,128]{2,1,0:T(8,128)(2,1)S(1)} %get-tuple-element.26), channel_id=1, source_target_pairs={{0,12},{1,13},{2,14},{3,15},{4,8},{5,9},{6,10},{7,11},{8,4},{9,5},... | collective-permute-start | bytes 221192 | tf_op jit(solution)/shard_map/ppermute | solution.py:423
  43.7 1.4 %copy-start = (bf16[48,128,128]{2,1,0:T(8,128)(2,1)S(1)}, bf16[48,128,128]{2,1,0:T(8,128)(2,1)}, u32[]{:S(2)}) copy-start(bf16[48,128,128]{2,1,0:T(8,128)(2,1)} %shard_map.105.pair.pair_before) | copy-start | bytes 4718596
  45.1 6.2 %collective-permute-start.12 = (bf16[5,48,128]{2,1,0:T(8,128)(2,1)S(1)}, bf16[5,48,128]{2,1,0:T(8,128)(2,1)S(1)}, u32[]{:S(2)}, u32[]{:S(2)}) collective-permute-start(bf16[5,48,128]{2,1,0:T(8,128)(2,1)S(1)} %get-tuple-element.28), channel_id=1, source_target_pairs={{0,18},{1,19},{2,16},{3,17},{4,22},{5,23},{6,20},{7,21},{8,26},{9,... | collective-permute-start | bytes 184328 | tf_op jit(solution)/shard_map/ppermute | solution.py:423
  47.1 4.2 %collective-permute-start.10 = (bf16[5,48,128]{2,1,0:T(8,128)(2,1)S(1)}, bf16[5,48,128]{2,1,0:T(8,128)(2,1)S(1)}, u32[]{:S(2)}, u32[]{:S(2)}) collective-permute-start(bf16[5,48,128]{2,1,0:T(8,128)(2,1)S(1)} %get-tuple-element.28), channel_id=1, source_target_pairs={{0,2},{1,3},{2,0},{3,1},{4,6},{5,7},{6,4},{7,5},{8,10},{9,11},{10,... | collective-permute-start | bytes 184328 | tf_op jit(solution)/shard_map/ppermute | solution.py:423
  47.7 5.7 %collective-permute-start.11 = (bf16[5,48,128]{2,1,0:T(8,128)(2,1)S(1)}, bf16[5,48,128]{2,1,0:T(8,128)(2,1)S(1)}, u32[]{:S(2)}, u32[]{:S(2)}) collective-permute-start(bf16[5,48,128]{2,1,0:T(8,128)(2,1)S(1)} %get-tuple-element.27.after.keep), channel_id=1, source_target_pairs={{0,16},{1,17},{2,18},{3,19},{4,20},{5,21},{6,22},{7,23},{8,24},{9,... | collective-permute-start | bytes 184328 | tf_op jit(solution)/shard_map/ppermute | solution.py:423
  53.5 1.4 %copy-start.1 = (bf16[48,128,128]{2,1,0:T(8,128)(2,1)S(1)}, bf16[48,128,128]{2,1,0:T(8,128)(2,1)}, u32[]{:S(2)}) copy-start(bf16[48,128,128]{2,1,0:T(8,128)(2,1)} %shard_map.107.pair.pair_before) | copy-start | bytes 4718596
  54.9 5.8 %collective-permute-start.15 = (bf16[5,48,128]{2,1,0:T(8,128)(2,1)S(1)}, bf16[5,48,128]{2,1,0:T(8,128)(2,1)S(1)}, u32[]{:S(2)}, u32[]{:S(2)}) collective-permute-start(bf16[5,48,128]{2,1,0:T(8,128)(2,1)S(1)} %shard_map.108.after.keep), channel_id=1, source_target_pairs={{0,96},{1,97},{2,98},{3,99},{4,100},{5,101},{6,102},{7,103},{8,104... | collective-permute-start | bytes 184328 | tf_op jit(solution)/shard_map/ppermute | solution.py:423
  58.0 5.7 %collective-permute-start.14 = (bf16[5,48,128]{2,1,0:T(8,128)(2,1)S(1)}, bf16[5,48,128]{2,1,0:T(8,128)(2,1)S(1)}, u32[]{:S(2)}, u32[]{:S(2)}) collective-permute-start(bf16[5,48,128]{2,1,0:T(8,128)(2,1)S(1)} %shard_map.108.after.keep), channel_id=1, source_target_pairs={{0,64},{1,65},{2,66},{3,67},{4,68},{5,69},{6,70},{7,71},{8,72},{9,... | collective-permute-start | bytes 184328 | tf_op jit(solution)/shard_map/ppermute | solution.py:423
  60.1 4.2 %collective-permute-start.13 = (bf16[5,48,128]{2,1,0:T(8,128)(2,1)S(1)}, bf16[5,48,128]{2,1,0:T(8,128)(2,1)S(1)}, u32[]{:S(2)}, u32[]{:S(2)}) collective-permute-start(bf16[5,48,128]{2,1,0:T(8,128)(2,1)S(1)} %shard_map.108.after.keep), channel_id=1, source_target_pairs={{0,32},{1,33},{2,34},{3,35},{4,36},{5,37},{6,38},{7,39},{8,40},{9,... | collective-permute-start | bytes 184328 | tf_op jit(solution)/shard_map/ppermute | solution.py:423

commit v6 on v5

--- a/solution.py
+++ b/solution.py
@@ -270,10 +270,12 @@
 
 
 def fold_kernel(
-    first, count, meta, around, weight, bias, pair_before, after, pair_hbm,
+    first, count, meta, around, weight, bias, pair_before, after, pair_hbm, token,
     table_i, table_j, stage32, stage, sems,
 ):
     tile_i, tile_j, rate_r, rate_c = meta[0], meta[1], meta[2], meta[3]
+    if token is not None:
+        token[...] = jnp.zeros_like(token)
 
     @pl.when(tile_i > tile_j)
     def two_triangles():
@@ -359,11 +361,16 @@
 
 def fold(which, meta, around, weight, bias, pair, after):
     first, count = PIECES[which]
-    return call(
-        functools.partial(fold_kernel, first, count),
+    last = which == len(PIECES) - 1
+
+    def kernel(*refs):
+        fold_kernel(first, count, *refs[:7], *([None] if last else []), *refs[7:])
+
+    done = call(
+        kernel,
         [SMEM, VMEM, VMEM, VMEM, HBM, ANY],
-        shape((C, B, B), BF16),
-        HBM,
+        (shape((C, B, B), BF16),) + (() if last else (shape((8, B), F32),)),
+        (HBM,) + (() if last else (VMEM,)),
         [
             pltpu.VMEM((count + 2 * DMAX, C, B), BF16),
             pltpu.VMEM((count + 2 * DMAX, C, B), BF16),
@@ -373,6 +380,7 @@
         ],
         {4: 0},
     )(meta, around, weight, bias, pair, after)
+    return (done[0], None) if last else done
 
 
 def after_core_kernel(keep, got, own, to1, to2, to3):
@@ -390,7 +398,7 @@
     return (own[k].astype(F32) + a[k].astype(F32)) + (b[k].astype(F32) + c[k].astype(F32))
 
 
-def after_z_kernel(keep, a, b, c, pair, own, other):
+def after_z_kernel(keep, a, b, c, token, own, other):
     x = place_of()[1]
     own[0] = sum4(keep, a, b, c, x).astype(BF16)
     other[0] = sum4(keep, a, b, c, 1 - x).astype(BF16)
@@ -400,7 +408,7 @@
         other[1 + k] = total
 
 
-def after_x_kernel(keep, a, b, c, pair, own):
+def after_x_kernel(keep, a, b, c, token, own):
     for k in range(5):
         own[k] = sum4(keep, a, b, c, k).astype(BF16)
 
@@ -445,15 +453,15 @@
     keep, to1, to2, to3 = call(
         after_core_kernel, [VMEM, VMEM], (half,) * 4, (VMEM,) * 4
     )(keep, got)
-    pair_out = next_rows(0, pair_out, keep)
+    pair_out, token = next_rows(0, pair_out, keep)
     a, b, c = swap(to1, 0, 4), swap(to2, 0, 8), swap(to3, 0, 12)
     keep, other = call(
-        after_z_kernel, [VMEM] * 4 + [HBM], (part, part), (VMEM, VMEM)
-    )(keep, a, b, c, pair_out)
-    pair_out = next_rows(1, pair_out, keep)
+        after_z_kernel, [VMEM] * 4 + [ANY], (part, part), (VMEM, VMEM)
+    )(keep, a, b, c, token)
+    pair_out, token = next_rows(1, pair_out, keep)
     a, b, c = swap(other, 0, 2), swap(keep, 1, 0), swap(other, 1, 2)
-    keep = call(after_x_kernel, [VMEM] * 4 + [HBM], part, VMEM)(keep, a, b, c, pair_out)
-    pair_out = next_rows(2, pair_out, keep)
+    keep = call(after_x_kernel, [VMEM] * 4 + [ANY], part, VMEM)(keep, a, b, c, token)
+    pair_out, token = next_rows(2, pair_out, keep)
     a, b, c = swap(keep, 2, 0), swap(keep, 4, 0), swap(keep, 6, 0)
     grad_embed, grad_weight, grad_bias = call(
         after_y_kernel,

time: 65.3 us -> 62.1 us (0.951)
  local copies, waits for them, and re-layouts: 6.84 us -> 4.02 us
  starting transfers between devices: 22.2 us -> 21.3 us
    unnamed x15 -> x11, local copies, waits for them, and re-layouts: 5.01 us -> 2.2 us
    ppermute x16, starting transfers between devices: 22.2 us -> 21.3 us  [swap(): return lax.ppermute(value, ('fold', 'col'), route)]
  transfers between devices with their start and end apart: 16 -> 16, of which waited for: 11 -> 12; matrix products, arithmetic and copies ran while one was open for 5% -> 5% of each run, Pallas kernels for 3% -> 3%
where the time goes in v6:
time: 62.1 us; the launch traced here: 61.9 us
  starting transfers between devices  21.3 us (34%)
  Pallas kernels  18.9 us (30%)
  waiting for transfers between devices  16.9 us (27%)
  local copies, waits for them, and re-layouts  4.02 us (6%)
  between operations  0.79 us (1%)
    ppermute x16, starting transfers between devices, swap(): return lax.ppermute(value, ('fold', 'col'), route)  21.3 us
    ppermute x16, waiting for transfers between devices, swap(): return lax.ppermute(value, ('fold', 'col'), route)  16.9 us
    pallas_call x1, Pallas kernels, gradients(): call(gradient_kernel, [SMEM, SMEM] + [VMEM] * 9, (shape((12, C, B), F32),...  16 us
    unnamed x11, local copies, waits for them, and re-layouts  2.2 us
    pallas_call x3, Pallas kernels, fold(): call(kernel, [SMEM, VMEM, VMEM, VMEM, HBM, ANY], (shape((C, B, B), BF16),...  1.93 us
  transfers between devices with their start and end apart: 16, of which 12 were waited for; matrix products, arithmetic and copies ran while one was open for 5% of the time, Pallas kernels for 3%

profile of v6, /device:TPU:0, one launch (start us, length us, event | category | flops | bytes accessed | tf_op | source)
XLA Modules:
  0.0 61.9 jit_solution(486170487773578103)
XLA Ops:
  0.6 0.1 collective-permute-start
  0.7 1.7 %collective-permute-start.2 = (bf16[48,128]{1,0:T(8,128)(2,1)}, bf16[48,128]{1,0:T(8,128)(2,1)S(1)}, u32[]{:S(2)}, u32[]{:S(2)}) collective-permute-start(bf16[48,128]{1,0:T(8,128)(2,1)} %param.7), channel_id=1, source_target_pairs={{0,3},{1,2},{2,1},{3,0},{4,7},{5,6},{6,5},{7,4},{8,11},{9,10},{10,... | collective-permute-start | bytes 36872 | tf_op jit(solution)/shard_map/ppermute | solution.py:431
  2.4 0.5 collective-permute-start.1
  2.9 0.0 collective-permute-done.core
  2.9 1.3 %collective-permute-done.2.both = bf16[48,128]{1,0:T(8,128)(2,1)S(1)} collective-permute-done((bf16[48,128]{1,0:T(8,128)(2,1)}, bf16[48,128]{1,0:T(8,128)(2,1)S(1)}, u32[]{:S(2)}, u32[]{:S(2)}) %collective-permute-start.2) | collective-permute-done | bytes 12320 | tf_op jit(solution)/shard_map/ppermute | solution.py:431
  4.1 2.2 %collective-permute-done.1.xlo = bf16[48,128]{1,0:T(8,128)(2,1)S(1)} collective-permute-done((bf16[48,128]{1,0:T(8,128)(2,1)}, bf16[48,128]{1,0:T(8,128)(2,1)S(1)}, u32[]{:S(2)}, u32[]{:S(2)}) %collective-permute-start.1) | collective-permute-done | bytes 12320 | tf_op jit(solution)/shard_map/ppermute | solution.py:431
  6.3 0.7 %broadcast_in_dim.9.own = bf16[2,48,128]{2,1,0:T(8,128)(2,1)S(1)} broadcast(bf16[48,128]{1,0:T(8,128)(2,1)} %param.7), dimensions={1,2} | broadcast | bytes 36864 | tf_op jit(solution)/shard_map/broadcast_in_dim | solution.py:435
  7.0 4.1 %collective-permute-start.5 = (bf16[4,48,128]{2,1,0:T(8,128)(2,1)S(1)}, bf16[4,48,128]{2,1,0:T(8,128)(2,1)}, u32[]{:S(2)}, u32[]{:S(2)}) collective-permute-start(bf16[4,48,128]{2,1,0:T(8,128)(2,1)S(1)} %shard_map.102.quad), channel_id=1, source_target_pairs={{0,12},{1,13},{2,14},{3,15},{4,8},{5,9},{6,10},{7,11},{8,4},{9,5},... | collective-permute-start | bytes 147464 | tf_op jit(solution)/shard_map/ppermute | solution.py:431
  11.1 0.0 collective-permute-start.4
  11.2 0.9 %collective-permute-start.3 = (bf16[4,48,128]{2,1,0:T(8,128)(2,1)S(1)}, bf16[4,48,128]{2,1,0:T(8,128)(2,1)}, u32[]{:S(2)}, u32[]{:S(2)}) collective-permute-start(bf16[4,48,128]{2,1,0:T(8,128)(2,1)S(1)} %shard_map.102.quad), channel_id=1, source_target_pairs={{0,4},{1,5},{2,6},{3,7},{4,0},{5,1},{6,2},{7,3},{8,12},{9,13},{10,... | collective-permute-start | bytes 147464 | tf_op jit(solution)/shard_map/ppermute | solution.py:431
  12.1 1.0 %copy.18.weight.refs_2_ = bf16[48,432]{1,0:T(8,128)(2,1)S(1)} copy(bf16[48,432]{0,1:T(8,128)(2,1)} %bitcast.14) | data formatting | bytes 82944 | tf_op jit(solution)/shard_map/reshape | solution.py:442
  13.1 0.0 copy-start.4
  13.1 0.0 copy-start.3
  13.1 0.0 copy-start
  13.1 0.0 copy-start.1
  13.1 0.0 copy-start.2
  13.1 2.2 %copy.17 = bf16[1,1,48,128,128]{3,2,4,1,0:T(8,128)(2,1)S(1)} copy(bf16[1,1,48,128,128]{4,3,2,1,0:T(8,128)(2,1)} %param.12) | data formatting | bytes 3145728 | tf_op args[5]
  15.3 0.0 collective-permute-done.5.z3
  15.3 1.5 %collective-permute-done.4.z2 = bf16[4,48,128]{2,1,0:T(8,128)(2,1)} collective-permute-done((bf16[4,48,128]{2,1,0:T(8,128)(2,1)S(1)}, bf16[4,48,128]{2,1,0:T(8,128)(2,1)}, u32[]{:S(2)}, u32[]{:S(2)}) %collective-permute-start.4) | collective-permute-done | bytes 49184 | tf_op jit(solution)/shard_map/ppermute | solution.py:431
  16.8 0.0 collective-permute-done.3.z1
  16.9 0.1 broadcast_in_dim.8.dilation
  16.9 0.0 copy-done.3
  16.9 0.1 broadcast_in_dim.10.bias.refs_3_
  17.0 16.0 %shard_map.103 = (f32[12,48,128]{2,1,0:T(8,128)S(1)}, f32[12,48,128]{2,1,0:T(8,128)S(1)}, f32[6,48,128]{2,1,0:T(8,128)S(1)}, s32[4]{0:T(128)S(1)}, bf16[48,128,128]{2,1,0:T(8,128)(2,1)}) custom-call(s32[2,128]{1,0:T(2,128)S(1)} %bitcast.12, s32[2,128]{1,0:T(2,128)S(1)} %broadcast_in_dim.8.dilation, bf16[4,48,128]{2,1,0:T(8,128)(2,1)S(1)} %shard_map.102.quad, ...), custom_call_target="tpu_custom_call" | custom-call | tf_op jit(solution)/shard_map/pallas_call | solution.py:334
  33.0 0.1 collective-permute-start.6
  33.1 1.6 %collective-permute-done.6.got = f32[12,48,128]{2,1,0:T(8,128)S(1)} collective-permute-done((f32[12,48,128]{2,1,0:T(8,128)S(1)}, f32[12,48,128]{2,1,0:T(8,128)S(1)}, u32[]{:S(2)}, u32[]{:S(2)}) %collective-permute-start.6) | collective-permute-done | bytes 294944 | tf_op jit(solution)/shard_map/ppermute | solution.py:431
  34.7 0.1 collective-permute-start.7
  34.8 3.1 %collective-permute-start.8 = (bf16[6,48,128]{2,1,0:T(8,128)(2,1)S(1)}, bf16[6,48,128]{2,1,0:T(8,128)(2,1)S(1)}, u32[]{:S(2)}, u32[]{:S(2)}) collective-permute-start(bf16[6,48,128]{2,1,0:T(8,128)(2,1)S(1)} %get-tuple-element.30), channel_id=1, source_target_pairs={{0,8},{1,9},{2,10},{3,11},{4,12},{5,13},{6,14},{7,15},{8,0},{9,1},... | collective-permute-start | bytes 221192 | tf_op jit(solution)/shard_map/ppermute | solution.py:431
  37.9 1.6 %collective-permute-start.9 = (bf16[6,48,128]{2,1,0:T(8,128)(2,1)S(1)}, bf16[6,48,128]{2,1,0:T(8,128)(2,1)S(1)}, u32[]{:S(2)}, u32[]{:S(2)}) collective-permute-start(bf16[6,48,128]{2,1,0:T(8,128)(2,1)S(1)} %get-tuple-element.31), channel_id=1, source_target_pairs={{0,12},{1,13},{2,14},{3,15},{4,8},{5,9},{6,10},{7,11},{8,4},{9,5},... | collective-permute-start | bytes 221192 | tf_op jit(solution)/shard_map/ppermute | solution.py:431
  39.5 0.8 %shard_map.105 = (bf16[48,128,128]{2,1,0:T(8,128)(2,1)}, f32[8,128]{1,0:T(8,128)S(1)}) custom-call(s32[4]{0:T(128)S(1)} %get-tuple-element.22.refs_0_, f32[6,48,128]{2,1,0:T(8,128)S(1)} %get-tuple-element.23.refs_1_, bf16[48,432]{1,0:T(8,128)(2,1)S(1)} %copy.18.weight.refs_2_, ...), custom_call_target="tpu_custom_call", output_to_operand_aliasing={{0}: (4, {})} | custom-call | tf_op jit(solution)/shard_map/pallas_call | solution.py:369
  40.3 0.0 collective-permute-done.7.a
  40.3 1.5 %collective-permute-done.8.b = bf16[6,48,128]{2,1,0:T(8,128)(2,1)S(1)} collective-permute-done((bf16[6,48,128]{2,1,0:T(8,128)(2,1)S(1)}, bf16[6,48,128]{2,1,0:T(8,128)(2,1)S(1)}, u32[]{:S(2)}, u32[]{:S(2)}) %collective-permute-start.8) | collective-permute-done | bytes 73760 | tf_op jit(solution)/shard_map/ppermute | solution.py:431
  41.8 1.7 %collective-permute-done.9.c = bf16[6,48,128]{2,1,0:T(8,128)(2,1)S(1)} collective-permute-done((bf16[6,48,128]{2,1,0:T(8,128)(2,1)S(1)}, bf16[6,48,128]{2,1,0:T(8,128)(2,1)S(1)}, u32[]{:S(2)}, u32[]{:S(2)}) %collective-permute-start.9) | collective-permute-done | bytes 73760 | tf_op jit(solution)/shard_map/ppermute | solution.py:431
  43.5 3.3 %collective-permute-start.12 = (bf16[5,48,128]{2,1,0:T(8,128)(2,1)S(1)}, bf16[5,48,128]{2,1,0:T(8,128)(2,1)S(1)}, u32[]{:S(2)}, u32[]{:S(2)}) collective-permute-start(bf16[5,48,128]{2,1,0:T(8,128)(2,1)S(1)} %get-tuple-element.35), channel_id=1, source_target_pairs={{0,18},{1,19},{2,16},{3,17},{4,22},{5,23},{6,20},{7,21},{8,26},{9,... | collective-permute-start | bytes 184328 | tf_op jit(solution)/shard_map/ppermute | solution.py:431
  46.9 0.0 collective-permute-start.10
  46.9 1.6 %collective-permute-start.11 = (bf16[5,48,128]{2,1,0:T(8,128)(2,1)S(1)}, bf16[5,48,128]{2,1,0:T(8,128)(2,1)S(1)}, u32[]{:S(2)}, u32[]{:S(2)}) collective-permute-start(bf16[5,48,128]{2,1,0:T(8,128)(2,1)S(1)} %get-tuple-element.33.refs_5_.keep), channel_id=1, source_target_pairs={{0,16},{1,17},{2,18},{3,19},{4,20},{5,21},{6,22},{7,23},{8,24},{9,... | collective-permute-start | bytes 184328 | tf_op jit(solution)/shard_map/ppermute | solution.py:431
  48.4 0.6 shard_map.107
  49.0 0.7 %collective-permute-done.12.c = bf16[5,48,128]{2,1,0:T(8,128)(2,1)S(1)} collective-permute-done((bf16[5,48,128]{2,1,0:T(8,128)(2,1)S(1)}, bf16[5,48,128]{2,1,0:T(8,128)(2,1)S(1)}, u32[]{:S(2)}, u32[]{:S(2)}) %collective-permute-start.12) | collective-permute-done | bytes 61472 | tf_op jit(solution)/shard_map/ppermute | solution.py:431
  49.7 1.4 %collective-permute-done.10.a = bf16[5,48,128]{2,1,0:T(8,128)(2,1)S(1)} collective-permute-done((bf16[5,48,128]{2,1,0:T(8,128)(2,1)S(1)}, bf16[5,48,128]{2,1,0:T(8,128)(2,1)S(1)}, u32[]{:S(2)}, u32[]{:S(2)}) %collective-permute-start.10) | collective-permute-done | bytes 61472 | tf_op jit(solution)/shard_map/ppermute | solution.py:431
  51.1 1.5 %collective-permute-done.11.b = bf16[5,48,128]{2,1,0:T(8,128)(2,1)S(1)} collective-permute-done((bf16[5,48,128]{2,1,0:T(8,128)(2,1)S(1)}, bf16[5,48,128]{2,1,0:T(8,128)(2,1)S(1)}, u32[]{:S(2)}, u32[]{:S(2)}) %collective-permute-start.11) | collective-permute-done | bytes 61472 | tf_op jit(solution)/shard_map/ppermute | solution.py:431
  52.6 2.5 %collective-permute-start.15 = (bf16[5,48,128]{2,1,0:T(8,128)(2,1)S(1)}, bf16[5,48,128]{2,1,0:T(8,128)(2,1)S(1)}, u32[]{:S(2)}, u32[]{:S(2)}) collective-permute-start(bf16[5,48,128]{2,1,0:T(8,128)(2,1)S(1)} %shard_map.108.refs_5_.keep), channel_id=1, source_target_pairs={{0,96},{1,97},{2,98},{3,99},{4,100},{5,101},{6,102},{7,103},{8,104... | collective-permute-start | bytes 184328 | tf_op jit(solution)/shard_map/ppermute | solution.py:431
  55.2 1.7 %collective-permute-start.14 = (bf16[5,48,128]{2,1,0:T(8,128)(2,1)S(1)}, bf16[5,48,128]{2,1,0:T(8,128)(2,1)S(1)}, u32[]{:S(2)}, u32[]{:S(2)}) collective-permute-start(bf16[5,48,128]{2,1,0:T(8,128)(2,1)S(1)} %shard_map.108.refs_5_.keep), channel_id=1, source_target_pairs={{0,64},{1,65},{2,66},{3,67},{4,68},{5,69},{6,70},{7,71},{8,72},{9,... | collective-permute-start | bytes 184328 | tf_op jit(solution)/shard_map/ppermute | solution.py:431
  56.9 0.0 collective-permute-start.13
  56.9 0.6 shard_map.109
  57.4 0.7 %collective-permute-done.15.c = bf16[5,48,128]{2,1,0:T(8,128)(2,1)S(1)} collective-permute-done((bf16[5,48,128]{2,1,0:T(8,128)(2,1)S(1)}, bf16[5,48,128]{2,1,0:T(8,128)(2,1)S(1)}, u32[]{:S(2)}, u32[]{:S(2)}) %collective-permute-start.15) | collective-permute-done | bytes 61472 | tf_op jit(solution)/shard_map/ppermute | solution.py:431
  58.1 2.7 %collective-permute-done.14.b = bf16[5,48,128]{2,1,0:T(8,128)(2,1)S(1)} collective-permute-done((bf16[5,48,128]{2,1,0:T(8,128)(2,1)S(1)}, bf16[5,48,128]{2,1,0:T(8,128)(2,1)S(1)}, u32[]{:S(2)}, u32[]{:S(2)}) %collective-permute-start.14) | collective-permute-done | bytes 61472 | tf_op jit(solution)/shard_map/ppermute | solution.py:431
  60.9 0.2 collective-permute-done.13.a
  61.1 0.8 %shard_map.110 = (f32[48,128]{1,0:T(8,128)}, f32[9,48,48]{2,1,0:T(8,128)}, f32[1,48]{1,0:T(1,128)}) custom-call(bf16[5,48,128]{2,1,0:T(8,128)(2,1)S(1)} %shard_map.108.refs_5_.keep, bf16[5,48,128]{2,1,0:T(8,128)(2,1)S(1)} %collective-permute-done.13.a, bf16[5,48,128]{2,1,0:T(8,128)(2,1)S(1)} %collective-permute-done.14.b, ...), custom_call_target="tpu_custom_call" | custom-call | tf_op jit(solution)/shard_map/pallas_call | solution.py:466
  (8 shorter events, 0.1 us)
Async XLA Ops:
  0.6 2.2 %collective-permute-start = (bf16[48,128]{1,0:T(8,128)(2,1)}, bf16[48,128]{1,0:T(8,128)(2,1)S(1)}, u32[]{:S(2)}, u32[]{:S(2)}) collective-permute-start(bf16[48,128]{1,0:T(8,128)(2,1)} %param.7), channel_id=1, source_target_pairs={{0,1},{1,0},{2,3},{3,2},{4,5},{5,4},{6,7},{7,6},{8,9},{9,8},{10,11... | collective-permute-start | bytes 36872 | tf_op jit(solution)/shard_map/ppermute | solution.py:431
  0.7 3.4 %collective-permute-start.2 = (bf16[48,128]{1,0:T(8,128)(2,1)}, bf16[48,128]{1,0:T(8,128)(2,1)S(1)}, u32[]{:S(2)}, u32[]{:S(2)}) collective-permute-start(bf16[48,128]{1,0:T(8,128)(2,1)} %param.7), channel_id=1, source_target_pairs={{0,3},{1,2},{2,1},{3,0},{4,7},{5,6},{6,5},{7,4},{8,11},{9,10},{10,... | collective-permute-start | bytes 36872 | tf_op jit(solution)/shard_map/ppermute | solution.py:431
  2.4 3.9 %collective-permute-start.1 = (bf16[48,128]{1,0:T(8,128)(2,1)}, bf16[48,128]{1,0:T(8,128)(2,1)S(1)}, u32[]{:S(2)}, u32[]{:S(2)}) collective-permute-start(bf16[48,128]{1,0:T(8,128)(2,1)} %param.7), channel_id=1, source_target_pairs={{0,2},{1,3},{2,0},{3,1},{4,6},{5,7},{6,4},{7,5},{8,10},{9,11},{10,... | collective-permute-start | bytes 36872 | tf_op jit(solution)/shard_map/ppermute | solution.py:431
  7.0 8.3 %collective-permute-start.5 = (bf16[4,48,128]{2,1,0:T(8,128)(2,1)S(1)}, bf16[4,48,128]{2,1,0:T(8,128)(2,1)}, u32[]{:S(2)}, u32[]{:S(2)}) collective-permute-start(bf16[4,48,128]{2,1,0:T(8,128)(2,1)S(1)} %shard_map.102.quad), channel_id=1, source_target_pairs={{0,12},{1,13},{2,14},{3,15},{4,8},{5,9},{6,10},{7,11},{8,4},{9,5},... | collective-permute-start | bytes 147464 | tf_op jit(solution)/shard_map/ppermute | solution.py:431
  11.1 5.7 %collective-permute-start.4 = (bf16[4,48,128]{2,1,0:T(8,128)(2,1)S(1)}, bf16[4,48,128]{2,1,0:T(8,128)(2,1)}, u32[]{:S(2)}, u32[]{:S(2)}) collective-permute-start(bf16[4,48,128]{2,1,0:T(8,128)(2,1)S(1)} %shard_map.102.quad), channel_id=1, source_target_pairs={{0,8},{1,9},{2,10},{3,11},{4,12},{5,13},{6,14},{7,15},{8,0},{9,1},... | collective-permute-start | bytes 147464 | tf_op jit(solution)/shard_map/ppermute | solution.py:431
  11.2 5.7 %collective-permute-start.3 = (bf16[4,48,128]{2,1,0:T(8,128)(2,1)S(1)}, bf16[4,48,128]{2,1,0:T(8,128)(2,1)}, u32[]{:S(2)}, u32[]{:S(2)}) collective-permute-start(bf16[4,48,128]{2,1,0:T(8,128)(2,1)S(1)} %shard_map.102.quad), channel_id=1, source_target_pairs={{0,4},{1,5},{2,6},{3,7},{4,0},{5,1},{6,2},{7,3},{8,12},{9,13},{10,... | collective-permute-start | bytes 147464 | tf_op jit(solution)/shard_map/ppermute | solution.py:431
  13.1 3.8 %copy-start.4 = (s32[2]{0:T(128)S(1)}, s32[2]{0:T(128)}, u32[]{:S(2)}) copy-start(s32[2]{0:T(128)} %param.10) | copy-start | bytes 28
  13.1 3.8 %copy-start.3 = (f32[48]{0:T(128)S(1)}, f32[48]{0:T(128)}, u32[]{:S(2)}) copy-start(f32[48]{0:T(128)} %param.9) | copy-start | bytes 580
  13.1 3.9 %copy-start = (bf16[1,1,48,128,128]{4,3,2,1,0:T(8,128)(2,1)S(1)}, bf16[1,1,48,128,128]{4,3,2,1,0:T(8,128)(2,1)}, u32[]{:S(2)}) copy-start(bf16[1,1,48,128,128]{4,3,2,1,0:T(8,128)(2,1)} %param.12) | copy-start | bytes 4718596
  13.1 3.9 %copy-start.1 = (bf16[2,144,512]{2,1,0:T(8,128)(2,1)S(1)}, bf16[2,144,512]{2,1,0:T(8,128)(2,1)}, u32[]{:S(2)}) copy-start(bf16[2,144,512]{2,1,0:T(8,128)(2,1)} %constant.2.clone.repeat) | copy-start | bytes 884740
  13.1 3.9 %copy-start.2 = (s32[128,2]{0,1:T(2,128)S(1)}, s32[128,2]{0,1:T(2,128)}, u32[]{:S(2)}) copy-start(s32[128,2]{0,1:T(2,128)} %param.11) | copy-start | bytes 3076
  33.0 1.7 %collective-permute-start.6 = (f32[12,48,128]{2,1,0:T(8,128)S(1)}, f32[12,48,128]{2,1,0:T(8,128)S(1)}, u32[]{:S(2)}, u32[]{:S(2)}) collective-permute-start(f32[12,48,128]{2,1,0:T(8,128)S(1)} %get-tuple-element.26), channel_id=1, source_target_pairs={{0,1},{1,0},{2,3},{3,2},{4,5},{5,4},{6,7},{7,6},{8,9},{9,8},{10,11... | collective-permute-start | bytes 884744 | tf_op jit(solution)/shard_map/ppermute | solution.py:431
  34.7 5.6 %collective-permute-start.7 = (bf16[6,48,128]{2,1,0:T(8,128)(2,1)S(1)}, bf16[6,48,128]{2,1,0:T(8,128)(2,1)S(1)}, u32[]{:S(2)}, u32[]{:S(2)}) collective-permute-start(bf16[6,48,128]{2,1,0:T(8,128)(2,1)S(1)} %get-tuple-element.29), channel_id=1, source_target_pairs={{0,4},{1,5},{2,6},{3,7},{4,0},{5,1},{6,2},{7,3},{8,12},{9,13},{10,... | collective-permute-start | bytes 221192 | tf_op jit(solution)/shard_map/ppermute | solution.py:431
  34.8 7.0 %collective-permute-start.8 = (bf16[6,48,128]{2,1,0:T(8,128)(2,1)S(1)}, bf16[6,48,128]{2,1,0:T(8,128)(2,1)S(1)}, u32[]{:S(2)}, u32[]{:S(2)}) collective-permute-start(bf16[6,48,128]{2,1,0:T(8,128)(2,1)S(1)} %get-tuple-element.30), channel_id=1, source_target_pairs={{0,8},{1,9},{2,10},{3,11},{4,12},{5,13},{6,14},{7,15},{8,0},{9,1},... | collective-permute-start | bytes 221192 | tf_op jit(solution)/shard_map/ppermute | solution.py:431
  37.9 5.6 %collective-permute-start.9 = (bf16[6,48,128]{2,1,0:T(8,128)(2,1)S(1)}, bf16[6,48,128]{2,1,0:T(8,128)(2,1)S(1)}, u32[]{:S(2)}, u32[]{:S(2)}) collective-permute-start(bf16[6,48,128]{2,1,0:T(8,128)(2,1)S(1)} %get-tuple-element.31), channel_id=1, source_target_pairs={{0,12},{1,13},{2,14},{3,15},{4,8},{5,9},{6,10},{7,11},{8,4},{9,5},... | collective-permute-start | bytes 221192 | tf_op jit(solution)/shard_map/ppermute | solution.py:431
  43.5 6.2 %collective-permute-start.12 = (bf16[5,48,128]{2,1,0:T(8,128)(2,1)S(1)}, bf16[5,48,128]{2,1,0:T(8,128)(2,1)S(1)}, u32[]{:S(2)}, u32[]{:S(2)}) collective-permute-start(bf16[5,48,128]{2,1,0:T(8,128)(2,1)S(1)} %get-tuple-element.35), channel_id=1, source_target_pairs={{0,18},{1,19},{2,16},{3,17},{4,22},{5,23},{6,20},{7,21},{8,26},{9,... | collective-permute-start | bytes 184328 | tf_op jit(solution)/shard_map/ppermute | solution.py:431
  46.9 4.2 %collective-permute-start.10 = (bf16[5,48,128]{2,1,0:T(8,128)(2,1)S(1)}, bf16[5,48,128]{2,1,0:T(8,128)(2,1)S(1)}, u32[]{:S(2)}, u32[]{:S(2)}) collective-permute-start(bf16[5,48,128]{2,1,0:T(8,128)(2,1)S(1)} %get-tuple-element.35), channel_id=1, source_target_pairs={{0,2},{1,3},{2,0},{3,1},{4,6},{5,7},{6,4},{7,5},{8,10},{9,11},{10,... | collective-permute-start | bytes 184328 | tf_op jit(solution)/shard_map/ppermute | solution.py:431
  46.9 5.7 %collective-permute-start.11 = (bf16[5,48,128]{2,1,0:T(8,128)(2,1)S(1)}, bf16[5,48,128]{2,1,0:T(8,128)(2,1)S(1)}, u32[]{:S(2)}, u32[]{:S(2)}) collective-permute-start(bf16[5,48,128]{2,1,0:T(8,128)(2,1)S(1)} %get-tuple-element.33.refs_5_.keep), channel_id=1, source_target_pairs={{0,16},{1,17},{2,18},{3,19},{4,20},{5,21},{6,22},{7,23},{8,24},{9,... | collective-permute-start | bytes 184328 | tf_op jit(solution)/shard_map/ppermute | solution.py:431
  52.6 5.5 %collective-permute-start.15 = (bf16[5,48,128]{2,1,0:T(8,128)(2,1)S(1)}, bf16[5,48,128]{2,1,0:T(8,128)(2,1)S(1)}, u32[]{:S(2)}, u32[]{:S(2)}) collective-permute-start(bf16[5,48,128]{2,1,0:T(8,128)(2,1)S(1)} %shard_map.108.refs_5_.keep), channel_id=1, source_target_pairs={{0,96},{1,97},{2,98},{3,99},{4,100},{5,101},{6,102},{7,103},{8,104... | collective-permute-start | bytes 184328 | tf_op jit(solution)/shard_map/ppermute | solution.py:431
  55.2 5.7 %collective-permute-start.14 = (bf16[5,48,128]{2,1,0:T(8,128)(2,1)S(1)}, bf16[5,48,128]{2,1,0:T(8,128)(2,1)S(1)}, u32[]{:S(2)}, u32[]{:S(2)}) collective-permute-start(bf16[5,48,128]{2,1,0:T(8,128)(2,1)S(1)} %shard_map.108.refs_5_.keep), channel_id=1, source_target_pairs={{0,64},{1,65},{2,66},{3,67},{4,68},{5,69},{6,70},{7,71},{8,72},{9,... | collective-permute-start | bytes 184328 | tf_op jit(solution)/shard_map/ppermute | solution.py:431
  56.9 4.2 %collective-permute-start.13 = (bf16[5,48,128]{2,1,0:T(8,128)(2,1)S(1)}, bf16[5,48,128]{2,1,0:T(8,128)(2,1)S(1)}, u32[]{:S(2)}, u32[]{:S(2)}) collective-permute-start(bf16[5,48,128]{2,1,0:T(8,128)(2,1)S(1)} %shard_map.108.refs_5_.keep), channel_id=1, source_target_pairs={{0,32},{1,33},{2,34},{3,35},{4,36},{5,37},{6,38},{7,39},{8,40},{9,... | collective-permute-start | bytes 184328 | tf_op jit(solution)/shard_map/ppermute | solution.py:431

commit v7 on v6

--- a/solution.py
+++ b/solution.py
@@ -113,7 +113,7 @@
 
 def gradient_kernel(
     fold_map, dilation, quad, z1, z2, z3, weight, repeat, bias, cot, cols,
-    send, keep, around, meta, pair_hbm,
+    send, keep, around, pair_hbm,
     blocks, shift, minus, sums, grads, wgrad, table, rows, cot32, stage32, stage, sem,
 ):
     tile_i, tile_j, rate_r, rate_c = tile_of(fold_map, dilation)
@@ -126,8 +126,6 @@
     column = lax.broadcasted_iota(jnp.int32, (B, NK), 1)
     bias_mark = jnp.where(column == 432, 1.0, 0.0)
     grads[...] = jnp.zeros_like(grads)
-    for k, value in enumerate((tile_i, tile_j, rate_r, rate_c)):
-        meta[k] = value
     weight_wide = jnp.concatenate([weight[...].astype(F32), jnp.zeros((C, NK - 432), F32)], 1)
     empty = jnp.zeros((C, NK), F32)
 
@@ -270,10 +268,10 @@
 
 
 def fold_kernel(
-    first, count, meta, around, weight, bias, pair_before, after, pair_hbm, token,
+    first, count, fold_map, dilation, around, weight, bias, pair_before, after, pair_hbm, token,
     table_i, table_j, stage32, stage, sems,
 ):
-    tile_i, tile_j, rate_r, rate_c = meta[0], meta[1], meta[2], meta[3]
+    tile_i, tile_j, rate_r, rate_c = tile_of(fold_map, dilation)
     if token is not None:
         token[...] = jnp.zeros_like(token)
 
@@ -338,10 +336,9 @@
             shape((12, C, B), F32),
             shape((12, C, B), F32),
             shape((6, C, B), F32),
-            shape((4,), jnp.int32),
             shape((C, B, B), BF16),
         ),
-        (VMEM, VMEM, VMEM, SMEM, HBM),
+        (VMEM, VMEM, VMEM, HBM),
         [
             pltpu.VMEM((18, C, B), F32),
             pltpu.VMEM((4, B, NK), F32),
@@ -359,16 +356,16 @@
     )(fold_map, dilation, *pieces, weight, repeat_table(), bias, cot, cot_cols)
 
 
-def fold(which, meta, around, weight, bias, pair, after):
+def fold(which, fold_map, dilation, around, weight, bias, pair, after):
     first, count = PIECES[which]
     last = which == len(PIECES) - 1
 
     def kernel(*refs):
-        fold_kernel(first, count, *refs[:7], *([None] if last else []), *refs[7:])
+        fold_kernel(first, count, *refs[:8], *([None] if last else []), *refs[8:])
 
     done = call(
         kernel,
-        [SMEM, VMEM, VMEM, VMEM, HBM, ANY],
+        [SMEM, SMEM, VMEM, VMEM, VMEM, HBM, ANY],
         (shape((C, B, B), BF16),) + (() if last else (shape((8, B), F32),)),
         (HBM,) + (() if last else (VMEM,)),
         [
@@ -378,8 +375,8 @@
             pltpu.VMEM((count // 16, C, 16, B), BF16),
             pltpu.SemaphoreType.DMA((count // 16,)),
         ],
-        {4: 0},
-    )(meta, around, weight, bias, pair, after)
+        {5: 0},
+    )(fold_map, dilation, around, weight, bias, pair, after)
     return (done[0], None) if last else done
 
 
@@ -441,12 +438,12 @@
     cot_cols = jnp.transpose(cot, (2, 0, 1))
     weight = jnp.transpose(conv_weight, (2, 0, 1)).reshape(C, 9 * C)
     bias = jnp.broadcast_to(conv_bias[:, None], (C, B))
-    send, keep, around, meta, pair_out = gradients(
+    send, keep, around, pair_out = gradients(
         fold_map, dilation, pieces, weight, bias, cot, cot_cols
     )
 
     def next_rows(which, pair_out, after):
-        return fold(which, meta, around, weight, bias, pair_out, after)
+        return fold(which, fold_map, dilation, around, weight, bias, pair_out, after)
 
     got = swap(send, 0, 1)
     half, part = shape((6, C, B), BF16), shape((5, C, B), BF16)

time: 62.1 us -> 61.9 us (level)
  transfers between devices with their start and end apart: 16 -> 16, of which waited for: 12 -> 11; matrix products, arithmetic and copies ran while one was open for 5% -> 5% of each run, Pallas kernels for 3% -> 3%
where the time goes in v7:
time: 61.9 us; the launch traced here: 61.3 us
  starting transfers between devices  21.1 us (34%)
  Pallas kernels  18.5 us (30%)
  waiting for transfers between devices  16.9 us (27%)
  local copies, waits for them, and re-layouts  4.02 us (6%)
  between operations  0.79 us (1%)
    ppermute x16, starting transfers between devices, swap(): return lax.ppermute(value, ('fold', 'col'), route)  21.1 us
    ppermute x16, waiting for transfers between devices, swap(): return lax.ppermute(value, ('fold', 'col'), route)  16.9 us
    pallas_call x1, Pallas kernels, gradients(): call(gradient_kernel, [SMEM, SMEM] + [VMEM] * 9, (shape((12, C, B), F32),...  15.5 us
    unnamed x11, local copies, waits for them, and re-layouts  2.2 us
    pallas_call x3, Pallas kernels, fold(): call(kernel, [SMEM, SMEM, VMEM, VMEM, VMEM, HBM, ANY], (shape((C, B, B),...  2.03 us
  transfers between devices with their start and end apart: 16, of which 11 were waited for; matrix products, arithmetic and copies ran while one was open for 5% of the time, Pallas kernels for 3%

profile of v7, /device:TPU:0, one launch (start us, length us, event | category | flops | bytes accessed | tf_op | source)
XLA Modules:
  0.0 61.3 jit_solution(15795815595394078152)
XLA Ops:
  0.6 0.1 collective-permute-start
  0.7 1.7 %collective-permute-start.2 = (bf16[48,128]{1,0:T(8,128)(2,1)}, bf16[48,128]{1,0:T(8,128)(2,1)S(1)}, u32[]{:S(2)}, u32[]{:S(2)}) collective-permute-start(bf16[48,128]{1,0:T(8,128)(2,1)} %param.7), channel_id=1, source_target_pairs={{0,3},{1,2},{2,1},{3,0},{4,7},{5,6},{6,5},{7,4},{8,11},{9,10},{10,... | collective-permute-start | bytes 36872 | tf_op jit(solution)/shard_map/ppermute | solution.py:428
  2.4 0.5 collective-permute-start.1
  2.9 0.0 collective-permute-done.core
  2.9 1.3 %collective-permute-done.2.both = bf16[48,128]{1,0:T(8,128)(2,1)S(1)} collective-permute-done((bf16[48,128]{1,0:T(8,128)(2,1)}, bf16[48,128]{1,0:T(8,128)(2,1)S(1)}, u32[]{:S(2)}, u32[]{:S(2)}) %collective-permute-start.2) | collective-permute-done | bytes 12320 | tf_op jit(solution)/shard_map/ppermute | solution.py:428
  4.1 2.2 %collective-permute-done.1.xlo = bf16[48,128]{1,0:T(8,128)(2,1)S(1)} collective-permute-done((bf16[48,128]{1,0:T(8,128)(2,1)}, bf16[48,128]{1,0:T(8,128)(2,1)S(1)}, u32[]{:S(2)}, u32[]{:S(2)}) %collective-permute-start.1) | collective-permute-done | bytes 12320 | tf_op jit(solution)/shard_map/ppermute | solution.py:428
  6.3 0.7 %broadcast_in_dim.9.own = bf16[2,48,128]{2,1,0:T(8,128)(2,1)S(1)} broadcast(bf16[48,128]{1,0:T(8,128)(2,1)} %param.7), dimensions={1,2} | broadcast | bytes 36864 | tf_op jit(solution)/shard_map/broadcast_in_dim | solution.py:432
  7.0 4.1 %collective-permute-start.5 = (bf16[4,48,128]{2,1,0:T(8,128)(2,1)S(1)}, bf16[4,48,128]{2,1,0:T(8,128)(2,1)}, u32[]{:S(2)}, u32[]{:S(2)}) collective-permute-start(bf16[4,48,128]{2,1,0:T(8,128)(2,1)S(1)} %shard_map.102.quad), channel_id=1, source_target_pairs={{0,12},{1,13},{2,14},{3,15},{4,8},{5,9},{6,10},{7,11},{8,4},{9,5},... | collective-permute-start | bytes 147464 | tf_op jit(solution)/shard_map/ppermute | solution.py:428
  11.1 0.0 collective-permute-start.4
  11.2 0.9 %collective-permute-start.3 = (bf16[4,48,128]{2,1,0:T(8,128)(2,1)S(1)}, bf16[4,48,128]{2,1,0:T(8,128)(2,1)}, u32[]{:S(2)}, u32[]{:S(2)}) collective-permute-start(bf16[4,48,128]{2,1,0:T(8,128)(2,1)S(1)} %shard_map.102.quad), channel_id=1, source_target_pairs={{0,4},{1,5},{2,6},{3,7},{4,0},{5,1},{6,2},{7,3},{8,12},{9,13},{10,... | collective-permute-start | bytes 147464 | tf_op jit(solution)/shard_map/ppermute | solution.py:428
  12.1 1.0 %copy.18.weight.refs_3_ = bf16[48,432]{1,0:T(8,128)(2,1)S(1)} copy(bf16[48,432]{0,1:T(8,128)(2,1)} %bitcast.17) | data formatting | bytes 82944 | tf_op jit(solution)/shard_map/reshape | solution.py:439
  13.1 0.0 copy-start.4
  13.1 0.0 copy-start.3
  13.1 0.0 copy-start
  13.1 0.0 copy-start.1
  13.1 0.0 copy-start.2
  13.1 2.2 %copy.17 = bf16[1,1,48,128,128]{3,2,4,1,0:T(8,128)(2,1)S(1)} copy(bf16[1,1,48,128,128]{4,3,2,1,0:T(8,128)(2,1)} %param.12) | data formatting | bytes 3145728 | tf_op args[5]
  15.3 0.0 collective-permute-done.5.z3
  15.3 1.5 %collective-permute-done.4.z2 = bf16[4,48,128]{2,1,0:T(8,128)(2,1)} collective-permute-done((bf16[4,48,128]{2,1,0:T(8,128)(2,1)S(1)}, bf16[4,48,128]{2,1,0:T(8,128)(2,1)}, u32[]{:S(2)}, u32[]{:S(2)}) %collective-permute-start.4) | collective-permute-done | bytes 49184 | tf_op jit(solution)/shard_map/ppermute | solution.py:428
  16.8 0.0 collective-permute-done.3.z1
  16.9 0.1 broadcast_in_dim.8.dilation.refs_1_
  16.9 0.1 broadcast_in_dim.10.bias.refs_4_
  17.0 15.5 %shard_map.103 = (f32[12,48,128]{2,1,0:T(8,128)S(1)}, f32[12,48,128]{2,1,0:T(8,128)S(1)}, f32[6,48,128]{2,1,0:T(8,128)S(1)}, bf16[48,128,128]{2,1,0:T(8,128)(2,1)}) custom-call(s32[2,128]{1,0:T(2,128)S(1)} %bitcast.12, s32[2,128]{1,0:T(2,128)S(1)} %broadcast_in_dim.8.dilation.refs_1_, bf16[4,48,128]{2,1,0:T(8,128)(2,1)S(1)} %shard_map.102.quad, ...), custom_call_target="tpu_custom_call" | custom-call | tf_op jit(solution)/shard_map/pallas_call | solution.py:332
  32.5 0.1 collective-permute-start.6
  32.6 1.6 %collective-permute-done.6.got = f32[12,48,128]{2,1,0:T(8,128)S(1)} collective-permute-done((f32[12,48,128]{2,1,0:T(8,128)S(1)}, f32[12,48,128]{2,1,0:T(8,128)S(1)}, u32[]{:S(2)}, u32[]{:S(2)}) %collective-permute-start.6) | collective-permute-done | bytes 294944 | tf_op jit(solution)/shard_map/ppermute | solution.py:428
  34.1 0.1 shard_map.104
  34.2 0.1 collective-permute-start.7
  34.3 3.1 %collective-permute-start.8 = (bf16[6,48,128]{2,1,0:T(8,128)(2,1)S(1)}, bf16[6,48,128]{2,1,0:T(8,128)(2,1)S(1)}, u32[]{:S(2)}, u32[]{:S(2)}) collective-permute-start(bf16[6,48,128]{2,1,0:T(8,128)(2,1)S(1)} %get-tuple-element.28), channel_id=1, source_target_pairs={{0,8},{1,9},{2,10},{3,11},{4,12},{5,13},{6,14},{7,15},{8,0},{9,1},... | collective-permute-start | bytes 221192 | tf_op jit(solution)/shard_map/ppermute | solution.py:428
  37.4 1.6 %collective-permute-start.9 = (bf16[6,48,128]{2,1,0:T(8,128)(2,1)S(1)}, bf16[6,48,128]{2,1,0:T(8,128)(2,1)S(1)}, u32[]{:S(2)}, u32[]{:S(2)}) collective-permute-start(bf16[6,48,128]{2,1,0:T(8,128)(2,1)S(1)} %get-tuple-element.29), channel_id=1, source_target_pairs={{0,12},{1,13},{2,14},{3,15},{4,8},{5,9},{6,10},{7,11},{8,4},{9,5},... | collective-permute-start | bytes 221192 | tf_op jit(solution)/shard_map/ppermute | solution.py:428
  39.0 0.8 %shard_map.105 = (bf16[48,128,128]{2,1,0:T(8,128)(2,1)}, f32[8,128]{1,0:T(8,128)S(1)}) custom-call(s32[2,128]{1,0:T(2,128)S(1)} %bitcast.13, s32[2,128]{1,0:T(2,128)S(1)} %broadcast_in_dim.8.dilation.refs_1_, f32[6,48,128]{2,1,0:T(8,128)S(1)} %get-tuple-element.21.refs_2_, bf16[48,432]{1,0:T(8,128)(2,1)S(1)} %copy.18.weight.refs_3_, ...), custom_call_target="tpu_custom_call", output_to_operand_aliasing={{0}: (5, {})} | custom-call | tf_op jit(solution)/shard_map/pallas_call | solution.py:366
  39.8 0.0 collective-permute-done.7.a
  39.8 1.5 %collective-permute-done.8.b = bf16[6,48,128]{2,1,0:T(8,128)(2,1)S(1)} collective-permute-done((bf16[6,48,128]{2,1,0:T(8,128)(2,1)S(1)}, bf16[6,48,128]{2,1,0:T(8,128)(2,1)S(1)}, u32[]{:S(2)}, u32[]{:S(2)}) %collective-permute-start.8) | collective-permute-done | bytes 73760 | tf_op jit(solution)/shard_map/ppermute | solution.py:428
  41.3 1.7 %collective-permute-done.9.c = bf16[6,48,128]{2,1,0:T(8,128)(2,1)S(1)} collective-permute-done((bf16[6,48,128]{2,1,0:T(8,128)(2,1)S(1)}, bf16[6,48,128]{2,1,0:T(8,128)(2,1)S(1)}, u32[]{:S(2)}, u32[]{:S(2)}) %collective-permute-start.9) | collective-permute-done | bytes 73760 | tf_op jit(solution)/shard_map/ppermute | solution.py:428
  43.0 2.2 %collective-permute-start.12 = (bf16[5,48,128]{2,1,0:T(8,128)(2,1)S(1)}, bf16[5,48,128]{2,1,0:T(8,128)(2,1)S(1)}, u32[]{:S(2)}, u32[]{:S(2)}) collective-permute-start(bf16[5,48,128]{2,1,0:T(8,128)(2,1)S(1)} %get-tuple-element.33), channel_id=1, source_target_pairs={{0,18},{1,19},{2,16},{3,17},{4,22},{5,23},{6,20},{7,21},{8,26},{9,... | collective-permute-start | bytes 184328 | tf_op jit(solution)/shard_map/ppermute | solution.py:428
  45.2 0.6 collective-permute-start.10
  45.8 2.0 %collective-permute-start.11 = (bf16[5,48,128]{2,1,0:T(8,128)(2,1)S(1)}, bf16[5,48,128]{2,1,0:T(8,128)(2,1)S(1)}, u32[]{:S(2)}, u32[]{:S(2)}) collective-permute-start(bf16[5,48,128]{2,1,0:T(8,128)(2,1)S(1)} %get-tuple-element.31.refs_6_.keep), channel_id=1, source_target_pairs={{0,16},{1,17},{2,18},{3,19},{4,20},{5,21},{6,22},{7,23},{8,24},{9,... | collective-permute-start | bytes 184328 | tf_op jit(solution)/shard_map/ppermute | solution.py:428
  47.8 0.6 shard_map.107
  48.4 0.8 %collective-permute-done.12.c = bf16[5,48,128]{2,1,0:T(8,128)(2,1)S(1)} collective-permute-done((bf16[5,48,128]{2,1,0:T(8,128)(2,1)S(1)}, bf16[5,48,128]{2,1,0:T(8,128)(2,1)S(1)}, u32[]{:S(2)}, u32[]{:S(2)}) %collective-permute-start.12) | collective-permute-done | bytes 61472 | tf_op jit(solution)/shard_map/ppermute | solution.py:428
  49.2 0.2 collective-permute-done.10.a
  49.4 2.1 %collective-permute-done.11.b = bf16[5,48,128]{2,1,0:T(8,128)(2,1)S(1)} collective-permute-done((bf16[5,48,128]{2,1,0:T(8,128)(2,1)S(1)}, bf16[5,48,128]{2,1,0:T(8,128)(2,1)S(1)}, u32[]{:S(2)}, u32[]{:S(2)}) %collective-permute-start.11) | collective-permute-done | bytes 61472 | tf_op jit(solution)/shard_map/ppermute | solution.py:428
  51.5 3.2 %collective-permute-start.15 = (bf16[5,48,128]{2,1,0:T(8,128)(2,1)S(1)}, bf16[5,48,128]{2,1,0:T(8,128)(2,1)S(1)}, u32[]{:S(2)}, u32[]{:S(2)}) collective-permute-start(bf16[5,48,128]{2,1,0:T(8,128)(2,1)S(1)} %shard_map.108.refs_6_.keep), channel_id=1, source_target_pairs={{0,96},{1,97},{2,98},{3,99},{4,100},{5,101},{6,102},{7,103},{8,104... | collective-permute-start | bytes 184328 | tf_op jit(solution)/shard_map/ppermute | solution.py:428
  54.8 0.5 collective-permute-start.14
  55.2 0.5 collective-permute-start.13
  55.7 0.6 shard_map.109
  56.3 1.4 %collective-permute-done.15.c = bf16[5,48,128]{2,1,0:T(8,128)(2,1)S(1)} collective-permute-done((bf16[5,48,128]{2,1,0:T(8,128)(2,1)S(1)}, bf16[5,48,128]{2,1,0:T(8,128)(2,1)S(1)}, u32[]{:S(2)}, u32[]{:S(2)}) %collective-permute-start.15) | collective-permute-done | bytes 61472 | tf_op jit(solution)/shard_map/ppermute | solution.py:428
  57.7 2.8 %collective-permute-done.14.b = bf16[5,48,128]{2,1,0:T(8,128)(2,1)S(1)} collective-permute-done((bf16[5,48,128]{2,1,0:T(8,128)(2,1)S(1)}, bf16[5,48,128]{2,1,0:T(8,128)(2,1)S(1)}, u32[]{:S(2)}, u32[]{:S(2)}) %collective-permute-start.14) | collective-permute-done | bytes 61472 | tf_op jit(solution)/shard_map/ppermute | solution.py:428
  60.5 0.0 collective-permute-done.13.a
  60.5 0.8 %shard_map.110 = (f32[48,128]{1,0:T(8,128)}, f32[9,48,48]{2,1,0:T(8,128)}, f32[1,48]{1,0:T(1,128)}) custom-call(bf16[5,48,128]{2,1,0:T(8,128)(2,1)S(1)} %shard_map.108.refs_6_.keep, bf16[5,48,128]{2,1,0:T(8,128)(2,1)S(1)} %collective-permute-done.13.a, bf16[5,48,128]{2,1,0:T(8,128)(2,1)S(1)} %collective-permute-done.14.b, ...), custom_call_target="tpu_custom_call" | custom-call | tf_op jit(solution)/shard_map/pallas_call | solution.py:463
  (8 shorter events, 0.1 us)
Async XLA Ops:
  0.6 2.2 %collective-permute-start = (bf16[48,128]{1,0:T(8,128)(2,1)}, bf16[48,128]{1,0:T(8,128)(2,1)S(1)}, u32[]{:S(2)}, u32[]{:S(2)}) collective-permute-start(bf16[48,128]{1,0:T(8,128)(2,1)} %param.7), channel_id=1, source_target_pairs={{0,1},{1,0},{2,3},{3,2},{4,5},{5,4},{6,7},{7,6},{8,9},{9,8},{10,11... | collective-permute-start | bytes 36872 | tf_op jit(solution)/shard_map/ppermute | solution.py:428
  0.7 3.4 %collective-permute-start.2 = (bf16[48,128]{1,0:T(8,128)(2,1)}, bf16[48,128]{1,0:T(8,128)(2,1)S(1)}, u32[]{:S(2)}, u32[]{:S(2)}) collective-permute-start(bf16[48,128]{1,0:T(8,128)(2,1)} %param.7), channel_id=1, source_target_pairs={{0,3},{1,2},{2,1},{3,0},{4,7},{5,6},{6,5},{7,4},{8,11},{9,10},{10,... | collective-permute-start | bytes 36872 | tf_op jit(solution)/shard_map/ppermute | solution.py:428
  2.4 3.9 %collective-permute-start.1 = (bf16[48,128]{1,0:T(8,128)(2,1)}, bf16[48,128]{1,0:T(8,128)(2,1)S(1)}, u32[]{:S(2)}, u32[]{:S(2)}) collective-permute-start(bf16[48,128]{1,0:T(8,128)(2,1)} %param.7), channel_id=1, source_target_pairs={{0,2},{1,3},{2,0},{3,1},{4,6},{5,7},{6,4},{7,5},{8,10},{9,11},{10,... | collective-permute-start | bytes 36872 | tf_op jit(solution)/shard_map/ppermute | solution.py:428
  7.0 8.3 %collective-permute-start.5 = (bf16[4,48,128]{2,1,0:T(8,128)(2,1)S(1)}, bf16[4,48,128]{2,1,0:T(8,128)(2,1)}, u32[]{:S(2)}, u32[]{:S(2)}) collective-permute-start(bf16[4,48,128]{2,1,0:T(8,128)(2,1)S(1)} %shard_map.102.quad), channel_id=1, source_target_pairs={{0,12},{1,13},{2,14},{3,15},{4,8},{5,9},{6,10},{7,11},{8,4},{9,5},... | collective-permute-start | bytes 147464 | tf_op jit(solution)/shard_map/ppermute | solution.py:428
  11.1 5.7 %collective-permute-start.4 = (bf16[4,48,128]{2,1,0:T(8,128)(2,1)S(1)}, bf16[4,48,128]{2,1,0:T(8,128)(2,1)}, u32[]{:S(2)}, u32[]{:S(2)}) collective-permute-start(bf16[4,48,128]{2,1,0:T(8,128)(2,1)S(1)} %shard_map.102.quad), channel_id=1, source_target_pairs={{0,8},{1,9},{2,10},{3,11},{4,12},{5,13},{6,14},{7,15},{8,0},{9,1},... | collective-permute-start | bytes 147464 | tf_op jit(solution)/shard_map/ppermute | solution.py:428
  11.2 5.7 %collective-permute-start.3 = (bf16[4,48,128]{2,1,0:T(8,128)(2,1)S(1)}, bf16[4,48,128]{2,1,0:T(8,128)(2,1)}, u32[]{:S(2)}, u32[]{:S(2)}) collective-permute-start(bf16[4,48,128]{2,1,0:T(8,128)(2,1)S(1)} %shard_map.102.quad), channel_id=1, source_target_pairs={{0,4},{1,5},{2,6},{3,7},{4,0},{5,1},{6,2},{7,3},{8,12},{9,13},{10,... | collective-permute-start | bytes 147464 | tf_op jit(solution)/shard_map/ppermute | solution.py:428
  13.1 3.8 %copy-start.4 = (s32[2]{0:T(128)S(1)}, s32[2]{0:T(128)}, u32[]{:S(2)}) copy-start(s32[2]{0:T(128)} %param.10) | copy-start | bytes 28
  13.1 3.8 %copy-start.3 = (f32[48]{0:T(128)S(1)}, f32[48]{0:T(128)}, u32[]{:S(2)}) copy-start(f32[48]{0:T(128)} %param.9) | copy-start | bytes 580
  13.1 3.9 %copy-start = (bf16[1,1,48,128,128]{4,3,2,1,0:T(8,128)(2,1)S(1)}, bf16[1,1,48,128,128]{4,3,2,1,0:T(8,128)(2,1)}, u32[]{:S(2)}) copy-start(bf16[1,1,48,128,128]{4,3,2,1,0:T(8,128)(2,1)} %param.12) | copy-start | bytes 4718596
  13.1 3.9 %copy-start.1 = (bf16[2,144,512]{2,1,0:T(8,128)(2,1)S(1)}, bf16[2,144,512]{2,1,0:T(8,128)(2,1)}, u32[]{:S(2)}) copy-start(bf16[2,144,512]{2,1,0:T(8,128)(2,1)} %constant.2.clone.repeat) | copy-start | bytes 884740
  13.1 3.9 %copy-start.2 = (s32[128,2]{0,1:T(2,128)S(1)}, s32[128,2]{0,1:T(2,128)}, u32[]{:S(2)}) copy-start(s32[128,2]{0,1:T(2,128)} %param.11) | copy-start | bytes 3076
  32.5 1.7 %collective-permute-start.6 = (f32[12,48,128]{2,1,0:T(8,128)S(1)}, f32[12,48,128]{2,1,0:T(8,128)S(1)}, u32[]{:S(2)}, u32[]{:S(2)}) collective-permute-start(f32[12,48,128]{2,1,0:T(8,128)S(1)} %get-tuple-element.24), channel_id=1, source_target_pairs={{0,1},{1,0},{2,3},{3,2},{4,5},{5,4},{6,7},{7,6},{8,9},{9,8},{10,11... | collective-permute-start | bytes 884744 | tf_op jit(solution)/shard_map/ppermute | solution.py:428
  34.2 5.6 %collective-permute-start.7 = (bf16[6,48,128]{2,1,0:T(8,128)(2,1)S(1)}, bf16[6,48,128]{2,1,0:T(8,128)(2,1)S(1)}, u32[]{:S(2)}, u32[]{:S(2)}) collective-permute-start(bf16[6,48,128]{2,1,0:T(8,128)(2,1)S(1)} %get-tuple-element.27), channel_id=1, source_target_pairs={{0,4},{1,5},{2,6},{3,7},{4,0},{5,1},{6,2},{7,3},{8,12},{9,13},{10,... | collective-permute-start | bytes 221192 | tf_op jit(solution)/shard_map/ppermute | solution.py:428
  34.3 7.0 %collective-permute-start.8 = (bf16[6,48,128]{2,1,0:T(8,128)(2,1)S(1)}, bf16[6,48,128]{2,1,0:T(8,128)(2,1)S(1)}, u32[]{:S(2)}, u32[]{:S(2)}) collective-permute-start(bf16[6,48,128]{2,1,0:T(8,128)(2,1)S(1)} %get-tuple-element.28), channel_id=1, source_target_pairs={{0,8},{1,9},{2,10},{3,11},{4,12},{5,13},{6,14},{7,15},{8,0},{9,1},... | collective-permute-start | bytes 221192 | tf_op jit(solution)/shard_map/ppermute | solution.py:428
  37.4 5.6 %collective-permute-start.9 = (bf16[6,48,128]{2,1,0:T(8,128)(2,1)S(1)}, bf16[6,48,128]{2,1,0:T(8,128)(2,1)S(1)}, u32[]{:S(2)}, u32[]{:S(2)}) collective-permute-start(bf16[6,48,128]{2,1,0:T(8,128)(2,1)S(1)} %get-tuple-element.29), channel_id=1, source_target_pairs={{0,12},{1,13},{2,14},{3,15},{4,8},{5,9},{6,10},{7,11},{8,4},{9,5},... | collective-permute-start | bytes 221192 | tf_op jit(solution)/shard_map/ppermute | solution.py:428
  43.0 6.2 %collective-permute-start.12 = (bf16[5,48,128]{2,1,0:T(8,128)(2,1)S(1)}, bf16[5,48,128]{2,1,0:T(8,128)(2,1)S(1)}, u32[]{:S(2)}, u32[]{:S(2)}) collective-permute-start(bf16[5,48,128]{2,1,0:T(8,128)(2,1)S(1)} %get-tuple-element.33), channel_id=1, source_target_pairs={{0,18},{1,19},{2,16},{3,17},{4,22},{5,23},{6,20},{7,21},{8,26},{9,... | collective-permute-start | bytes 184328 | tf_op jit(solution)/shard_map/ppermute | solution.py:428
  45.2 4.2 %collective-permute-start.10 = (bf16[5,48,128]{2,1,0:T(8,128)(2,1)S(1)}, bf16[5,48,128]{2,1,0:T(8,128)(2,1)S(1)}, u32[]{:S(2)}, u32[]{:S(2)}) collective-permute-start(bf16[5,48,128]{2,1,0:T(8,128)(2,1)S(1)} %get-tuple-element.33), channel_id=1, source_target_pairs={{0,2},{1,3},{2,0},{3,1},{4,6},{5,7},{6,4},{7,5},{8,10},{9,11},{10,... | collective-permute-start | bytes 184328 | tf_op jit(solution)/shard_map/ppermute | solution.py:428
  45.8 5.7 %collective-permute-start.11 = (bf16[5,48,128]{2,1,0:T(8,128)(2,1)S(1)}, bf16[5,48,128]{2,1,0:T(8,128)(2,1)S(1)}, u32[]{:S(2)}, u32[]{:S(2)}) collective-permute-start(bf16[5,48,128]{2,1,0:T(8,128)(2,1)S(1)} %get-tuple-element.31.refs_6_.keep), channel_id=1, source_target_pairs={{0,16},{1,17},{2,18},{3,19},{4,20},{5,21},{6,22},{7,23},{8,24},{9,... | collective-permute-start | bytes 184328 | tf_op jit(solution)/shard_map/ppermute | solution.py:428
  51.5 6.2 %collective-permute-start.15 = (bf16[5,48,128]{2,1,0:T(8,128)(2,1)S(1)}, bf16[5,48,128]{2,1,0:T(8,128)(2,1)S(1)}, u32[]{:S(2)}, u32[]{:S(2)}) collective-permute-start(bf16[5,48,128]{2,1,0:T(8,128)(2,1)S(1)} %shard_map.108.refs_6_.keep), channel_id=1, source_target_pairs={{0,96},{1,97},{2,98},{3,99},{4,100},{5,101},{6,102},{7,103},{8,104... | collective-permute-start | bytes 184328 | tf_op jit(solution)/shard_map/ppermute | solution.py:428
  54.8 5.7 %collective-permute-start.14 = (bf16[5,48,128]{2,1,0:T(8,128)(2,1)S(1)}, bf16[5,48,128]{2,1,0:T(8,128)(2,1)S(1)}, u32[]{:S(2)}, u32[]{:S(2)}) collective-permute-start(bf16[5,48,128]{2,1,0:T(8,128)(2,1)S(1)} %shard_map.108.refs_6_.keep), channel_id=1, source_target_pairs={{0,64},{1,65},{2,66},{3,67},{4,68},{5,69},{6,70},{7,71},{8,72},{9,... | collective-permute-start | bytes 184328 | tf_op jit(solution)/shard_map/ppermute | solution.py:428
  55.2 5.2 %collective-permute-start.13 = (bf16[5,48,128]{2,1,0:T(8,128)(2,1)S(1)}, bf16[5,48,128]{2,1,0:T(8,128)(2,1)S(1)}, u32[]{:S(2)}, u32[]{:S(2)}) collective-permute-start(bf16[5,48,128]{2,1,0:T(8,128)(2,1)S(1)} %shard_map.108.refs_6_.keep), channel_id=1, source_target_pairs={{0,32},{1,33},{2,34},{3,35},{4,36},{5,37},{6,38},{7,39},{8,40},{9,... | collective-permute-start | bytes 184328 | tf_op jit(solution)/shard_map/ppermute | solution.py:428
